TPU v7x, 32 devices: a whole 2x2x4 slice. The times are simulated.
32 devices in a mesh: parts: 2 (over y), tm: 4 (over z), fiber: 2 (over x), rep: 2 (over core).
Axes of the slice: x: 2, y: 2, z: 4, core: 2. Of those that a mesh axis runs over, the one named last changes fastest.
Arguments:
- strain: bfloat16 [4, 32, 256, 512], P(('parts', 'rep'), None, 'fiber', 'tm'), parts along dimension 0, may hold values from -6 to 6
- time_kernel: bfloat16 [32, 32, 32], replicated, may hold values from -0.1875 to 0.1875
- fiber_kernel: bfloat16 [32, 4, 9], replicated, may hold values from -1 to 1
- cotangent: bfloat16 [4, 32, 2, 128, 256], P(('parts', 'rep'), None, 'fiber', 'tm'), parts along dimension 0, may hold values from -6 to 6
Outputs:
- activation: bfloat16 [4, 32, 2, 128, 256], P(('parts', 'rep'), None, 'fiber', 'tm'), parts along dimension 0
- strain_grad: bfloat16 [4, 32, 256, 512], P(('parts', 'rep'), None, 'fiber', 'tm'), parts along dimension 0
- time_kernel_grad: float32 [64, 32, 32], P('parts'), parts along dimension 0
- fiber_kernel_grad: float32 [64, 4, 9], P('parts'), parts along dimension 0
There are 2 independent parts, one for each index of `parts`. A program takes and returns all parts, laid end to end along the dimension named above; an argument that names none is the same for every part. Nothing has to cross between parts.
All inputs are finite; a program needn't handle non-finite values.
Results may differ from a plain program's by a relative error of at most 0.0095.
Values may be sent and summed in bfloat16 or wider, within the bound.
No kernel may reach another device: no remote copies, remote signals or barrier semaphores. Data moves between devices by JAX's collectives and lax.ppermute only.
A program may use at most 64 MiB of HBM per device.

v0:
```python
import math

import jax
import jax.numpy as jnp
from jax import lax
from jax.sharding import PartitionSpec as P


def shifted(array, axis, by):
    length = lax.axis_size(axis)
    pairs = [(i, i + by) for i in range(length) if 0 <= i + by < length]
    return lax.ppermute(array, axis, pairs)


def padded(array, sides, width):
    for axis, dim in sides:
        size, length = (lax.axis_size(axis), array.shape[dim])
        up = [(i, (i + 1) % size) for i in range(size - 1)]
        down = [(j, i) for i, j in up]
        last = lax.slice_in_dim(array, length - width, length, axis=dim)
        leading = lax.slice_in_dim(array, 0, width, axis=dim)
        before = lax.ppermute(last, axis, up)
        after = lax.ppermute(leading, axis, down)
        array = jnp.concatenate([before, array, after], axis=dim)
    return array


def gelu_slope(value):
    return 0.5 * (1.0 + jax.scipy.special.erf(value / math.sqrt(2.0))) + value * jnp.exp(
        -0.5 * value * value
    ) / math.sqrt(2.0 * math.pi)


def time_forward(extended, time_kernel, tout):
    slabs, feats, chans, length = extended.shape
    phases = extended.reshape(slabs, feats, chans, length // 2, 2)
    total = jnp.zeros((slabs, time_kernel.shape[0], chans, tout), jnp.float32)
    for tap in range(time_kernel.shape[2]):
        offset = tap // 2
        piece = phases[:, :, :, offset : offset + tout, tap % 2]
        total = total + jnp.einsum(
            "oi,bict->boct", time_kernel[:, :, tap], piece, preferred_element_type=jnp.float32
        )
    return total


def time_backward(gradient, time_kernel):
    slabs, feats, chans, steps_in = gradient.shape
    taps = time_kernel.shape[2]
    span = steps_in + taps // 2 - 1
    even = jnp.zeros((slabs, time_kernel.shape[1], chans, span), jnp.float32)
    odd = jnp.zeros((slabs, time_kernel.shape[1], chans, span), jnp.float32)
    for tap in range(taps):
        offset = tap // 2
        term = jnp.einsum(
            "oi,boct->bict", time_kernel[:, :, tap], gradient, preferred_element_type=jnp.float32
        )
        placed = jnp.pad(term, ((0, 0), (0, 0), (0, 0), (offset, span - steps_in - offset)))
        if tap % 2 == 0:
            even = even + placed
        else:
            odd = odd + placed
    return jnp.stack([even, odd], axis=4).reshape(slabs, time_kernel.shape[1], chans, 2 * span)


def time_weight_grad(extended, gradient, taps):
    slabs, feats, chans, length = extended.shape
    tout = gradient.shape[3]
    phases = extended.reshape(slabs, feats, chans, length // 2, 2)
    pieces = []
    for tap in range(taps):
        offset = tap // 2
        piece = phases[:, :, :, offset : offset + tout, tap % 2]
        pieces.append(
            jnp.einsum("boct,bict->oi", gradient, piece, preferred_element_type=jnp.float32)
        )
    return jnp.stack(pieces, axis=2)


def on_device(strain, time_kernel, fiber_kernel, cotangent):
    slabs, feats, chans, steps = strain.shape
    taps = time_kernel.shape[2]
    rim_cols = taps - 2
    tout = steps // 2
    per_group = fiber_kernel.shape[1]
    group_count = feats // per_group
    kf_taps = fiber_kernel.shape[2]
    reach = kf_taps // 2
    total = (
        slabs * lax.axis_size("rep") * chans * lax.axis_size("fiber") * tout * lax.axis_size("tm")
    )
    scale = 1.0 / math.sqrt(total)
    before = shifted(strain[:, :, :, steps - rim_cols :], "tm", 1)
    extended = jnp.concatenate([before, strain], axis=3)
    inner = time_forward(extended, time_kernel, tout).astype(jnp.bfloat16)
    tiled = jnp.tile(fiber_kernel, (1, group_count, 1))
    feat_ids = jnp.arange(feats, dtype=jnp.int32) // per_group
    same_group = feat_ids[:, None] == feat_ids[None, :]
    dense = jnp.where(same_group[:, :, None], tiled, jnp.zeros_like(tiled))
    inner_ext = padded(inner, (("fiber", 2),), reach)
    pre_sum = jnp.zeros((slabs, feats, chans, tout), jnp.float32)
    for tap in range(kf_taps):
        pre_sum = pre_sum + jnp.einsum(
            "oi,bict->boct",
            dense[:, :, tap],
            inner_ext[:, :, tap : tap + chans],
            preferred_element_type=jnp.float32,
        )
    pre_act = pre_sum.astype(jnp.bfloat16)
    act_time = jax.nn.gelu(pre_act.astype(jnp.float32), approximate=False).astype(jnp.bfloat16)
    act_chan = lax.all_to_all(act_time, "tm", split_axis=2, concat_axis=3, tiled=True)
    upstream = lax.all_to_all(cotangent[:, :, 0], "tm", split_axis=3, concat_axis=2, tiled=True)
    d_pre = (upstream.astype(jnp.float32) * gelu_slope(pre_act.astype(jnp.float32))).astype(
        jnp.bfloat16
    )
    activation = act_chan[:, :, None]
    d_ext = padded(d_pre, (("fiber", 2),), reach)
    back_sum = jnp.zeros((slabs, feats, chans, tout), jnp.float32)
    dense_grads = []
    for tap in range(kf_taps):
        start = 2 * reach - tap
        back_sum = back_sum + jnp.einsum(
            "oi,boct->bict",
            dense[:, :, tap],
            d_ext[:, :, start : start + chans],
            preferred_element_type=jnp.float32,
        )
        dense_grads.append(
            jnp.einsum(
                "boct,bict->oi",
                d_pre,
                inner_ext[:, :, tap : tap + chans],
                preferred_element_type=jnp.float32,
            )
        )
    d_inner = back_sum.astype(jnp.bfloat16)
    blocks = jnp.stack(dense_grads, axis=2).reshape(
        group_count, per_group, group_count, per_group, kf_taps
    )
    diagonal = jnp.diagonal(blocks, axis1=0, axis2=2)
    fiber_grad = jnp.transpose(diagonal, (3, 0, 1, 2)).reshape(feats, per_group, kf_taps) * scale
    time_grad = time_weight_grad(extended, d_inner, taps) * scale
    wide = time_backward(d_inner, time_kernel)
    arrived = shifted(wide[:, :, :, :rim_cols].astype(jnp.bfloat16), "tm", -1).astype(jnp.float32)
    own = wide[:, :, :, rim_cols:]
    d_signal = jnp.concatenate(
        [own[:, :, :, : steps - rim_cols], own[:, :, :, steps - rim_cols :] + arrived], axis=3
    )
    strain_grad = d_signal.astype(jnp.bfloat16)
    time_sum, fiber_sum = lax.psum((time_grad, fiber_grad), ("tm", "fiber", "rep"))
    return (activation, strain_grad, time_sum, fiber_sum)


def solution(mesh):
    placed = (
        P(("parts", "rep"), None, "fiber", "tm"),
        P(),
        P(),
        P(("parts", "rep"), None, "fiber", "tm", None),
    )
    return jax.shard_map(
        on_device,
        mesh=mesh,
        in_specs=placed,
        out_specs=(
            P(("parts", "rep"), None, "fiber", "tm", None),
            P(("parts", "rep"), None, "fiber", "tm"),
            P("parts", None, None),
            P("parts", None, None),
        ),
        check_vma=False,
    )
```

profile of v0, /device:TPU:0, one launch (start us, length us, event | category | flops | bytes accessed | tf_op | source)
XLA Modules:
  0.0 317.2 jit_solution(16687084823280271707)
XLA Ops:
  7.2 2.0 copy.653
  9.9 5.6 %collective-permute-start = (bf16[1,32,128,30]{2,1,3,0:T(8,128)(2,1)}, bf16[1,32,128,30]{2,1,3,0:T(8,128)(2,1)}, u32[]{:S(2)}, u32[]{:S(2)}) collective-permute-start(bf16[1,32,128,30]{2,1,3,0:T(8,128)(2,1)} %slice.493), channel_id=1, source_target_pairs={{0,4},{4,8},{8,12},{1,5},{5,9},{9,13},{2,6},{6,10},{10,14},{3,7},{... | collective-permute-start | bytes 737288 | tf_op jit(solution)/shard_map/ppermute | solution.py:12
  15.5 3.7 %copy.723 = bf16[1,32,1,32,256]{3,1,4,2,0:T(8,128)(2,1)} copy(bf16[1,32,1,32,256]{4,3,2,1,0:T(8,128)(2,1)S(1)} %copy-done.18) | data formatting | bytes 1048576 | tf_op args[3]
  19.2 2.0 bitcast_bitcast_fusion
  21.2 2.9 reshape.879
  24.1 3.7 %all-to-all-start.1 = ((bf16[4,2,32768]{2,1,0:T(2,128)(2,1)}), bf16[4,2,32768]{2,1,0:T(2,128)(2,1)S(1)}, u32[]{:S(2)}, u32[]{:S(2)}) async-start(bf16[4,2,32768]{2,1,0:T(2,128)(2,1)} %reshape.879), calls=%async_computation.1 | async-start | bytes 1048576 | tf_op jit(solution)/shard_map/all_to_all | solution.py:112
  27.9 2.6 fusion.154
  30.4 3.2 %fusion.153 = (bf16[32,32,1]{2,1,0:T(8,128)(2,1)}, bf16[32,32,1]{2,1,0:T(8,128)(2,1)}, bf16[32,32,1]{2,1,0:T(8,128)(2,1)}, bf16[32,32,1]{2,1,0:T(8,128)(2,1)}, b...) fusion(bf16[32,32,32]{2,1,0:T(8,128)(2,1)S(1)} %copy-done), kind=kLoop, calls=%fused_computation.349 | loop fusion | bytes 77824 | tf_op jit(solution)/shard_map/slice | solution.py:42
  45.7 1.8 copy.913
  48.7 1.8 copy.973
  50.6 1.8 copy.965
  52.4 1.8 copy.971
  55.1 1.9 copy.967
  56.9 1.8 copy.963
  58.7 1.8 copy.961
  60.5 1.8 copy.959
  62.3 1.8 copy.957
  64.1 1.8 copy.955
  65.9 1.8 copy.953
  67.7 1.8 copy.951
  69.6 1.8 copy.949
  71.4 1.8 copy.947
  92.8 4.6 %collective-permute-start.1 = (bf16[1,32,4,64]{2,1,3,0:T(8,128)(2,1)S(1)}, bf16[1,32,4,64]{2,1,3,0:T(8,128)(2,1)S(1)}, u32[]{:S(2)}, u32[]{:S(2)}) collective-permute-start(bf16[1,32,4,64]{2,1,3,0:T(8,128)(2,1)S(1)} %get-tuple-element.45), channel_id=1, source_target_pairs={{0,2},{1,3},{4,6},{5,7},{8,10},{9,11},{12,14},{13,15},{16,18},{17,... | collective-permute-start | bytes 49160 | tf_op jit(solution)/shard_map/ppermute | solution.py:22
  97.7 9.1 %collective-permute-done.2 = bf16[1,32,4,64]{2,1,3,0:T(8,128)(2,1)S(1)} collective-permute-done((bf16[1,32,4,64]{2,1,3,0:T(8,128)(2,1)S(1)}, bf16[1,32,4,64]{2,1,3,0:T(8,128)(2,1)S(1)}, u32[]{:S(2)}, u32[]{:S(2)}) %collective-permute-start.2) | collective-permute-done | bytes 16416 | tf_op jit(solution)/shard_map/ppermute | solution.py:23
  108.0 2.9 pad_maximum_fusion.5
  114.5 2.4 reshape.880
  116.9 4.3 %copy.724 = f32[1,32,32,4,64]{4,2,3,1,0:T(8,128)} copy(bf16[1,32,32,4,64]{2,1,4,3,0:T(8,128)(2,1)} %bitcast.1000) | data formatting | bytes 1572864 | tf_op jit(solution)/shard_map/convert_element_type | solution.py:113
  121.2 3.4 %copy.725 = f32[1,32,128,64]{2,1,3,0:T(8,128)} copy(f32[1,32,128,64]{3,2,1,0:T(8,128)} %bitcast.1001) | data formatting | bytes 2097152 | tf_op jit(solution)/shard_map/convert_element_type | solution.py:113
  124.6 4.9 %fusion.44 = (bf16[1,32,128,64]{2,1,3,0:T(8,128)(2,1)S(1)}, bf16[1,32,128,64]{2,1,3,0:T(8,128)(2,1)}) fusion(f32[1,32,128,64]{2,1,3,0:T(8,128)} %copy.725, f32[128,64,32]{0,2,1:T(8,128)} %convolution_add_fusion.1, bf16[1,32,128,64]{2,1,3,0:T(8,128)(2,1)S(1)} %copy-done.20, bf16[32,32,9]{1,0,2:T(8,128)(2,1)S(1)} %broadcast_select_fusion), kind=kOutput, calls=%fused_computation.193 | convolution fusion | flops 37224448 | bytes 3678208 | tf_op jit(solution)/shard_map/oi,bict->boct/dot_general | solution.py:103
  133.5 1.6 fusion.35
  135.1 1.6 fusion.34
  140.1 1.6 fusion.31
  143.5 1.6 fusion.29
  146.8 1.6 fusion.27
  149.2 1.9 copy.786
  151.2 2.6 copy.720
  153.8 2.6 reshape.877
  156.3 4.8 %all-to-all-start = ((bf16[4,2,32768]{2,1,0:T(2,128)(2,1)}), bf16[4,2,32768]{2,1,0:T(2,128)(2,1)}, u32[]{:S(2)}, u32[]{:S(2)}) async-start(bf16[4,2,32768]{2,1,0:T(2,128)(2,1)} %reshape.877), calls=%async_computation | async-start | bytes 1048576 | tf_op jit(solution)/shard_map/all_to_all | solution.py:111
  161.1 4.8 %collective-permute-start.4 = (bf16[1,32,4,64]{2,1,3,0:T(8,128)(2,1)}, bf16[1,32,4,64]{2,1,3,0:T(8,128)(2,1)S(1)}, u32[]{:S(2)}, u32[]{:S(2)}) collective-permute-start(bf16[1,32,4,64]{2,1,3,0:T(8,128)(2,1)} %get-tuple-element.38), channel_id=1, source_target_pairs={{0,2},{1,3},{4,6},{5,7},{8,10},{9,11},{12,14},{13,15},{16,18},{17,... | collective-permute-start | bytes 49160 | tf_op jit(solution)/shard_map/ppermute | solution.py:22
  169.4 5.5 %collective-permute-done.4 = bf16[1,32,4,64]{2,1,3,0:T(8,128)(2,1)S(1)} collective-permute-done((bf16[1,32,4,64]{2,1,3,0:T(8,128)(2,1)}, bf16[1,32,4,64]{2,1,3,0:T(8,128)(2,1)S(1)}, u32[]{:S(2)}, u32[]{:S(2)}) %collective-permute-start.4) | collective-permute-done | bytes 16416 | tf_op jit(solution)/shard_map/ppermute | solution.py:22
  197.7 2.2 add_bitcast_fusion
  199.9 2.2 add_bitcast_fusion.1
  207.1 60.1 %psum.15 = f32[32,4,9]{2,0,1:T(8,128)S(1)} all-reduce(f32[32,4,9]{2,0,1:T(8,128)S(1)} %bitcast.1016), channel_id=1, replica_groups=mesh['parts'=2,'tm'=4,'fiber'=2,'rep'=2] {'tm','fiber','rep'}, use_global_device_ids=true, to_apply=%region_1.2 | all-reduce | flops 1152 | bytes 9216 | tf_op jit(solution)/shard_map/psum | solution.py:150
  267.9 2.1 slice.562
  270.0 30.6 %all-reduce.34.cloned.1.call-done = f32[32,32,32]{1,0,2:T(8,128)} async-done(((f32[32,32,32]{1,0,2:T(8,128)}), f32[32,32,32]{1,0,2:T(8,128)}) %all-reduce.34.cloned.1.call-update) | async-done | bytes 131088 | tf_op jit(solution)/shard_map/psum | solution.py:150
  300.6 2.1 copy.791
  304.0 1.7 copy.790
  305.7 1.7 reshape.878
  (336 shorter events, 85.5 us)
Async XLA Ops:
  7.2 8.4 %copy-start.18 = (bf16[1,32,1,32,256]{4,3,2,1,0:T(8,128)(2,1)S(1)}, bf16[1,32,1,32,256]{4,3,2,1,0:T(8,128)(2,1)}, u32[]{:S(2)}) copy-start(bf16[1,32,1,32,256]{4,3,2,1,0:T(8,128)(2,1)} %param.7) | copy-start | bytes 1572868
  9.9 67.9 %collective-permute-start = (bf16[1,32,128,30]{2,1,3,0:T(8,128)(2,1)}, bf16[1,32,128,30]{2,1,3,0:T(8,128)(2,1)}, u32[]{:S(2)}, u32[]{:S(2)}) collective-permute-start(bf16[1,32,128,30]{2,1,3,0:T(8,128)(2,1)} %slice.493), channel_id=1, source_target_pairs={{0,4},{4,8},{8,12},{1,5},{5,9},{9,13},{2,6},{6,10},{10,14},{3,7},{... | collective-permute-start | bytes 737288 | tf_op jit(solution)/shard_map/ppermute | solution.py:12
  21.2 6.7 %copy-start = (bf16[32,32,32]{2,1,0:T(8,128)(2,1)S(1)}, bf16[32,32,32]{2,1,0:T(8,128)(2,1)}, u32[]{:S(2)}) copy-start(bf16[32,32,32]{2,1,0:T(8,128)(2,1)} %param.5) | copy-start | bytes 196612
  24.1 90.4 %all-to-all-start.1 = ((bf16[4,2,32768]{2,1,0:T(2,128)(2,1)}), bf16[4,2,32768]{2,1,0:T(2,128)(2,1)S(1)}, u32[]{:S(2)}, u32[]{:S(2)}) async-start(bf16[4,2,32768]{2,1,0:T(2,128)(2,1)} %reshape.879), calls=%async_computation.1 | async-start | bytes 1048576 | tf_op jit(solution)/shard_map/all_to_all | solution.py:112
  30.4 3.8 %copy-start.82 = (bf16[32,4,9]{0,1,2:T(4,128)(2,1)S(1)}, bf16[32,4,9]{0,1,2:T(4,128)(2,1)}, u32[]{:S(2)}) copy-start(bf16[32,4,9]{0,1,2:T(4,128)(2,1)} %param.6) | copy-start | bytes 6916
  33.6 5.6 %copy-start.16 = (bf16[32,32,1]{2,1,0:T(8,128)(2,1)S(1)}, bf16[32,32,1]{2,1,0:T(8,128)(2,1)}, u32[]{:S(2)}) copy-start(bf16[32,32,1]{2,1,0:T(8,128)(2,1)} %get-tuple-element.69) | copy-start | bytes 6148
  35.6 51.4 %copy-start.32 = (bf16[32,32,1]{1,0,2:T(8,128)(2,1)}, bf16[32,32,1]{1,0,2:T(8,128)(2,1)S(1)}, u32[]{:S(2)}) copy-start(bf16[32,32,1]{1,0,2:T(8,128)(2,1)S(1)} %copy.933) | copy-start | bytes 6148
  38.0 48.3 %copy-start.34 = (bf16[32,32,1]{1,0,2:T(8,128)(2,1)}, bf16[32,32,1]{1,0,2:T(8,128)(2,1)S(1)}, u32[]{:S(2)}) copy-start(bf16[32,32,1]{1,0,2:T(8,128)(2,1)S(1)} %copy.929) | copy-start | bytes 6148
  39.3 46.8 %copy-start.22 = (bf16[32,32,1]{1,0,2:T(8,128)(2,1)}, bf16[32,32,1]{1,0,2:T(8,128)(2,1)S(1)}, u32[]{:S(2)}) copy-start(bf16[32,32,1]{1,0,2:T(8,128)(2,1)S(1)} %copy.927) | copy-start | bytes 6148
  39.5 46.2 %copy-start.36 = (bf16[32,32,1]{1,0,2:T(8,128)(2,1)}, bf16[32,32,1]{1,0,2:T(8,128)(2,1)S(1)}, u32[]{:S(2)}) copy-start(bf16[32,32,1]{1,0,2:T(8,128)(2,1)S(1)} %copy.925) | copy-start | bytes 6148
  39.5 14.7 %copy-start.15 = (bf16[32,32,1]{2,1,0:T(8,128)(2,1)S(1)}, bf16[32,32,1]{2,1,0:T(8,128)(2,1)}, u32[]{:S(2)}) copy-start(bf16[32,32,1]{2,1,0:T(8,128)(2,1)} %get-tuple-element.48) | copy-start | bytes 6148
  40.8 44.7 %copy-start.24 = (bf16[32,32,1]{1,0,2:T(8,128)(2,1)}, bf16[32,32,1]{1,0,2:T(8,128)(2,1)S(1)}, u32[]{:S(2)}) copy-start(bf16[32,32,1]{1,0,2:T(8,128)(2,1)S(1)} %copy.923) | copy-start | bytes 6148
  42.0 43.2 %copy-start.38 = (bf16[32,32,1]{1,0,2:T(8,128)(2,1)}, bf16[32,32,1]{1,0,2:T(8,128)(2,1)S(1)}, u32[]{:S(2)}) copy-start(bf16[32,32,1]{1,0,2:T(8,128)(2,1)S(1)} %copy.921) | copy-start | bytes 6148
  43.3 41.7 %copy-start.26 = (bf16[32,32,1]{1,0,2:T(8,128)(2,1)}, bf16[32,32,1]{1,0,2:T(8,128)(2,1)S(1)}, u32[]{:S(2)}) copy-start(bf16[32,32,1]{1,0,2:T(8,128)(2,1)S(1)} %copy.919) | copy-start | bytes 6148
  44.5 40.1 %copy-start.40 = (bf16[32,32,1]{1,0,2:T(8,128)(2,1)}, bf16[32,32,1]{1,0,2:T(8,128)(2,1)S(1)}, u32[]{:S(2)}) copy-start(bf16[32,32,1]{1,0,2:T(8,128)(2,1)S(1)} %copy.917) | copy-start | bytes 6148
  45.7 38.6 %copy-start.28 = (bf16[32,32,1]{1,0,2:T(8,128)(2,1)}, bf16[32,32,1]{1,0,2:T(8,128)(2,1)S(1)}, u32[]{:S(2)}) copy-start(bf16[32,32,1]{1,0,2:T(8,128)(2,1)S(1)} %copy.915) | copy-start | bytes 6148
  48.7 30.4 %copy-start.30 = (bf16[32,32,1]{1,0,2:T(8,128)(2,1)}, bf16[32,32,1]{1,0,2:T(8,128)(2,1)S(1)}, u32[]{:S(2)}) copy-start(bf16[32,32,1]{1,0,2:T(8,128)(2,1)S(1)} %copy.911) | copy-start | bytes 6148
  55.1 18.1 %copy-start.14 = (bf16[32,32,1]{2,1,0:T(8,128)(2,1)S(1)}, bf16[32,32,1]{2,1,0:T(8,128)(2,1)}, u32[]{:S(2)}) copy-start(bf16[32,32,1]{2,1,0:T(8,128)(2,1)} %get-tuple-element.59) | copy-start | bytes 6148
  77.7 9.5 %copy-start.58 = (bf16[32,32,1]{1,0,2:T(8,128)(2,1)}, bf16[32,32,1]{1,0,2:T(8,128)(2,1)S(1)}, u32[]{:S(2)}) copy-start(bf16[32,32,1]{1,0,2:T(8,128)(2,1)S(1)} %copy.935) | copy-start | bytes 6148
  77.8 1.1 copy-start.62
  90.0 0.8 copy-start.60
  91.5 15.3 %collective-permute-start.2 = (bf16[1,32,4,64]{2,1,3,0:T(8,128)(2,1)S(1)}, bf16[1,32,4,64]{2,1,3,0:T(8,128)(2,1)S(1)}, u32[]{:S(2)}, u32[]{:S(2)}) collective-permute-start(bf16[1,32,4,64]{2,1,3,0:T(8,128)(2,1)S(1)} %get-tuple-element.44), channel_id=1, source_target_pairs={{2,0},{3,1},{6,4},{7,5},{10,8},{11,9},{14,12},{15,13},{18,16},{19,... | collective-permute-start | bytes 49160 | tf_op jit(solution)/shard_map/ppermute | solution.py:23
  92.8 15.2 %collective-permute-start.1 = (bf16[1,32,4,64]{2,1,3,0:T(8,128)(2,1)S(1)}, bf16[1,32,4,64]{2,1,3,0:T(8,128)(2,1)S(1)}, u32[]{:S(2)}, u32[]{:S(2)}) collective-permute-start(bf16[1,32,4,64]{2,1,3,0:T(8,128)(2,1)S(1)} %get-tuple-element.45), channel_id=1, source_target_pairs={{0,2},{1,3},{4,6},{5,7},{8,10},{9,11},{12,14},{13,15},{16,18},{17,... | collective-permute-start | bytes 49160 | tf_op jit(solution)/shard_map/ppermute | solution.py:22
  110.9 0.8 copy-start.10
  110.9 1.0 copy-start.12
  110.9 1.1 copy-start.8
  110.9 1.4 copy-start.6
  110.9 1.8 copy-start.4
  110.9 2.0 copy-start.2
  121.2 3.4 %copy-start.20 = (bf16[1,32,128,64]{2,1,3,0:T(8,128)(2,1)S(1)}, bf16[1,32,128,64]{2,1,3,0:T(8,128)(2,1)}, u32[]{:S(2)}) copy-start(bf16[1,32,128,64]{2,1,3,0:T(8,128)(2,1)} %get-tuple-element.30) | copy-start | bytes 1572868
  130.8 2.7 copy-start.13
  132.0 34.7 %collective-permute-start.3 = (bf16[1,32,4,64]{2,1,3,0:T(8,128)(2,1)}, bf16[1,32,4,64]{2,1,3,0:T(8,128)(2,1)S(1)}, u32[]{:S(2)}, u32[]{:S(2)}) collective-permute-start(bf16[1,32,4,64]{2,1,3,0:T(8,128)(2,1)} %get-tuple-element.39), channel_id=1, source_target_pairs={{2,0},{3,1},{6,4},{7,5},{10,8},{11,9},{14,12},{15,13},{18,16},{19,... | collective-permute-start | bytes 49160 | tf_op jit(solution)/shard_map/ppermute | solution.py:23
  133.5 1.7 copy-start.11
  135.1 1.7 copy-start.9
  136.8 1.7 copy-start.7
  140.1 1.7 copy-start.5
  141.8 1.7 copy-start.3
  145.1 1.7 copy-start.21
  148.4 0.8 copy-start.17
  149.2 1.9 copy-start.19
  156.3 149.4 %all-to-all-start = ((bf16[4,2,32768]{2,1,0:T(2,128)(2,1)}), bf16[4,2,32768]{2,1,0:T(2,128)(2,1)}, u32[]{:S(2)}, u32[]{:S(2)}) async-start(bf16[4,2,32768]{2,1,0:T(2,128)(2,1)} %reshape.877), calls=%async_computation | async-start | bytes 1048576 | tf_op jit(solution)/shard_map/all_to_all | solution.py:111
  161.1 139.5 %all-reduce.34.cloned.1.call-start = ((), (), s32[]{:S(2)}) async-start(), calls=%async_computation.2 | async-start | bytes 1048576 | tf_op jit(solution)/shard_map/psum | solution.py:150
  161.1 13.9 %collective-permute-start.4 = (bf16[1,32,4,64]{2,1,3,0:T(8,128)(2,1)}, bf16[1,32,4,64]{2,1,3,0:T(8,128)(2,1)S(1)}, u32[]{:S(2)}, u32[]{:S(2)}) collective-permute-start(bf16[1,32,4,64]{2,1,3,0:T(8,128)(2,1)} %get-tuple-element.38), channel_id=1, source_target_pairs={{0,2},{1,3},{4,6},{5,7},{8,10},{9,11},{12,14},{13,15},{16,18},{17,... | collective-permute-start | bytes 49160 | tf_op jit(solution)/shard_map/ppermute | solution.py:22
  167.7 1.2 copy-start.1
  177.2 0.8 copy-start.61
  180.2 0.7 copy-start.33
  180.6 0.7 copy-start.35
  204.9 97.9 %collective-permute-start.5 = (bf16[1,32,128,30]{2,1,3,0:T(8,128)(2,1)S(1)}, bf16[1,32,128,30]{2,1,3,0:T(8,128)(2,1)S(1)}, u32[]{:S(2)}, u32[]{:S(2)}) collective-permute-start(bf16[1,32,128,30]{2,1,3,0:T(8,128)(2,1)S(1)} %slice.564), channel_id=1, source_target_pairs={{4,0},{8,4},{12,8},{5,1},{9,5},{13,9},{6,2},{10,6},{14,10},{7,3},{... | collective-permute-start | bytes 737288 | tf_op jit(solution)/shard_map/ppermute | solution.py:12
  (44 other events, 31.2 us)
Sparse Core Ops, SparseCore 0:
  207.2 93.4 all-reduce.33
where the time goes:
time: 323 us; the launch traced here: 317 us
  local copies, waits for them, and re-layouts  96.4 us (30%)
  blocking collectives  60.1 us (19%)
  matrix products  58 us (18%)
  waiting for transfers between devices  46.5 us (14%)
  starting transfers between devices  27.5 us (9%)
  between operations  16 us (5%)
  other arithmetic  12.7 us (4%)
    unnamed x208, local copies, waits for them, and re-layouts  69.7 us
    psum x1, blocking collectives, on_device(): lax.psum((time_grad, fiber_grad), ('tm', 'fiber', 'rep'))  60.1 us
    psum x1, waiting for transfers between devices, on_device(): lax.psum((time_grad, fiber_grad), ('tm', 'fiber', 'rep'))  30.6 us
    dot_general x9, matrix products, on_device(): jnp.einsum('boct,bict->oi', d_pre, inner_ext[:, :, tap:tap + chans], pref...  14.8 us
    dot_general x32, matrix products, time_backward(): jnp.einsum('oi,boct->bict', time_kernel[:, :, tap], gradient, preferred_e...  10.9 us
    dot_general x32, matrix products, time_forward(): jnp.einsum('oi,bict->boct', time_kernel[:, :, tap], piece, preferred_elem...  9.82 us
    ppermute x2, starting transfers between devices, padded(): before = lax.ppermute(last, axis, up)  9.41 us
    dot_general x32, matrix products, time_weight_grad(): jnp.einsum('boct,bict->oi', gradient, piece, preferred_element_type=jnp.f...  9.09 us
  transfers between devices with their start and end apart: 9, of which 4 were waited for; matrix products, arithmetic and copies ran while one was open for 44% of the time, Pallas kernels for 0%

commit v1 on v0

v1 whole, which is shorter than its diff:
```python
import functools
import math

import jax
import jax.numpy as jnp
from jax import lax
from jax.experimental import pallas as pl
from jax.experimental.pallas import tpu as pltpu
from jax.sharding import PartitionSpec as P

F = 32
PER = 4
TAPS = 32
KF = 9
REACH = KF // 2
CH = 128
STEPS = 128
TOUT = STEPS // 2
HALO = 32
TB = 8
WIN = (2 * TB + TAPS) * F
TG = 4
GROWS = TG * F
NG = TOUT // TG
VWIN = 24 * F
LATE = 16
BF = jnp.bfloat16
F32 = jnp.float32
NT = (((1,), (1,)), ((), ()))
VMEM_LIMIT = 56 * 1024 * 1024


def call(kernel, outs, *args, scratch=(), name=None):
    return pl.pallas_call(
        kernel,
        out_shape=outs,
        in_specs=[pl.BlockSpec(memory_space=pltpu.VMEM)] * len(args),
        out_specs=jax.tree.map(lambda o: pl.BlockSpec(memory_space=pltpu.VMEM), outs),
        scratch_shapes=list(scratch),
        compiler_params=pltpu.CompilerParams(vmem_limit_bytes=VMEM_LIMIT),
        name=name,
    )(*args)


def out(shape, dtype):
    return jax.ShapeDtypeStruct(shape, dtype)


def lanes(shape):
    return lax.broadcasted_iota(jnp.int32, shape, len(shape) - 1)


def rows(shape):
    return lax.broadcasted_iota(jnp.int32, shape, len(shape) - 2)


def roll(x, by, axis=1):
    by = by % x.shape[axis]
    return x if by == 0 else pltpu.roll(x, by, axis)


def pack_kernel(strain_ref, cot_ref, cot_out, halo_out, scratch):
    n = cot_out.shape[0]
    low = lanes((1, 128)) < TOUT
    for f2 in range(F // 2):
        for tile in range(n // 2):
            a = cot_ref[2 * f2, :, 128 * tile : 128 * (tile + 1)].astype(F32)
            b = cot_ref[2 * f2 + 1, :, 128 * tile : 128 * (tile + 1)].astype(F32)
            cot_out[2 * tile, f2] = jnp.where(low, a, roll(b, TOUT)).astype(BF)
            cot_out[2 * tile + 1, f2] = jnp.where(low, roll(a, TOUT), b).astype(BF)
    group = lanes((1, 128)) // HALO
    for i4 in range(F // 4):
        tile = strain_ref[4 * i4].astype(F32)
        tile = roll(tile, HALO)
        for e in range(1, 4):
            other = roll(strain_ref[4 * i4 + e].astype(F32), HALO * (e + 1))
            tile = jnp.where(group == e, other, tile)
        turned = tile.T
        for e in range(4):
            scratch[pl.ds(4 * i4 + e, HALO, stride=F), :] = turned[HALO * e : HALO * (e + 1)]
    halo_out[...] = scratch[...].astype(BF)


def turn_kernel(strain_ref, out_ref, scratch):
    for i in range(F):
        scratch[pl.ds(i, STEPS, stride=F), :] = strain_ref[i].astype(F32).T
    out_ref[...] = scratch[...].astype(BF)


def weight_kernel(wb_ref, vb_ref, d_ref, dt_ref, w_out, v_out, d_out, dt_out):
    base = wb_ref[...].astype(F32)
    base = jnp.concatenate([base, jnp.zeros((F, WIN - base.shape[1]), F32)], axis=1)
    for t in range(TB):
        w_out[F * t : F * (t + 1)] = roll(base, 2 * F * (t + 1)).astype(BF)
    for p in range(2):
        part = vb_ref[F * p : F * (p + 1)].astype(F32)
        part = jnp.concatenate([part, jnp.zeros((F, VWIN - part.shape[1]), F32)], axis=1)
        for h in range(TB):
            v_out[F * (2 * h + p) : F * (2 * h + p + 1)] = roll(part, F * h).astype(BF)
    step = (lanes((1, KF * GROWS)) % GROWS) // F
    for t in range(TG):
        d_out[F * t : F * (t + 1)] = jnp.where(step == t, d_ref[...].astype(F32), 0.0).astype(BF)
        dt_out[F * t : F * (t + 1)] = jnp.where(step == t, dt_ref[...].astype(F32), 0.0).astype(BF)


def pack_edges(read):
    group = lanes((1, 128)) // 8
    packed = jnp.zeros((GROWS, CH), F32)
    for g in range(NG):
        packed = jnp.where(group == g, roll(read(g), 8 * g + REACH), packed)
    return packed.astype(BF)


def edges_of(before_ref, after_ref):
    me, size = lax.axis_index("fiber"), lax.axis_size("fiber")
    first = lanes((1, 128)) % 8 < REACH
    keep_before = jnp.where(me > 0, 1.0, 0.0).astype(F32)
    keep_after = jnp.where(me < size - 1, 1.0, 0.0).astype(F32)
    return jnp.where(first, before_ref[...].astype(F32) * keep_before, after_ref[...].astype(F32) * keep_after)


def shifted_stack(tile, edges, g, shifts):
    around = roll(edges, -(8 * g + REACH))
    lane = lanes((1, 128))
    pieces = []
    for by in shifts:
        if by > 0:
            piece = roll(jnp.where(lane < by, around, tile), -by)
        elif by < 0:
            piece = roll(jnp.where(lane >= CH + by, around, tile), -by)
        else:
            piece = tile
        pieces.append(piece.astype(BF))
    return jnp.concatenate(pieces, axis=0)


def window(early_ref, main_ref, b, size):
    start = 2 * TB * F * b
    early = early_ref.shape[0]
    if start >= early:
        return main_ref[start - early : start - early + size]
    return jnp.concatenate([early_ref[start:early], main_ref[0 : size - (early - start)]], axis=0)


def inner_kernel(halo_ref, strain_ref, w_ref, u_out, edge_out, scratch):
    size = TB * F
    for b in range(0, TOUT // TB, 2):
        pair = jnp.concatenate([window(halo_ref, strain_ref, b + k, WIN) for k in range(2)], axis=1)
        u = jnp.dot(w_ref[...], pair, preferred_element_type=F32)
        for k in range(2):
            scratch[size * (b + k) : size * (b + k + 1)] = u[:, CH * k : CH * (k + 1)]
            u_out[size * (b + k) : size * (b + k + 1)] = u[:, CH * k : CH * (k + 1)].astype(BF)
    edge_out[...] = pack_edges(lambda g: scratch[GROWS * g : GROWS * (g + 1)])


def forward_kernel(u_ref, before_ref, after_ref, d_ref, act_out, slope_out, scratch):
    edges = edges_of(before_ref, after_ref)
    for g in range(0, NG, 2):
        pair = jnp.concatenate(
            [
                shifted_stack(
                    u_ref[GROWS * (g + k) : GROWS * (g + k + 1)].astype(F32), edges, g + k, range(-REACH, REACH + 1)
                )
                for k in range(2)
            ],
            axis=1,
        )
        z = jnp.dot(d_ref[...], pair, preferred_element_type=F32).astype(BF).astype(F32)
        half = 0.5 * (1.0 + lax.erf(z * (1.0 / math.sqrt(2.0))))
        slope = half + z * jnp.exp(-0.5 * z * z) * (1.0 / math.sqrt(2.0 * math.pi))
        act = z * half
        for k in range(2):
            where = slice(GROWS * (g + k), GROWS * (g + k + 1))
            scratch[where] = act[:, CH * k : CH * (k + 1)]
            slope_out[where] = slope[:, CH * k : CH * (k + 1)]
    n, _, local, _ = act_out.shape
    for f2 in range(F // 2):
        both = jnp.concatenate([scratch[pl.ds(2 * f2 + e, TOUT, stride=F), :] for e in range(2)], axis=0)
        turned = both.T
        for q in range(n):
            act_out[q, f2] = turned[local * q : local * (q + 1)].astype(BF)


def slope_kernel(slope_ref, cot_ref, dz_out, edge_out, scratch):
    n, _, local, _ = cot_ref.shape
    for f2 in range(F // 2):
        turned = cot_ref[:, f2].astype(F32).reshape(CH, 128).T
        for e in range(2):
            scratch[pl.ds(2 * f2 + e, TOUT, stride=F), :] = turned[TOUT * e : TOUT * (e + 1)]
    dz = (scratch[...] * slope_ref[...]).astype(BF)
    dz_out[...] = dz
    scratch[...] = dz.astype(F32)
    edge_out[...] = pack_edges(lambda g: scratch[GROWS * g : GROWS * (g + 1)])


def backward_kernel(dz_ref, before_ref, after_ref, dt_ref, u_ref, halo_ref, strain_ref, du_out, grad_out):
    edges = edges_of(before_ref, after_ref)
    taps = jnp.zeros((GROWS, KF * GROWS), F32)
    for g in range(0, NG, 2):
        stacks = [
            shifted_stack(
                dz_ref[GROWS * (g + k) : GROWS * (g + k + 1)].astype(F32),
                edges,
                g + k,
                [REACH - m for m in range(KF)],
            )
            for k in range(2)
        ]
        pair = jnp.concatenate(stacks, axis=1)
        du = jnp.dot(dt_ref[...], pair, preferred_element_type=F32).astype(BF)
        u = jnp.concatenate([u_ref[GROWS * (g + k) : GROWS * (g + k + 1)] for k in range(2)], axis=1)
        taps = taps + lax.dot_general(u, pair, NT, preferred_element_type=F32)
        for k in range(2):
            du_out[GROWS * (g + k) : GROWS * (g + k + 1)] = du[:, CH * k : CH * (k + 1)]
    lane = lanes((1, KF * GROWS))
    step = (lane % GROWS) // F
    kept = jnp.where(step == 0, taps[0:F], 0.0)
    for t in range(1, TG):
        kept = jnp.where(step == t, taps[F * t : F * (t + 1)], kept)
    feat = lane % F
    row = rows((F, 1))
    lines = []
    for j in range(PER):
        lines.append(jnp.sum(jnp.where(row == feat // PER * PER + j, kept, 0.0), axis=0, keepdims=True))
    lines = jnp.concatenate(lines + [jnp.zeros((8 - PER, KF * GROWS), F32)], axis=0)
    tiles = []
    for top in range(0, KF, TG):
        tile = jnp.zeros((8, GROWS), F32)
        for m in range(top, min(KF, top + TG)):
            line = lines[:, GROWS * m : GROWS * (m + 1)]
            total = line
            for t in range(1, TG):
                total = total + roll(line, F * t)
            tile = jnp.where(lanes((1, GROWS)) // F == m - top, total, tile)
        tiles.append(tile)
    size = TB * F
    wide = jnp.zeros((size, WIN), F32)
    for b in range(0, TOUT // TB, 2):
        left = jnp.concatenate([du_out[size * (b + k) : size * (b + k + 1)] for k in range(2)], axis=1)
        right = jnp.concatenate([window(halo_ref, strain_ref, b + k, WIN) for k in range(2)], axis=1)
        wide = wide + lax.dot_general(left, right, NT, preferred_element_type=F32)
    total = jnp.zeros((F, WIN), F32)
    for t in range(TB):
        total = total + roll(wide[F * t : F * (t + 1)], -2 * F * (t + 1))
    grad_out[0:F] = total[:, 0 : TAPS * F]
    tiles.append(jnp.zeros((8, TAPS * F - len(tiles) * GROWS), F32))
    grad_out[F : F + 8] = jnp.concatenate(tiles, axis=1)


def signal_kernel(du_ref, late_ref, v_ref, grad_out, scratch):
    size = TB * F
    last = TOUT * F

    def rows_of(b):
        start, stop = size * b, size * b + VWIN
        if stop <= last:
            return du_ref[start:stop]
        return jnp.concatenate([du_ref[start:last], late_ref[0 : stop - last]], axis=0)

    step = 2 * TB * F
    for b in range(0, TOUT // TB, 2):
        pair = jnp.concatenate([rows_of(b + k) for k in range(2)], axis=1)
        part = jnp.dot(v_ref[...], pair, preferred_element_type=F32)
        for k in range(2):
            scratch[step * (b + k) : step * (b + k + 1)] = part[:, CH * k : CH * (k + 1)]
    for i in range(F):
        grad_out[i] = scratch[pl.ds(i, STEPS, stride=F), :].T.astype(BF)


def unpack_kernel(act_ref, act_out):
    n = act_ref.shape[0]
    low = lanes((1, 128)) < TOUT
    for f2 in range(F // 2):
        for tile in range(n // 2):
            a = act_ref[2 * tile, f2].astype(F32)
            b = act_ref[2 * tile + 1, f2].astype(F32)
            where = slice(128 * tile, 128 * (tile + 1))
            act_out[2 * f2, :, where] = jnp.where(low, a, roll(b, TOUT)).astype(BF)
            act_out[2 * f2 + 1, :, where] = jnp.where(low, roll(a, TOUT), b).astype(BF)


def neighbours(array, axis):
    size = lax.axis_size(axis)
    if size == 2:
        other = lax.ppermute(array, axis, [(0, 1), (1, 0)])
        return other, other
    before = lax.ppermute(array, axis, [(i, i + 1) for i in range(size - 1)])
    after = lax.ppermute(array, axis, [(i + 1, i) for i in range(size - 1)])
    return before, after


def summed(array, axes):
    for axis in axes:
        size = lax.axis_size(axis)
        hop = 1
        while hop < size:
            mine = array.astype(BF)
            other = lax.ppermute(mine, axis, [(i, i ^ hop) for i in range(size)])
            array = mine.astype(F32) + other.astype(F32)
            hop *= 2
    return array


def on_device(strain, time_kernel, fiber_kernel, cotangent):
    n = lax.axis_size("tm")
    size = lax.axis_size("rep") * CH * lax.axis_size("fiber") * TOUT * n
    scale = 1.0 / math.sqrt(size)
    local = cotangent.shape[3]
    x = strain[0]
    packed = (n, F // 2, local, 128)
    sent, tail = call(
        pack_kernel,
        (out(packed, BF), out((HALO * F, CH), BF)),
        x,
        cotangent[0, :, 0],
        scratch=[pltpu.VMEM((HALO * F, CH), F32)],
        name="pack",
    )
    upstream = lax.all_to_all(sent, "tm", 0, 0, tiled=True)
    halo = lax.ppermute(tail, "tm", [(i, i + 1) for i in range(n - 1)])

    wb = jnp.transpose(time_kernel, (0, 2, 1)).reshape(F, TAPS * F)
    vb = time_kernel.reshape(F, F, TAPS // 2, 2)[:, :, ::-1]
    vb = jnp.transpose(vb, (3, 1, 2, 0)).reshape(2 * F, TAPS // 2 * F)
    ids = jnp.arange(F, dtype=jnp.int32) // PER
    same = ids[:, None] == ids[None, :]
    dense = jnp.where(same[:, :, None], jnp.tile(fiber_kernel, (1, F // PER, 1)), jnp.zeros((), BF))
    d0 = jnp.tile(jnp.transpose(dense, (0, 2, 1)), (1, 1, TG)).reshape(F, KF * GROWS)
    dt0 = jnp.tile(jnp.transpose(dense, (1, 2, 0)), (1, 1, TG)).reshape(F, KF * GROWS)
    w, v, d, dt = call(
        weight_kernel,
        (
            out((TB * F, WIN), BF),
            out((2 * TB * F, VWIN), BF),
            out((GROWS, KF * GROWS), BF),
            out((GROWS, KF * GROWS), BF),
        ),
        wb,
        vb,
        d0,
        dt0,
        name="weights",
    )
    (turned,) = call(
        turn_kernel, (out((STEPS * F, CH), BF),), x, scratch=[pltpu.VMEM((STEPS * F, CH), F32)], name="turn"
    )
    flat = (TOUT * F, CH)
    u, u_edge = call(
        inner_kernel,
        (out(flat, BF), out((GROWS, CH), BF)),
        halo,
        turned,
        w,
        scratch=[pltpu.VMEM(flat, F32)],
        name="inner",
    )
    before, after = neighbours(u_edge, "fiber")
    act, slope = call(
        forward_kernel,
        (out(packed, BF), out(flat, F32)),
        u,
        before,
        after,
        d,
        scratch=[pltpu.VMEM(flat, F32)],
        name="forward",
    )
    act = lax.all_to_all(act, "tm", 0, 0, tiled=True)
    dz, dz_edge = call(
        slope_kernel,
        (out(flat, BF), out((GROWS, CH), BF)),
        slope,
        upstream,
        scratch=[pltpu.VMEM(flat, F32)],
        name="slope",
    )
    before, after = neighbours(dz_edge, "fiber")
    du, grads = call(
        backward_kernel,
        (out(flat, BF), out((F + 8, TAPS * F), F32)),
        dz,
        before,
        after,
        dt,
        u,
        halo,
        turned,
        name="backward",
    )
    late = lax.ppermute(du[0 : LATE * F], "tm", [(i + 1, i) for i in range(n - 1)])
    grads = summed(grads, ("rep", "fiber", "tm")) * scale
    (strain_grad,) = call(
        signal_kernel,
        (out((F, CH, STEPS), BF),),
        du,
        late,
        v,
        scratch=[pltpu.VMEM((STEPS * F, CH), F32)],
        name="signal",
    )
    (activation,) = call(unpack_kernel, (out((F, local, n * TOUT), BF),), act, name="unpack")
    time_grad = jnp.transpose(grads[0:F].reshape(F, TAPS, F), (0, 2, 1))
    fiber_grad = grads[F : F + PER, 0 : KF * F].reshape(PER, KF, F)
    fiber_grad = jnp.transpose(fiber_grad, (2, 0, 1))
    return activation[None, :, None], strain_grad[None], time_grad, fiber_grad


def solution(mesh):
    placed = (
        P(("parts", "rep"), None, "fiber", "tm"),
        P(),
        P(),
        P(("parts", "rep"), None, "fiber", "tm", None),
    )
    return jax.shard_map(
        on_device,
        mesh=mesh,
        in_specs=placed,
        out_specs=(
            P(("parts", "rep"), None, "fiber", "tm", None),
            P(("parts", "rep"), None, "fiber", "tm"),
            P("parts", None, None),
            P("parts", None, None),
        ),
        check_vma=False,
    )
```

time: 323 us -> 89.9 us (0.28)
  the two profiles are of different devices: /device:TPU:0 before, /device:TPU:12 now
where the time goes in v1:
time: 89.9 us; the launch traced here: 89.2 us
  Pallas kernels  32.7 us (36%)
  starting transfers between devices  25.4 us (28%)
  waiting for transfers between devices  17.5 us (19%)
  local copies, waits for them, and re-layouts  11.7 us (13%)
  other arithmetic  1.12 us (1%)
    pallas_call x9, Pallas kernels, call(): pl.pallas_call(kernel, out_shape=outs, in_specs=[pl.BlockSpec(memory_spac...  32.7 us
    all_to_all x1, starting transfers between devices, on_device(): upstream = lax.all_to_all(sent, 'tm', 0, 0, tiled=True)  5.45 us
    all_to_all x1, starting transfers between devices, on_device(): act = lax.all_to_all(act, 'tm', 0, 0, tiled=True)  5.35 us
    unnamed x23, local copies, waits for them, and re-layouts  5.31 us
    ppermute x2, waiting for transfers between devices, neighbours(): other = lax.ppermute(array, axis, [(0, 1), (1, 0)])  5.27 us
    ppermute x1, waiting for transfers between devices, on_device(): lax.ppermute(du[0:LATE * F], 'tm', [(i + 1, i) for i in range(n - 1)])  4.99 us
    ppermute x4, waiting for transfers between devices, summed(): other = lax.ppermute(mine, axis, [(i, i ^ hop) for i in range(size)])  4.96 us
    ppermute x4, starting transfers between devices, summed(): other = lax.ppermute(mine, axis, [(i, i ^ hop) for i in range(size)])  4.27 us
  transfers between devices with their start and end apart: 10, of which 6 were waited for; matrix products, arithmetic and copies ran while one was open for 6% of the time, Pallas kernels for 23%

profile of v1, /device:TPU:12, one launch (start us, length us, event | category | flops | bytes accessed | tf_op | source)
XLA Modules:
  0.0 89.2 jit_solution(15651347547697773482)
XLA Ops:
  0.6 2.9 %pack.1 = (bf16[4,16,32,128]{3,2,1,0:T(8,128)(2,1)}, bf16[1024,128]{1,0:T(8,128)(2,1)}) custom-call(bf16[32,128,128]{2,1,0:T(8,128)(2,1)} %bitcast.18, bf16[32,32,256]{2,1,0:T(8,128)(2,1)} %bitcast.25), custom_call_target="tpu_custom_call" | custom-call | tf_op jit(solution)/shard_map/pack/pallas_call | solution.py:34
  3.6 5.4 %all-to-all-start.1 = ((bf16[4,16,32,128]{3,2,1,0:T(8,128)(2,1)}), bf16[4,16,32,128]{3,2,1,0:T(8,128)(2,1)S(1)}, u32[]{:S(2)}, u32[]{:S(2)}) async-start(bf16[4,16,32,128]{3,2,1,0:T(8,128)(2,1)} %get-tuple-element.25), calls=%async_computation.1 | async-start | bytes 1048576 | tf_op jit(solution)/shard_map/all_to_all | solution.py:319
  9.0 3.5 %collective-permute-start = (bf16[1024,128]{1,0:T(8,128)(2,1)S(1)}, bf16[1024,128]{1,0:T(8,128)(2,1)S(1)}, u32[]{:S(2)}, u32[]{:S(2)}) collective-permute-start(bf16[1024,128]{1,0:T(8,128)(2,1)S(1)} %copy-done.9), channel_id=1, source_target_pairs={{0,4},{4,8},{8,12},{1,5},{5,9},{9,13},{2,6},{6,10},{10,14},{3,7},{... | collective-permute-start | bytes 786440 | tf_op jit(solution)/shard_map/ppermute | solution.py:320
  12.5 3.6 %turn.1.strain_ref = bf16[4096,128]{1,0:T(8,128)(2,1)} custom-call(bf16[32,128,128]{2,1,0:T(8,128)(2,1)} %bitcast.19), custom_call_target="tpu_custom_call" | custom-call | tf_op jit(solution)/shard_map/turn/pallas_call | solution.py:34
  16.1 0.1 broadcast_compare_fusion
  16.2 0.2 copy.19
  16.4 0.1 tile.27
  16.5 0.8 tile.28.d_ref
  17.4 0.1 copy-done.2
  17.5 0.4 copy.16
  17.9 0.2 copy.15
  18.1 0.9 %reshape.88.wb_ref = bf16[32,1024]{1,0:T(8,128)(2,1)} reshape(bf16[32,32,32]{2,1,0:T(8,128)(2,1)S(1)} %copy.15) | data formatting | bytes 131072 | tf_op jit(solution)/shard_map/reshape | solution.py:322
  19.0 0.3 copy.17
  19.3 0.9 reshape.90.vb_ref
  20.1 0.1 tile.29
  20.2 0.8 tile.30.dt_ref
  21.0 2.4 %weights.1 = (bf16[256,1536]{1,0:T(8,128)(2,1)}, bf16[512,768]{1,0:T(8,128)(2,1)}, bf16[128,1152]{1,0:T(8,128)(2,1)}, bf16[128,1152]{1,0:T(8,128)(2,1)}) custom-call(bf16[32,1024]{1,0:T(8,128)(2,1)} %reshape.88.wb_ref, bf16[64,512]{1,0:T(8,128)(2,1)} %reshape.90.vb_ref, bf16[32,1152]{1,0:T(8,128)(2,1)} %tile.28.d_ref, bf16[32,1152]{1,0:T(8,128)(2,1)} %tile.30.dt_ref), custom_call_target="tpu_custom_call" | custom-call | tf_op jit(solution)/shard_map/weights/pallas_call | solution.py:34
  23.5 2.3 %collective-permute-done.halo_ref = bf16[1024,128]{1,0:T(8,128)(2,1)S(1)} collective-permute-done((bf16[1024,128]{1,0:T(8,128)(2,1)S(1)}, bf16[1024,128]{1,0:T(8,128)(2,1)S(1)}, u32[]{:S(2)}, u32[]{:S(2)}) %collective-permute-start) | collective-permute-done | bytes 262176 | tf_op jit(solution)/shard_map/ppermute | solution.py:320
  25.7 0.7 copy-done.3
  26.4 3.3 %inner.1 = (bf16[2048,128]{1,0:T(8,128)(2,1)}, bf16[128,128]{1,0:T(8,128)(2,1)}) custom-call(bf16[1024,128]{1,0:T(8,128)(2,1)} %copy-done.3, bf16[4096,128]{1,0:T(8,128)(2,1)} %turn.1.strain_ref, bf16[256,1536]{1,0:T(8,128)(2,1)} %get-tuple-element.19.w_ref), custom_call_target="tpu_custom_call" | custom-call | tf_op jit(solution)/shard_map/inner/pallas_call | solution.py:34
  29.8 1.5 %collective-permute-start.1 = (bf16[128,128]{1,0:T(8,128)(2,1)}, bf16[128,128]{1,0:T(8,128)(2,1)S(1)}, u32[]{:S(2)}, u32[]{:S(2)}) collective-permute-start(bf16[128,128]{1,0:T(8,128)(2,1)} %get-tuple-element.21), channel_id=1, source_target_pairs={{0,2},{2,0},{1,3},{3,1},{4,6},{6,4},{5,7},{7,5},{8,10},{10,8},{9,1... | collective-permute-start | bytes 98312 | tf_op jit(solution)/shard_map/ppermute | solution.py:285
  31.2 2.6 %collective-permute-done.1.before_ref.after_ref = bf16[128,128]{1,0:T(8,128)(2,1)S(1)} collective-permute-done((bf16[128,128]{1,0:T(8,128)(2,1)}, bf16[128,128]{1,0:T(8,128)(2,1)S(1)}, u32[]{:S(2)}, u32[]{:S(2)}) %collective-permute-start.1) | collective-permute-done | bytes 32800 | tf_op jit(solution)/shard_map/ppermute | solution.py:285
  33.9 0.6 copy-done.6
  34.5 5.1 %forward.1 = (bf16[4,16,32,128]{3,2,1,0:T(8,128)(2,1)}, f32[2048,128]{1,0:T(8,128)}) custom-call(bf16[2048,128]{1,0:T(8,128)(2,1)} %get-tuple-element.20.u_ref, bf16[128,128]{1,0:T(8,128)(2,1)} %copy-done.6, bf16[128,128]{1,0:T(8,128)(2,1)} %copy-done.6, bf16[128,1152]{1,0:T(8,128)(2,1)} %get-tuple-element.22.d_ref), custom_call_target="tpu_custom_call" | custom-call | tf_op jit(solution)/shard_map/forward/pallas_call | solution.py:34
  39.6 0.8 copy-done
  40.4 3.0 %slope.1 = (bf16[2048,128]{1,0:T(8,128)(2,1)}, bf16[128,128]{1,0:T(8,128)(2,1)}) custom-call(f32[2048,128]{1,0:T(8,128)} %get-tuple-element.24.slope_ref, bf16[4,16,32,128]{3,2,1,0:T(8,128)(2,1)} %copy-done), custom_call_target="tpu_custom_call" | custom-call | tf_op jit(solution)/shard_map/slope/pallas_call | solution.py:34
  43.4 1.5 %collective-permute-start.2 = (bf16[128,128]{1,0:T(8,128)(2,1)}, bf16[128,128]{1,0:T(8,128)(2,1)S(1)}, u32[]{:S(2)}, u32[]{:S(2)}) collective-permute-start(bf16[128,128]{1,0:T(8,128)(2,1)} %get-tuple-element.27), channel_id=1, source_target_pairs={{0,2},{2,0},{1,3},{3,1},{4,6},{6,4},{5,7},{7,5},{8,10},{10,8},{9,1... | collective-permute-start | bytes 98312 | tf_op jit(solution)/shard_map/ppermute | solution.py:285
  44.9 2.6 %collective-permute-done.2.before_ref.after_ref = bf16[128,128]{1,0:T(8,128)(2,1)S(1)} collective-permute-done((bf16[128,128]{1,0:T(8,128)(2,1)}, bf16[128,128]{1,0:T(8,128)(2,1)S(1)}, u32[]{:S(2)}, u32[]{:S(2)}) %collective-permute-start.2) | collective-permute-done | bytes 32800 | tf_op jit(solution)/shard_map/ppermute | solution.py:285
  47.5 0.6 copy-done.5
  48.1 5.9 %backward.1 = (bf16[2048,128]{1,0:T(8,128)(2,1)}, f32[40,1024]{1,0:T(8,128)}) custom-call(bf16[2048,128]{1,0:T(8,128)(2,1)} %get-tuple-element.26.dz_ref, bf16[128,128]{1,0:T(8,128)(2,1)} %copy-done.5, bf16[128,128]{1,0:T(8,128)(2,1)} %copy-done.5, bf16[128,1152]{1,0:T(8,128)(2,1)} %get-tuple-element.28.dt_ref, bf16[2048,128]{1,0:T(8,128)(2,1)} %get-tuple-element.20.u_ref, ...), custom_call_target="tpu_custom_call" | custom-call | tf_op jit(solution)/shard_map/backward/pallas_call | solution.py:34
  54.0 0.9 %convert_element_type.36 = bf16[40,1024]{1,0:T(8,128)(2,1)S(1)} convert(f32[40,1024]{1,0:T(8,128)} %get-tuple-element.31) | non-fusion elementwise | flops 40960 | bytes 245760 | tf_op jit(solution)/shard_map/convert_element_type | solution.py:297
  55.1 5.4 %all-to-all-start = ((bf16[4,16,32,128]{3,2,1,0:T(8,128)(2,1)}), bf16[4,16,32,128]{3,2,1,0:T(8,128)(2,1)S(1)}, u32[]{:S(2)}, u32[]{:S(2)}) async-start(bf16[4,16,32,128]{3,2,1,0:T(8,128)(2,1)} %get-tuple-element.23), calls=%async_computation | async-start | bytes 1048576 | tf_op jit(solution)/shard_map/all_to_all | solution.py:368
  60.4 1.6 %collective-permute-start.5 = (bf16[40,1024]{1,0:T(8,128)(2,1)S(1)}, bf16[40,1024]{1,0:T(8,128)(2,1)S(1)}, u32[]{:S(2)}, u32[]{:S(2)}) collective-permute-start(bf16[40,1024]{1,0:T(8,128)(2,1)S(1)} %add_convert_fusion.2), channel_id=1, source_target_pairs={{0,2},{2,0},{1,3},{3,1},{4,6},{6,4},{5,7},{7,5},{8,10},{10,8},{9,1... | collective-permute-start | bytes 245768 | tf_op jit(solution)/shard_map/ppermute | solution.py:298
  62.0 3.0 %collective-permute-done.5 = bf16[40,1024]{1,0:T(8,128)(2,1)S(1)} collective-permute-done((bf16[40,1024]{1,0:T(8,128)(2,1)S(1)}, bf16[40,1024]{1,0:T(8,128)(2,1)S(1)}, u32[]{:S(2)}, u32[]{:S(2)}) %collective-permute-start.5) | collective-permute-done | bytes 81952 | tf_op jit(solution)/shard_map/ppermute | solution.py:298
  65.0 0.2 collective-permute-start.6
  65.1 0.9 %slice.9 = bf16[512,128]{1,0:T(8,128)(2,1)S(1)} slice(bf16[2048,128]{1,0:T(8,128)(2,1)} %get-tuple-element.29.du_ref), slice={[0:512], [0:128]} | slice | bytes 262144 | tf_op jit(solution)/shard_map/slice | solution.py:390
  66.1 3.8 %collective-permute-start.3 = (bf16[512,128]{1,0:T(8,128)(2,1)S(1)}, bf16[512,128]{1,0:T(8,128)(2,1)S(1)}, u32[]{:S(2)}, u32[]{:S(2)}) collective-permute-start(bf16[512,128]{1,0:T(8,128)(2,1)S(1)} %slice.9), channel_id=1, source_target_pairs={{4,0},{8,4},{12,8},{5,1},{9,5},{13,9},{6,2},{10,6},{14,10},{7,3},{... | collective-permute-start | bytes 393224 | tf_op jit(solution)/shard_map/ppermute | solution.py:390
  69.9 2.0 %collective-permute-done.6 = bf16[40,1024]{1,0:T(8,128)(2,1)S(1)} collective-permute-done((bf16[40,1024]{1,0:T(8,128)(2,1)S(1)}, bf16[40,1024]{1,0:T(8,128)(2,1)S(1)}, u32[]{:S(2)}, u32[]{:S(2)}) %collective-permute-start.6) | collective-permute-done | bytes 81952 | tf_op jit(solution)/shard_map/ppermute | solution.py:298
  71.9 2.5 %collective-permute-start.7 = (bf16[40,1024]{1,0:T(8,128)(2,1)S(1)}, bf16[40,1024]{1,0:T(8,128)(2,1)S(1)}, u32[]{:S(2)}, u32[]{:S(2)}) collective-permute-start(bf16[40,1024]{1,0:T(8,128)(2,1)S(1)} %add_convert_fusion), channel_id=1, source_target_pairs={{0,8},{4,12},{8,0},{12,4},{1,9},{5,13},{9,1},{13,5},{2,10},{6,14},... | collective-permute-start | bytes 245768 | tf_op jit(solution)/shard_map/ppermute | solution.py:298
  74.4 5.0 %collective-permute-done.3.late_ref = bf16[512,128]{1,0:T(8,128)(2,1)S(1)} collective-permute-done((bf16[512,128]{1,0:T(8,128)(2,1)S(1)}, bf16[512,128]{1,0:T(8,128)(2,1)S(1)}, u32[]{:S(2)}, u32[]{:S(2)}) %collective-permute-start.3) | collective-permute-done | bytes 131104 | tf_op jit(solution)/shard_map/ppermute | solution.py:390
  79.4 0.7 copy-done.7
  80.0 4.4 %signal.1 = bf16[32,128,128]{2,1,0:T(8,128)(2,1)} custom-call(bf16[2048,128]{1,0:T(8,128)(2,1)} %get-tuple-element.29.du_ref, bf16[512,128]{1,0:T(8,128)(2,1)} %copy-done.7, bf16[512,768]{1,0:T(8,128)(2,1)} %get-tuple-element.30.v_ref), custom_call_target="tpu_custom_call" | custom-call | tf_op jit(solution)/shard_map/signal/pallas_call | solution.py:34
  84.4 0.8 copy-done.1
  85.2 2.1 %unpack.1 = bf16[32,32,256]{2,1,0:T(8,128)(2,1)} custom-call(bf16[4,16,32,128]{3,2,1,0:T(8,128)(2,1)} %copy-done.1), custom_call_target="tpu_custom_call" | custom-call | tf_op jit(solution)/shard_map/unpack/pallas_call | solution.py:34
  87.3 0.1 reshape.92
  87.4 0.6 copy.22
  88.0 0.2 reshape.91
  88.2 1.0 %copy.20 = f32[32,32,32]{1,2,0:T(8,128)} copy(f32[32,32,32]{2,1,0:T(8,128)S(1)} %reshape.91) | data formatting | bytes 262144 | tf_op jit(solution)/shard_map/reshape | solution.py:402
  (28 shorter events, 0.3 us)
Async XLA Ops:
  3.6 5.5 %copy-start.9 = (bf16[1024,128]{1,0:T(8,128)(2,1)S(1)}, bf16[1024,128]{1,0:T(8,128)(2,1)}, u32[]{:S(2)}) copy-start(bf16[1024,128]{1,0:T(8,128)(2,1)} %get-tuple-element.18) | copy-start | bytes 786436
  3.6 36.0 %all-to-all-start.1 = ((bf16[4,16,32,128]{3,2,1,0:T(8,128)(2,1)}), bf16[4,16,32,128]{3,2,1,0:T(8,128)(2,1)S(1)}, u32[]{:S(2)}, u32[]{:S(2)}) async-start(bf16[4,16,32,128]{3,2,1,0:T(8,128)(2,1)} %get-tuple-element.25), calls=%async_computation.1 | async-start | bytes 1048576 | tf_op jit(solution)/shard_map/all_to_all | solution.py:319
  9.0 7.1 %copy-start.8 = (bf16[32,4,9]{0,1,2:T(4,128)(2,1)S(1)}, bf16[32,4,9]{0,1,2:T(4,128)(2,1)}, u32[]{:S(2)}) copy-start(bf16[32,4,9]{0,1,2:T(4,128)(2,1)} %param.6) | copy-start | bytes 6916
  9.0 16.7 %collective-permute-start = (bf16[1024,128]{1,0:T(8,128)(2,1)S(1)}, bf16[1024,128]{1,0:T(8,128)(2,1)S(1)}, u32[]{:S(2)}, u32[]{:S(2)}) collective-permute-start(bf16[1024,128]{1,0:T(8,128)(2,1)S(1)} %copy-done.9), channel_id=1, source_target_pairs={{0,4},{4,8},{8,12},{1,5},{5,9},{9,13},{2,6},{6,10},{10,14},{3,7},{... | collective-permute-start | bytes 786440 | tf_op jit(solution)/shard_map/ppermute | solution.py:320
  16.5 1.0 %copy-start.2 = (bf16[32,32,32]{2,1,0:T(8,128)(2,1)S(1)}, bf16[32,32,32]{2,1,0:T(8,128)(2,1)}, u32[]{:S(2)}) copy-start(bf16[32,32,32]{2,1,0:T(8,128)(2,1)} %param.5) | copy-start | bytes 196612
  25.7 0.7 copy-start.3
  29.8 4.1 %collective-permute-start.1 = (bf16[128,128]{1,0:T(8,128)(2,1)}, bf16[128,128]{1,0:T(8,128)(2,1)S(1)}, u32[]{:S(2)}, u32[]{:S(2)}) collective-permute-start(bf16[128,128]{1,0:T(8,128)(2,1)} %get-tuple-element.21), channel_id=1, source_target_pairs={{0,2},{2,0},{1,3},{3,1},{4,6},{6,4},{5,7},{7,5},{8,10},{10,8},{9,1... | collective-permute-start | bytes 98312 | tf_op jit(solution)/shard_map/ppermute | solution.py:285
  33.9 0.6 copy-start.6
  39.6 0.8 copy-start
  43.4 4.1 %collective-permute-start.2 = (bf16[128,128]{1,0:T(8,128)(2,1)}, bf16[128,128]{1,0:T(8,128)(2,1)S(1)}, u32[]{:S(2)}, u32[]{:S(2)}) collective-permute-start(bf16[128,128]{1,0:T(8,128)(2,1)} %get-tuple-element.27), channel_id=1, source_target_pairs={{0,2},{2,0},{1,3},{3,1},{4,6},{6,4},{5,7},{7,5},{8,10},{10,8},{9,1... | collective-permute-start | bytes 98312 | tf_op jit(solution)/shard_map/ppermute | solution.py:285
  47.5 0.6 copy-start.5
  55.0 5.4 %collective-permute-start.4 = (bf16[40,1024]{1,0:T(8,128)(2,1)S(1)}, bf16[40,1024]{1,0:T(8,128)(2,1)S(1)}, u32[]{:S(2)}, u32[]{:S(2)}) collective-permute-start(bf16[40,1024]{1,0:T(8,128)(2,1)S(1)} %convert_element_type.36), channel_id=1, source_target_pairs={{0,1},{1,0},{2,3},{3,2},{4,5},{5,4},{6,7},{7,6},{8,9},{9,8},{10,11... | collective-permute-start | bytes 245768 | tf_op jit(solution)/shard_map/ppermute | solution.py:298
  55.0 5.4 %copy-start.4 = (f32[40,1024]{1,0:T(8,128)S(1)}, f32[40,1024]{1,0:T(8,128)}, u32[]{:S(2)}) copy-start(f32[40,1024]{1,0:T(8,128)} %get-tuple-element.31) | copy-start | bytes 491524
  55.1 29.4 %all-to-all-start = ((bf16[4,16,32,128]{3,2,1,0:T(8,128)(2,1)}), bf16[4,16,32,128]{3,2,1,0:T(8,128)(2,1)S(1)}, u32[]{:S(2)}, u32[]{:S(2)}) async-start(bf16[4,16,32,128]{3,2,1,0:T(8,128)(2,1)} %get-tuple-element.23), calls=%async_computation | async-start | bytes 1048576 | tf_op jit(solution)/shard_map/all_to_all | solution.py:368
  60.4 4.5 %collective-permute-start.5 = (bf16[40,1024]{1,0:T(8,128)(2,1)S(1)}, bf16[40,1024]{1,0:T(8,128)(2,1)S(1)}, u32[]{:S(2)}, u32[]{:S(2)}) collective-permute-start(bf16[40,1024]{1,0:T(8,128)(2,1)S(1)} %add_convert_fusion.2), channel_id=1, source_target_pairs={{0,2},{2,0},{1,3},{3,1},{4,6},{6,4},{5,7},{7,5},{8,10},{10,8},{9,1... | collective-permute-start | bytes 245768 | tf_op jit(solution)/shard_map/ppermute | solution.py:298
  65.0 6.9 %collective-permute-start.6 = (bf16[40,1024]{1,0:T(8,128)(2,1)S(1)}, bf16[40,1024]{1,0:T(8,128)(2,1)S(1)}, u32[]{:S(2)}, u32[]{:S(2)}) collective-permute-start(bf16[40,1024]{1,0:T(8,128)(2,1)S(1)} %add_convert_fusion.1), channel_id=1, source_target_pairs={{0,4},{4,0},{8,12},{12,8},{1,5},{5,1},{9,13},{13,9},{2,6},{6,2},{1... | collective-permute-start | bytes 245768 | tf_op jit(solution)/shard_map/ppermute | solution.py:298
  66.1 13.3 %collective-permute-start.3 = (bf16[512,128]{1,0:T(8,128)(2,1)S(1)}, bf16[512,128]{1,0:T(8,128)(2,1)S(1)}, u32[]{:S(2)}, u32[]{:S(2)}) collective-permute-start(bf16[512,128]{1,0:T(8,128)(2,1)S(1)} %slice.9), channel_id=1, source_target_pairs={{4,0},{8,4},{12,8},{5,1},{9,5},{13,9},{6,2},{10,6},{14,10},{7,3},{... | collective-permute-start | bytes 393224 | tf_op jit(solution)/shard_map/ppermute | solution.py:390
  71.9 15.4 %collective-permute-start.7 = (bf16[40,1024]{1,0:T(8,128)(2,1)S(1)}, bf16[40,1024]{1,0:T(8,128)(2,1)S(1)}, u32[]{:S(2)}, u32[]{:S(2)}) collective-permute-start(bf16[40,1024]{1,0:T(8,128)(2,1)S(1)} %add_convert_fusion), channel_id=1, source_target_pairs={{0,8},{4,12},{8,0},{12,4},{1,9},{5,13},{9,1},{13,5},{2,10},{6,14},... | collective-permute-start | bytes 245768 | tf_op jit(solution)/shard_map/ppermute | solution.py:298
  79.4 0.7 copy-start.7
  84.4 0.8 copy-start.1

commit v2 on v1

--- a/solution.py
+++ b/solution.py
@@ -27,7 +27,7 @@
 BF = jnp.bfloat16
 F32 = jnp.float32
 NT = (((1,), (1,)), ((), ()))
-VMEM_LIMIT = 56 * 1024 * 1024
+VMEM_LIMIT = 16 * 1024 * 1024
 
 
 def call(kernel, outs, *args, scratch=(), name=None):
@@ -59,23 +59,38 @@
     return x if by == 0 else pltpu.roll(x, by, axis)
 
 
-def pack_kernel(strain_ref, cot_ref, cot_out, halo_out, scratch):
-    n = cot_out.shape[0]
+def place(chunks, refs):
+    me = lax.axis_index("tm")
+    for hop, ref in enumerate(refs):
+        ref[...] = chunks[me ^ hop]
+
+
+def gather(chunks, refs):
+    me = lax.axis_index("tm")
+    for hop, ref in enumerate(refs):
+        chunks[me ^ hop] = ref[...]
+
+
+def pack_kernel(cot_ref, *refs):
+    chunks = refs[-1]
+    n = chunks.shape[0]
     low = lanes((1, 128)) < TOUT
     for f2 in range(F // 2):
         for tile in range(n // 2):
-            a = cot_ref[2 * f2, :, 128 * tile : 128 * (tile + 1)].astype(F32)
-            b = cot_ref[2 * f2 + 1, :, 128 * tile : 128 * (tile + 1)].astype(F32)
-            cot_out[2 * tile, f2] = jnp.where(low, a, roll(b, TOUT)).astype(BF)
-            cot_out[2 * tile + 1, f2] = jnp.where(low, roll(a, TOUT), b).astype(BF)
+            a = cot_ref[2 * f2, :, 128 * tile : 128 * (tile + 1)]
+            b = cot_ref[2 * f2 + 1, :, 128 * tile : 128 * (tile + 1)]
+            chunks[2 * tile, f2] = jnp.where(low, a, roll(b, TOUT))
+            chunks[2 * tile + 1, f2] = jnp.where(low, roll(a, TOUT), b)
+    place(chunks, refs[:-1])
+
+
+def tail_kernel(strain_ref, halo_out, scratch):
     group = lanes((1, 128)) // HALO
     for i4 in range(F // 4):
-        tile = strain_ref[4 * i4].astype(F32)
-        tile = roll(tile, HALO)
+        tile = roll(strain_ref[4 * i4], HALO)
         for e in range(1, 4):
-            other = roll(strain_ref[4 * i4 + e].astype(F32), HALO * (e + 1))
-            tile = jnp.where(group == e, other, tile)
-        turned = tile.T
+            tile = jnp.where(group == e, roll(strain_ref[4 * i4 + e], HALO * (e + 1)), tile)
+        turned = tile.T.astype(F32)
         for e in range(4):
             scratch[pl.ds(4 * i4 + e, HALO, stride=F), :] = turned[HALO * e : HALO * (e + 1)]
     halo_out[...] = scratch[...].astype(BF)
@@ -83,7 +98,7 @@
 
 def turn_kernel(strain_ref, out_ref, scratch):
     for i in range(F):
-        scratch[pl.ds(i, STEPS, stride=F), :] = strain_ref[i].astype(F32).T
+        scratch[pl.ds(i, STEPS, stride=F), :] = strain_ref[i].T.astype(F32)
     out_ref[...] = scratch[...].astype(BF)
 
 
@@ -105,10 +120,10 @@
 
 def pack_edges(read):
     group = lanes((1, 128)) // 8
-    packed = jnp.zeros((GROWS, CH), F32)
-    for g in range(NG):
+    packed = roll(read(0), REACH)
+    for g in range(1, NG):
         packed = jnp.where(group == g, roll(read(g), 8 * g + REACH), packed)
-    return packed.astype(BF)
+    return packed
 
 
 def edges_of(before_ref, after_ref):
@@ -116,7 +131,8 @@
     first = lanes((1, 128)) % 8 < REACH
     keep_before = jnp.where(me > 0, 1.0, 0.0).astype(F32)
     keep_after = jnp.where(me < size - 1, 1.0, 0.0).astype(F32)
-    return jnp.where(first, before_ref[...].astype(F32) * keep_before, after_ref[...].astype(F32) * keep_after)
+    both = jnp.where(first, before_ref[...].astype(F32) * keep_before, after_ref[...].astype(F32) * keep_after)
+    return both.astype(BF)
 
 
 def shifted_stack(tile, edges, g, shifts):
@@ -125,12 +141,11 @@
     pieces = []
     for by in shifts:
         if by > 0:
-            piece = roll(jnp.where(lane < by, around, tile), -by)
+            pieces.append(roll(jnp.where(lane < by, around, tile), -by))
         elif by < 0:
-            piece = roll(jnp.where(lane >= CH + by, around, tile), -by)
+            pieces.append(roll(jnp.where(lane >= CH + by, around, tile), -by))
         else:
-            piece = tile
-        pieces.append(piece.astype(BF))
+            pieces.append(tile)
     return jnp.concatenate(pieces, axis=0)
 
 
@@ -142,24 +157,24 @@
     return jnp.concatenate([early_ref[start:early], main_ref[0 : size - (early - start)]], axis=0)
 
 
-def inner_kernel(halo_ref, strain_ref, w_ref, u_out, edge_out, scratch):
+def inner_kernel(halo_ref, strain_ref, w_ref, u_out, edge_out):
     size = TB * F
     for b in range(0, TOUT // TB, 2):
         pair = jnp.concatenate([window(halo_ref, strain_ref, b + k, WIN) for k in range(2)], axis=1)
         u = jnp.dot(w_ref[...], pair, preferred_element_type=F32)
         for k in range(2):
-            scratch[size * (b + k) : size * (b + k + 1)] = u[:, CH * k : CH * (k + 1)]
             u_out[size * (b + k) : size * (b + k + 1)] = u[:, CH * k : CH * (k + 1)].astype(BF)
-    edge_out[...] = pack_edges(lambda g: scratch[GROWS * g : GROWS * (g + 1)])
-
-
-def forward_kernel(u_ref, before_ref, after_ref, d_ref, act_out, slope_out, scratch):
+    edge_out[...] = pack_edges(lambda g: u_out[GROWS * g : GROWS * (g + 1)])
+
+
+def forward_kernel(u_ref, before_ref, after_ref, d_ref, slope_out, *refs):
+    chunks, scratch = refs[-2:]
     edges = edges_of(before_ref, after_ref)
     for g in range(0, NG, 2):
         pair = jnp.concatenate(
             [
                 shifted_stack(
-                    u_ref[GROWS * (g + k) : GROWS * (g + k + 1)].astype(F32), edges, g + k, range(-REACH, REACH + 1)
+                    u_ref[GROWS * (g + k) : GROWS * (g + k + 1)], edges, g + k, range(-REACH, REACH + 1)
                 )
                 for k in range(2)
             ],
@@ -173,24 +188,28 @@
             where = slice(GROWS * (g + k), GROWS * (g + k + 1))
             scratch[where] = act[:, CH * k : CH * (k + 1)]
             slope_out[where] = slope[:, CH * k : CH * (k + 1)]
-    n, _, local, _ = act_out.shape
+    n, _, local, _ = chunks.shape
     for f2 in range(F // 2):
         both = jnp.concatenate([scratch[pl.ds(2 * f2 + e, TOUT, stride=F), :] for e in range(2)], axis=0)
         turned = both.T
         for q in range(n):
-            act_out[q, f2] = turned[local * q : local * (q + 1)].astype(BF)
-
-
-def slope_kernel(slope_ref, cot_ref, dz_out, edge_out, scratch):
-    n, _, local, _ = cot_ref.shape
+            chunks[q, f2] = turned[local * q : local * (q + 1)].astype(BF)
+    place(chunks, refs[:-2])
+
+
+def slope_kernel(slope_ref, *refs):
+    dz_out, edge_out, chunks, scratch = refs[-4:]
+    gather(chunks, refs[:-4])
+    local = chunks.shape[2]
     for f2 in range(F // 2):
-        turned = cot_ref[:, f2].astype(F32).reshape(CH, 128).T
+        if local % 16 == 0:
+            turned = chunks[:, f2].reshape(CH, 128).T.astype(F32)
+        else:
+            turned = chunks[:, f2].astype(F32).reshape(CH, 128).T
         for e in range(2):
             scratch[pl.ds(2 * f2 + e, TOUT, stride=F), :] = turned[TOUT * e : TOUT * (e + 1)]
-    dz = (scratch[...] * slope_ref[...]).astype(BF)
-    dz_out[...] = dz
-    scratch[...] = dz.astype(F32)
-    edge_out[...] = pack_edges(lambda g: scratch[GROWS * g : GROWS * (g + 1)])
+    dz_out[...] = (scratch[...] * slope_ref[...]).astype(BF)
+    edge_out[...] = pack_edges(lambda g: dz_out[GROWS * g : GROWS * (g + 1)])
 
 
 def backward_kernel(dz_ref, before_ref, after_ref, dt_ref, u_ref, halo_ref, strain_ref, du_out, grad_out):
@@ -199,7 +218,7 @@
     for g in range(0, NG, 2):
         stacks = [
             shifted_stack(
-                dz_ref[GROWS * (g + k) : GROWS * (g + k + 1)].astype(F32),
+                dz_ref[GROWS * (g + k) : GROWS * (g + k + 1)],
                 edges,
                 g + k,
                 [REACH - m for m in range(KF)],
@@ -264,19 +283,29 @@
         for k in range(2):
             scratch[step * (b + k) : step * (b + k + 1)] = part[:, CH * k : CH * (k + 1)]
     for i in range(F):
-        grad_out[i] = scratch[pl.ds(i, STEPS, stride=F), :].T.astype(BF)
-
-
-def unpack_kernel(act_ref, act_out):
-    n = act_ref.shape[0]
+        grad_out[i] = scratch[pl.ds(i, STEPS, stride=F), :].astype(BF).T
+
+
+def unpack_kernel(*refs):
+    act_out, chunks = refs[-2:]
+    gather(chunks, refs[:-2])
+    n = chunks.shape[0]
     low = lanes((1, 128)) < TOUT
     for f2 in range(F // 2):
         for tile in range(n // 2):
-            a = act_ref[2 * tile, f2].astype(F32)
-            b = act_ref[2 * tile + 1, f2].astype(F32)
+            a = chunks[2 * tile, f2]
+            b = chunks[2 * tile + 1, f2]
             where = slice(128 * tile, 128 * (tile + 1))
-            act_out[2 * f2, :, where] = jnp.where(low, a, roll(b, TOUT)).astype(BF)
-            act_out[2 * f2 + 1, :, where] = jnp.where(low, roll(a, TOUT), b).astype(BF)
+            act_out[2 * f2, :, where] = jnp.where(low, a, roll(b, TOUT))
+            act_out[2 * f2 + 1, :, where] = jnp.where(low, roll(a, TOUT), b)
+
+
+def exchanged(chunks):
+    size = len(chunks)
+    got = [chunks[0]]
+    for hop in range(1, size):
+        got.append(lax.ppermute(chunks[hop], "tm", [(i, i ^ hop) for i in range(size)]))
+    return got
 
 
 def neighbours(array, axis):
@@ -307,17 +336,16 @@
     scale = 1.0 / math.sqrt(size)
     local = cotangent.shape[3]
     x = strain[0]
-    packed = (n, F // 2, local, 128)
-    sent, tail = call(
-        pack_kernel,
-        (out(packed, BF), out((HALO * F, CH), BF)),
-        x,
-        cotangent[0, :, 0],
-        scratch=[pltpu.VMEM((HALO * F, CH), F32)],
-        name="pack",
-    )
-    upstream = lax.all_to_all(sent, "tm", 0, 0, tiled=True)
+    chunk = (F // 2, local, 128)
+    packed = (n,) + chunk
+    flat = (TOUT * F, CH)
+    (tail,) = call(
+        tail_kernel, (out((HALO * F, CH), BF),), x, scratch=[pltpu.VMEM((HALO * F, CH), F32)], name="tail"
+    )
     halo = lax.ppermute(tail, "tm", [(i, i + 1) for i in range(n - 1)])
+    cot, tail = lax.optimization_barrier((cotangent[0, :, 0], tail))
+    sent = call(pack_kernel, (out(chunk, BF),) * n, cot, scratch=[pltpu.VMEM(packed, BF)], name="pack")
+    upstream = exchanged(sent)
 
     wb = jnp.transpose(time_kernel, (0, 2, 1)).reshape(F, TAPS * F)
     vb = time_kernel.reshape(F, F, TAPS // 2, 2)[:, :, ::-1]
@@ -344,34 +372,32 @@
     (turned,) = call(
         turn_kernel, (out((STEPS * F, CH), BF),), x, scratch=[pltpu.VMEM((STEPS * F, CH), F32)], name="turn"
     )
-    flat = (TOUT * F, CH)
     u, u_edge = call(
         inner_kernel,
         (out(flat, BF), out((GROWS, CH), BF)),
         halo,
         turned,
         w,
-        scratch=[pltpu.VMEM(flat, F32)],
         name="inner",
     )
     before, after = neighbours(u_edge, "fiber")
-    act, slope = call(
+    slope, *act = call(
         forward_kernel,
-        (out(packed, BF), out(flat, F32)),
+        (out(flat, F32),) + (out(chunk, BF),) * n,
         u,
         before,
         after,
         d,
-        scratch=[pltpu.VMEM(flat, F32)],
+        scratch=[pltpu.VMEM(packed, BF), pltpu.VMEM(flat, F32)],
         name="forward",
     )
-    act = lax.all_to_all(act, "tm", 0, 0, tiled=True)
+    act = exchanged(act)
     dz, dz_edge = call(
         slope_kernel,
         (out(flat, BF), out((GROWS, CH), BF)),
         slope,
-        upstream,
-        scratch=[pltpu.VMEM(flat, F32)],
+        *upstream,
+        scratch=[pltpu.VMEM(packed, BF), pltpu.VMEM(flat, F32)],
         name="slope",
     )
     before, after = neighbours(dz_edge, "fiber")
@@ -398,7 +424,9 @@
         scratch=[pltpu.VMEM((STEPS * F, CH), F32)],
         name="signal",
     )
-    (activation,) = call(unpack_kernel, (out((F, local, n * TOUT), BF),), act, name="unpack")
+    (activation,) = call(
+        unpack_kernel, (out((F, local, n * TOUT), BF),), *act, scratch=[pltpu.VMEM(packed, BF)], name="unpack"
+    )
     time_grad = jnp.transpose(grads[0:F].reshape(F, TAPS, F), (0, 2, 1))
     fiber_grad = grads[F : F + PER, 0 : KF * F].reshape(PER, KF, F)
     fiber_grad = jnp.transpose(fiber_grad, (2, 0, 1))

time: 89.9 us -> 67 us (0.75)
  the two profiles are of different devices: /device:TPU:12 before, /device:TPU:0 now
where the time goes in v2:
time: 67 us; the launch traced here: 66.7 us
  starting transfers between devices  23.1 us (34%)
  waiting for transfers between devices  17.9 us (27%)
  Pallas kernels  16.1 us (24%)
  local copies, waits for them, and re-layouts  8.39 us (13%)
  between operations  0.91 us (1%)
    pallas_call x10, Pallas kernels, call(): pl.pallas_call(kernel, out_shape=outs, in_specs=[pl.BlockSpec(memory_spac...  16.1 us
    ppermute x6, starting transfers between devices, exchanged(): lax.ppermute(chunks[hop], 'tm', [(i, i ^ hop) for i in range(size)])  8.84 us
    ppermute x4, waiting for transfers between devices, summed(): other = lax.ppermute(mine, axis, [(i, i ^ hop) for i in range(size)])  7.03 us
    ppermute x6, waiting for transfers between devices, exchanged(): lax.ppermute(chunks[hop], 'tm', [(i, i ^ hop) for i in range(size)])  5.99 us
    unnamed x15, local copies, waits for them, and re-layouts  5.4 us
    ppermute x1, starting transfers between devices, on_device(): halo = lax.ppermute(tail, 'tm', [(i, i + 1) for i in range(n - 1)])  4.94 us
    ppermute x2, waiting for transfers between devices, neighbours(): other = lax.ppermute(array, axis, [(0, 1), (1, 0)])  4.85 us
    ppermute x4, starting transfers between devices, summed(): other = lax.ppermute(mine, axis, [(i, i ^ hop) for i in range(size)])  4.77 us
  transfers between devices with their start and end apart: 14, of which 6 were waited for; matrix products, arithmetic and copies ran while one was open for 4% of the time, Pallas kernels for 16%

profile of v2, /device:TPU:0, one launch (start us, length us, event | category | flops | bytes accessed | tf_op | source)
XLA Modules:
  0.0 66.7 jit_solution(923071015869933969)
XLA Ops:
  0.6 1.2 %copy-done = bf16[1,32,128,128]{3,2,1,0:T(8,128)(2,1)S(1)} copy-done((bf16[1,32,128,128]{3,2,1,0:T(8,128)(2,1)S(1)}, bf16[1,32,128,128]{3,2,1,0:T(8,128)(2,1)}, u32[]{:S(2)}) %copy-start) | copy-done | bytes 1048600
  1.9 0.8 %tail.1 = bf16[1024,128]{1,0:T(8,128)(2,1)S(1)} custom-call(bf16[32,128,128]{2,1,0:T(8,128)(2,1)S(1)} %bitcast.18), custom_call_target="tpu_custom_call" | custom-call | tf_op jit(solution)/shard_map/tail/pallas_call | solution.py:34
  2.7 4.9 %collective-permute-start = (bf16[1024,128]{1,0:T(8,128)(2,1)S(1)}, bf16[1024,128]{1,0:T(8,128)(2,1)S(1)}, u32[]{:S(2)}, u32[]{:S(2)}) collective-permute-start(bf16[1024,128]{1,0:T(8,128)(2,1)S(1)} %tail.1), channel_id=1, source_target_pairs={{0,4},{4,8},{8,12},{1,5},{5,9},{9,13},{2,6},{6,10},{10,14},{3,7},{... | collective-permute-start | bytes 786440 | tf_op jit(solution)/shard_map/ppermute | solution.py:345
  7.7 1.0 %copy-done.2 = bf16[1,32,1,32,256]{4,3,2,1,0:T(8,128)(2,1)S(1)} copy-done((bf16[1,32,1,32,256]{4,3,2,1,0:T(8,128)(2,1)S(1)}, bf16[1,32,1,32,256]{4,3,2,1,0:T(8,128)(2,1)}, u32[]{:S(2)}) %copy-start.2) | copy-done | bytes 524312
  8.7 0.3 pack.1
  9.0 1.6 %collective-permute-start.5 = (bf16[16,32,128]{2,1,0:T(8,128)(2,1)S(1)}, bf16[16,32,128]{2,1,0:T(8,128)(2,1)S(1)}, u32[]{:S(2)}, u32[]{:S(2)}) collective-permute-start(bf16[16,32,128]{2,1,0:T(8,128)(2,1)S(1)} %get-tuple-element.35), channel_id=1, source_target_pairs={{0,4},{4,0},{8,12},{12,8},{1,5},{5,1},{9,13},{13,9},{2,6},{6,2},{1... | collective-permute-start | bytes 393224 | tf_op jit(solution)/shard_map/ppermute | solution.py:307
  10.6 1.1 %collective-permute-start.6 = (bf16[16,32,128]{2,1,0:T(8,128)(2,1)S(1)}, bf16[16,32,128]{2,1,0:T(8,128)(2,1)S(1)}, u32[]{:S(2)}, u32[]{:S(2)}) collective-permute-start(bf16[16,32,128]{2,1,0:T(8,128)(2,1)S(1)} %get-tuple-element.36), channel_id=1, source_target_pairs={{0,8},{4,12},{8,0},{12,4},{1,9},{5,13},{9,1},{13,5},{2,10},{6,14},... | collective-permute-start | bytes 393224 | tf_op jit(solution)/shard_map/ppermute | solution.py:307
  11.7 1.7 %collective-permute-start.7 = (bf16[16,32,128]{2,1,0:T(8,128)(2,1)S(1)}, bf16[16,32,128]{2,1,0:T(8,128)(2,1)S(1)}, u32[]{:S(2)}, u32[]{:S(2)}) collective-permute-start(bf16[16,32,128]{2,1,0:T(8,128)(2,1)S(1)} %get-tuple-element.37), channel_id=1, source_target_pairs={{0,12},{4,8},{8,4},{12,0},{1,13},{5,9},{9,5},{13,1},{2,14},{6,10},... | collective-permute-start | bytes 393224 | tf_op jit(solution)/shard_map/ppermute | solution.py:307
  13.4 1.8 %turn.1.strain_ref = bf16[4096,128]{1,0:T(8,128)(2,1)S(1)} custom-call(bf16[32,128,128]{2,1,0:T(8,128)(2,1)S(1)} %bitcast.19), custom_call_target="tpu_custom_call" | custom-call | tf_op jit(solution)/shard_map/turn/pallas_call | solution.py:34
  15.3 0.1 broadcast_compare_fusion
  15.4 0.2 copy.19
  15.6 0.1 tile.27
  15.7 0.2 tile.28.d_ref
  15.9 0.7 %copy-done.3 = bf16[32,32,32]{2,1,0:T(8,128)(2,1)S(1)} copy-done((bf16[32,32,32]{2,1,0:T(8,128)(2,1)S(1)}, bf16[32,32,32]{2,1,0:T(8,128)(2,1)}, u32[]{:S(2)}) %copy-start.3) | copy-done | bytes 65560
  16.7 1.1 %copy.16 = bf16[32,32,32]{1,0,2:T(8,128)(2,1)} copy(bf16[32,32,32]{2,1,0:T(8,128)(2,1)S(1)} %copy-done.3) | data formatting | bytes 131072 | tf_op args[1]
  17.8 0.2 copy.15
  18.0 0.3 reshape.88.wb_ref
  18.2 0.7 copy-done.4
  18.9 0.3 copy.17
  19.2 0.2 reshape.90.vb_ref
  19.4 0.1 tile.29
  19.5 0.2 tile.30.dt_ref
  19.7 0.3 weights.1
  20.0 1.1 %inner.1 = (bf16[2048,128]{1,0:T(8,128)(2,1)S(1)}, bf16[128,128]{1,0:T(8,128)(2,1)S(1)}) custom-call(bf16[1024,128]{1,0:T(8,128)(2,1)S(1)} %collective-permute-done.halo_ref, bf16[4096,128]{1,0:T(8,128)(2,1)S(1)} %turn.1.strain_ref, bf16[256,1536]{1,0:T(8,128)(2,1)S(1)} %get-tuple-element.24.w_ref), custom_call_target="tpu_custom_call" | custom-call | tf_op jit(solution)/shard_map/inner/pallas_call | solution.py:34
  21.1 1.6 %collective-permute-start.1 = (bf16[128,128]{1,0:T(8,128)(2,1)S(1)}, bf16[128,128]{1,0:T(8,128)(2,1)S(1)}, u32[]{:S(2)}, u32[]{:S(2)}) collective-permute-start(bf16[128,128]{1,0:T(8,128)(2,1)S(1)} %get-tuple-element.26), channel_id=1, source_target_pairs={{0,2},{2,0},{1,3},{3,1},{4,6},{6,4},{5,7},{7,5},{8,10},{10,8},{9,1... | collective-permute-start | bytes 98312 | tf_op jit(solution)/shard_map/ppermute | solution.py:314
  22.7 2.4 %collective-permute-done.1.before_ref.after_ref = bf16[128,128]{1,0:T(8,128)(2,1)S(1)} collective-permute-done((bf16[128,128]{1,0:T(8,128)(2,1)S(1)}, bf16[128,128]{1,0:T(8,128)(2,1)S(1)}, u32[]{:S(2)}, u32[]{:S(2)}) %collective-permute-start.1) | collective-permute-done | bytes 32800 | tf_op jit(solution)/shard_map/ppermute | solution.py:314
  25.1 2.9 %forward.1 = (f32[2048,128]{1,0:T(8,128)S(1)}, bf16[16,32,128]{2,1,0:T(8,128)(2,1)S(1)}, bf16[16,32,128]{2,1,0:T(8,128)(2,1)S(1)}, bf16[16,32,128]{2,1,0:T(8,128)(2,1)S(1)}, bf16[16,32,128]{2,1,0:T(8,128)(2,1)S(1)}) custom-call(bf16[2048,128]{1,0:T(8,128)(2,1)S(1)} %get-tuple-element.25.u_ref, ...), custom_call_target="tpu_custom_call" | custom-call | tf_op jit(solution)/shard_map/forward/pallas_call | solution.py:34
  28.1 1.2 %slope.1 = (bf16[2048,128]{1,0:T(8,128)(2,1)S(1)}, bf16[128,128]{1,0:T(8,128)(2,1)S(1)}) custom-call(f32[2048,128]{1,0:T(8,128)S(1)} %get-tuple-element.32.slope_ref, bf16[16,32,128]{2,1,0:T(8,128)(2,1)S(1)} %get-tuple-element.34.refs_0_, bf16[16,32,128]{2,1,0:T(8,128)(2,1)S(1)} %collective-permute-done.5.refs_1_, ...), custom_call_target="tpu_custom_call" | custom-call | tf_op jit(solution)/shard_map/slope/pallas_call | solution.py:34
  29.3 1.6 %collective-permute-start.8 = (bf16[128,128]{1,0:T(8,128)(2,1)S(1)}, bf16[128,128]{1,0:T(8,128)(2,1)S(1)}, u32[]{:S(2)}, u32[]{:S(2)}) collective-permute-start(bf16[128,128]{1,0:T(8,128)(2,1)S(1)} %get-tuple-element.39), channel_id=1, source_target_pairs={{0,2},{2,0},{1,3},{3,1},{4,6},{6,4},{5,7},{7,5},{8,10},{10,8},{9,1... | collective-permute-start | bytes 98312 | tf_op jit(solution)/shard_map/ppermute | solution.py:314
  30.9 2.4 %collective-permute-done.8.before_ref.after_ref = bf16[128,128]{1,0:T(8,128)(2,1)S(1)} collective-permute-done((bf16[128,128]{1,0:T(8,128)(2,1)S(1)}, bf16[128,128]{1,0:T(8,128)(2,1)S(1)}, u32[]{:S(2)}, u32[]{:S(2)}) %collective-permute-start.8) | collective-permute-done | bytes 32800 | tf_op jit(solution)/shard_map/ppermute | solution.py:314
  33.3 3.5 %backward.1 = (bf16[2048,128]{1,0:T(8,128)(2,1)S(1)}, f32[40,1024]{1,0:T(8,128)S(1)}) custom-call(bf16[2048,128]{1,0:T(8,128)(2,1)S(1)} %get-tuple-element.38.dz_ref, bf16[128,128]{1,0:T(8,128)(2,1)S(1)} %collective-permute-done.8.before_ref.after_ref, bf16[128,128]{1,0:T(8,128)(2,1)S(1)} %collective-permute-done.8.before_ref.after_ref, ...), custom_call_target="tpu_custom_call" | custom-call | tf_op jit(solution)/shard_map/backward/pallas_call | solution.py:34
  36.9 1.3 %collective-permute-done.10 = bf16[40,1024]{1,0:T(8,128)(2,1)S(1)} collective-permute-done((bf16[40,1024]{1,0:T(8,128)(2,1)S(1)}, bf16[40,1024]{1,0:T(8,128)(2,1)S(1)}, u32[]{:S(2)}, u32[]{:S(2)}) %collective-permute-start.10) | collective-permute-done | bytes 81952 | tf_op jit(solution)/shard_map/ppermute | solution.py:327
  38.2 1.5 %collective-permute-start.11 = (bf16[40,1024]{1,0:T(8,128)(2,1)S(1)}, bf16[40,1024]{1,0:T(8,128)(2,1)S(1)}, u32[]{:S(2)}, u32[]{:S(2)}) collective-permute-start(bf16[40,1024]{1,0:T(8,128)(2,1)S(1)} %add_convert_fusion.2), channel_id=1, source_target_pairs={{0,2},{2,0},{1,3},{3,1},{4,6},{6,4},{5,7},{7,5},{8,10},{10,8},{9,1... | collective-permute-start | bytes 245768 | tf_op jit(solution)/shard_map/ppermute | solution.py:327
  39.7 3.0 %collective-permute-done.11 = bf16[40,1024]{1,0:T(8,128)(2,1)S(1)} collective-permute-done((bf16[40,1024]{1,0:T(8,128)(2,1)S(1)}, bf16[40,1024]{1,0:T(8,128)(2,1)S(1)}, u32[]{:S(2)}, u32[]{:S(2)}) %collective-permute-start.11) | collective-permute-done | bytes 81952 | tf_op jit(solution)/shard_map/ppermute | solution.py:327
  42.8 0.7 %collective-permute-start.12 = (bf16[40,1024]{1,0:T(8,128)(2,1)S(1)}, bf16[40,1024]{1,0:T(8,128)(2,1)S(1)}, u32[]{:S(2)}, u32[]{:S(2)}) collective-permute-start(bf16[40,1024]{1,0:T(8,128)(2,1)S(1)} %add_convert_fusion.1), channel_id=1, source_target_pairs={{0,4},{4,0},{8,12},{12,8},{1,5},{5,1},{9,13},{13,9},{2,6},{6,2},{1... | collective-permute-start | bytes 245768 | tf_op jit(solution)/shard_map/ppermute | solution.py:327
  43.5 1.4 %collective-permute-start.2 = (bf16[16,32,128]{2,1,0:T(8,128)(2,1)S(1)}, bf16[16,32,128]{2,1,0:T(8,128)(2,1)S(1)}, u32[]{:S(2)}, u32[]{:S(2)}) collective-permute-start(bf16[16,32,128]{2,1,0:T(8,128)(2,1)S(1)} %get-tuple-element.29), channel_id=1, source_target_pairs={{0,4},{4,0},{8,12},{12,8},{1,5},{5,1},{9,13},{13,9},{2,6},{6,2},{1... | collective-permute-start | bytes 393224 | tf_op jit(solution)/shard_map/ppermute | solution.py:307
  44.8 1.7 %collective-permute-start.3 = (bf16[16,32,128]{2,1,0:T(8,128)(2,1)S(1)}, bf16[16,32,128]{2,1,0:T(8,128)(2,1)S(1)}, u32[]{:S(2)}, u32[]{:S(2)}) collective-permute-start(bf16[16,32,128]{2,1,0:T(8,128)(2,1)S(1)} %get-tuple-element.30), channel_id=1, source_target_pairs={{0,8},{4,12},{8,0},{12,4},{1,9},{5,13},{9,1},{13,5},{2,10},{6,14},... | collective-permute-start | bytes 393224 | tf_op jit(solution)/shard_map/ppermute | solution.py:307
  46.5 1.3 %collective-permute-start.4 = (bf16[16,32,128]{2,1,0:T(8,128)(2,1)S(1)}, bf16[16,32,128]{2,1,0:T(8,128)(2,1)S(1)}, u32[]{:S(2)}, u32[]{:S(2)}) collective-permute-start(bf16[16,32,128]{2,1,0:T(8,128)(2,1)S(1)} %get-tuple-element.31), channel_id=1, source_target_pairs={{0,12},{4,8},{8,4},{12,0},{1,13},{5,9},{9,5},{13,1},{2,14},{6,10},... | collective-permute-start | bytes 393224 | tf_op jit(solution)/shard_map/ppermute | solution.py:307
  47.9 1.5 %collective-permute-start.9 = (bf16[512,128]{1,0:T(8,128)(2,1)S(1)}, bf16[512,128]{1,0:T(8,128)(2,1)S(1)}, u32[]{:S(2)}, u32[]{:S(2)}) collective-permute-start(bf16[512,128]{1,0:T(8,128)(2,1)S(1)} %slice.9), channel_id=1, source_target_pairs={{4,0},{8,4},{12,8},{5,1},{9,5},{13,9},{6,2},{10,6},{14,10},{7,3},{... | collective-permute-start | bytes 393224 | tf_op jit(solution)/shard_map/ppermute | solution.py:416
  49.4 2.4 %collective-permute-start.13 = (bf16[40,1024]{1,0:T(8,128)(2,1)S(1)}, bf16[40,1024]{1,0:T(8,128)(2,1)S(1)}, u32[]{:S(2)}, u32[]{:S(2)}) collective-permute-start(bf16[40,1024]{1,0:T(8,128)(2,1)S(1)} %add_convert_fusion), channel_id=1, source_target_pairs={{0,8},{4,12},{8,0},{12,4},{1,9},{5,13},{9,1},{13,5},{2,10},{6,14},... | collective-permute-start | bytes 245768 | tf_op jit(solution)/shard_map/ppermute | solution.py:327
  51.8 6.0 %collective-permute-done.3.refs_2_ = bf16[16,32,128]{2,1,0:T(8,128)(2,1)S(1)} collective-permute-done((bf16[16,32,128]{2,1,0:T(8,128)(2,1)S(1)}, bf16[16,32,128]{2,1,0:T(8,128)(2,1)S(1)}, u32[]{:S(2)}, u32[]{:S(2)}) %collective-permute-start.3) | collective-permute-done | bytes 131104 | tf_op jit(solution)/shard_map/ppermute | solution.py:307
  57.8 1.0 %unpack.1 = bf16[32,32,256]{2,1,0:T(8,128)(2,1)} custom-call(bf16[16,32,128]{2,1,0:T(8,128)(2,1)S(1)} %get-tuple-element.28.refs_0_, bf16[16,32,128]{2,1,0:T(8,128)(2,1)S(1)} %collective-permute-done.2.refs_1_, bf16[16,32,128]{2,1,0:T(8,128)(2,1)S(1)} %collective-permute-done.3.refs_2_, bf16[16,32,128]{2,1,0:T(8,128)(2,1)S(1)} %collective-permute-done.4.refs_3_), custom_call_target="tpu_custom_call" | custom-call | tf_op jit(solution)/shard_map/unpack/pallas_call | solution.py:34
  58.9 3.1 %signal.1 = bf16[32,128,128]{2,1,0:T(8,128)(2,1)} custom-call(bf16[2048,128]{1,0:T(8,128)(2,1)S(1)} %get-tuple-element.41.du_ref, bf16[512,128]{1,0:T(8,128)(2,1)S(1)} %collective-permute-done.9.late_ref, bf16[512,768]{1,0:T(8,128)(2,1)S(1)} %get-tuple-element.42.v_ref), custom_call_target="tpu_custom_call" | custom-call | tf_op jit(solution)/shard_map/signal/pallas_call | solution.py:34
  62.0 2.7 %collective-permute-done.13 = bf16[40,1024]{1,0:T(8,128)(2,1)S(1)} collective-permute-done((bf16[40,1024]{1,0:T(8,128)(2,1)S(1)}, bf16[40,1024]{1,0:T(8,128)(2,1)S(1)}, u32[]{:S(2)}, u32[]{:S(2)}) %collective-permute-start.13) | collective-permute-done | bytes 81952 | tf_op jit(solution)/shard_map/ppermute | solution.py:327
  64.8 0.1 reshape.92
  64.9 0.6 copy.22
  65.5 0.2 reshape.91
  65.7 1.0 %copy.20 = f32[32,32,32]{1,2,0:T(8,128)} copy(f32[32,32,32]{2,1,0:T(8,128)S(1)} %reshape.91) | data formatting | bytes 262144 | tf_op jit(solution)/shard_map/reshape | solution.py:430
  (29 shorter events, 0.3 us)
Async XLA Ops:
  0.6 1.2 %copy-start = (bf16[1,32,128,128]{3,2,1,0:T(8,128)(2,1)S(1)}, bf16[1,32,128,128]{3,2,1,0:T(8,128)(2,1)}, u32[]{:S(2)}) copy-start(bf16[1,32,128,128]{3,2,1,0:T(8,128)(2,1)} %param.4) | copy-start | bytes 3145732
  1.9 11.6 %copy-start.1 = (bf16[1,32,128,128]{3,2,1,0:T(8,128)(2,1)S(1)}, bf16[1,32,128,128]{3,2,1,0:T(8,128)(2,1)}, u32[]{:S(2)}) copy-start(bf16[1,32,128,128]{3,2,1,0:T(8,128)(2,1)} %param.4) | copy-start | bytes 3145732
  2.7 17.3 %collective-permute-start = (bf16[1024,128]{1,0:T(8,128)(2,1)S(1)}, bf16[1024,128]{1,0:T(8,128)(2,1)S(1)}, u32[]{:S(2)}, u32[]{:S(2)}) collective-permute-start(bf16[1024,128]{1,0:T(8,128)(2,1)S(1)} %tail.1), channel_id=1, source_target_pairs={{0,4},{4,8},{8,12},{1,5},{5,9},{9,13},{2,6},{6,10},{10,14},{3,7},{... | collective-permute-start | bytes 786440 | tf_op jit(solution)/shard_map/ppermute | solution.py:345
  7.6 1.0 %copy-start.2 = (bf16[1,32,1,32,256]{4,3,2,1,0:T(8,128)(2,1)S(1)}, bf16[1,32,1,32,256]{4,3,2,1,0:T(8,128)(2,1)}, u32[]{:S(2)}) copy-start(bf16[1,32,1,32,256]{4,3,2,1,0:T(8,128)(2,1)} %param.7) | copy-start | bytes 1572868
  9.0 19.1 %collective-permute-start.5 = (bf16[16,32,128]{2,1,0:T(8,128)(2,1)S(1)}, bf16[16,32,128]{2,1,0:T(8,128)(2,1)S(1)}, u32[]{:S(2)}, u32[]{:S(2)}) collective-permute-start(bf16[16,32,128]{2,1,0:T(8,128)(2,1)S(1)} %get-tuple-element.35), channel_id=1, source_target_pairs={{0,4},{4,0},{8,12},{12,8},{1,5},{5,1},{9,13},{13,9},{2,6},{6,2},{1... | collective-permute-start | bytes 393224 | tf_op jit(solution)/shard_map/ppermute | solution.py:307
  10.6 17.4 %collective-permute-start.6 = (bf16[16,32,128]{2,1,0:T(8,128)(2,1)S(1)}, bf16[16,32,128]{2,1,0:T(8,128)(2,1)S(1)}, u32[]{:S(2)}, u32[]{:S(2)}) collective-permute-start(bf16[16,32,128]{2,1,0:T(8,128)(2,1)S(1)} %get-tuple-element.36), channel_id=1, source_target_pairs={{0,8},{4,12},{8,0},{12,4},{1,9},{5,13},{9,1},{13,5},{2,10},{6,14},... | collective-permute-start | bytes 393224 | tf_op jit(solution)/shard_map/ppermute | solution.py:307
  11.7 16.3 %collective-permute-start.7 = (bf16[16,32,128]{2,1,0:T(8,128)(2,1)S(1)}, bf16[16,32,128]{2,1,0:T(8,128)(2,1)S(1)}, u32[]{:S(2)}, u32[]{:S(2)}) collective-permute-start(bf16[16,32,128]{2,1,0:T(8,128)(2,1)S(1)} %get-tuple-element.37), channel_id=1, source_target_pairs={{0,12},{4,8},{8,4},{12,0},{1,13},{5,9},{9,5},{13,1},{2,14},{6,10},... | collective-permute-start | bytes 393224 | tf_op jit(solution)/shard_map/ppermute | solution.py:307
  13.4 1.8 %copy-start.5 = (bf16[32,4,9]{0,1,2:T(4,128)(2,1)S(1)}, bf16[32,4,9]{0,1,2:T(4,128)(2,1)}, u32[]{:S(2)}) copy-start(bf16[32,4,9]{0,1,2:T(4,128)(2,1)} %param.6) | copy-start | bytes 6916
  15.7 1.0 %copy-start.3 = (bf16[32,32,32]{2,1,0:T(8,128)(2,1)S(1)}, bf16[32,32,32]{2,1,0:T(8,128)(2,1)}, u32[]{:S(2)}) copy-start(bf16[32,32,32]{2,1,0:T(8,128)(2,1)} %param.5) | copy-start | bytes 196612
  17.9 1.0 %copy-start.4 = (bf16[32,32,32]{1,0,2:T(8,128)(2,1)S(1)}, bf16[32,32,32]{1,0,2:T(8,128)(2,1)}, u32[]{:S(2)}) copy-start(bf16[32,32,32]{1,0,2:T(8,128)(2,1)} %copy.16) | copy-start | bytes 196612
  21.1 4.0 %collective-permute-start.1 = (bf16[128,128]{1,0:T(8,128)(2,1)S(1)}, bf16[128,128]{1,0:T(8,128)(2,1)S(1)}, u32[]{:S(2)}, u32[]{:S(2)}) collective-permute-start(bf16[128,128]{1,0:T(8,128)(2,1)S(1)} %get-tuple-element.26), channel_id=1, source_target_pairs={{0,2},{2,0},{1,3},{3,1},{4,6},{6,4},{5,7},{7,5},{8,10},{10,8},{9,1... | collective-permute-start | bytes 98312 | tf_op jit(solution)/shard_map/ppermute | solution.py:314
  29.3 4.0 %collective-permute-start.8 = (bf16[128,128]{1,0:T(8,128)(2,1)S(1)}, bf16[128,128]{1,0:T(8,128)(2,1)S(1)}, u32[]{:S(2)}, u32[]{:S(2)}) collective-permute-start(bf16[128,128]{1,0:T(8,128)(2,1)S(1)} %get-tuple-element.39), channel_id=1, source_target_pairs={{0,2},{2,0},{1,3},{3,1},{4,6},{6,4},{5,7},{7,5},{8,10},{10,8},{9,1... | collective-permute-start | bytes 98312 | tf_op jit(solution)/shard_map/ppermute | solution.py:314
  36.8 1.3 %collective-permute-start.10 = (bf16[40,1024]{1,0:T(8,128)(2,1)S(1)}, bf16[40,1024]{1,0:T(8,128)(2,1)S(1)}, u32[]{:S(2)}, u32[]{:S(2)}) collective-permute-start(bf16[40,1024]{1,0:T(8,128)(2,1)S(1)} %convert_element_type.36), channel_id=1, source_target_pairs={{0,1},{1,0},{2,3},{3,2},{4,5},{5,4},{6,7},{7,6},{8,9},{9,8},{10,11... | collective-permute-start | bytes 245768 | tf_op jit(solution)/shard_map/ppermute | solution.py:327
  38.2 4.6 %collective-permute-start.11 = (bf16[40,1024]{1,0:T(8,128)(2,1)S(1)}, bf16[40,1024]{1,0:T(8,128)(2,1)S(1)}, u32[]{:S(2)}, u32[]{:S(2)}) collective-permute-start(bf16[40,1024]{1,0:T(8,128)(2,1)S(1)} %add_convert_fusion.2), channel_id=1, source_target_pairs={{0,2},{2,0},{1,3},{3,1},{4,6},{6,4},{5,7},{7,5},{8,10},{10,8},{9,1... | collective-permute-start | bytes 245768 | tf_op jit(solution)/shard_map/ppermute | solution.py:327
  42.8 6.6 %collective-permute-start.12 = (bf16[40,1024]{1,0:T(8,128)(2,1)S(1)}, bf16[40,1024]{1,0:T(8,128)(2,1)S(1)}, u32[]{:S(2)}, u32[]{:S(2)}) collective-permute-start(bf16[40,1024]{1,0:T(8,128)(2,1)S(1)} %add_convert_fusion.1), channel_id=1, source_target_pairs={{0,4},{4,0},{8,12},{12,8},{1,5},{5,1},{9,13},{13,9},{2,6},{6,2},{1... | collective-permute-start | bytes 245768 | tf_op jit(solution)/shard_map/ppermute | solution.py:327
  43.5 8.4 %collective-permute-start.2 = (bf16[16,32,128]{2,1,0:T(8,128)(2,1)S(1)}, bf16[16,32,128]{2,1,0:T(8,128)(2,1)S(1)}, u32[]{:S(2)}, u32[]{:S(2)}) collective-permute-start(bf16[16,32,128]{2,1,0:T(8,128)(2,1)S(1)} %get-tuple-element.29), channel_id=1, source_target_pairs={{0,4},{4,0},{8,12},{12,8},{1,5},{5,1},{9,13},{13,9},{2,6},{6,2},{1... | collective-permute-start | bytes 393224 | tf_op jit(solution)/shard_map/ppermute | solution.py:307
  44.8 13.0 %collective-permute-start.3 = (bf16[16,32,128]{2,1,0:T(8,128)(2,1)S(1)}, bf16[16,32,128]{2,1,0:T(8,128)(2,1)S(1)}, u32[]{:S(2)}, u32[]{:S(2)}) collective-permute-start(bf16[16,32,128]{2,1,0:T(8,128)(2,1)S(1)} %get-tuple-element.30), channel_id=1, source_target_pairs={{0,8},{4,12},{8,0},{12,4},{1,9},{5,13},{9,1},{13,5},{2,10},{6,14},... | collective-permute-start | bytes 393224 | tf_op jit(solution)/shard_map/ppermute | solution.py:307
  46.5 11.3 %collective-permute-start.4 = (bf16[16,32,128]{2,1,0:T(8,128)(2,1)S(1)}, bf16[16,32,128]{2,1,0:T(8,128)(2,1)S(1)}, u32[]{:S(2)}, u32[]{:S(2)}) collective-permute-start(bf16[16,32,128]{2,1,0:T(8,128)(2,1)S(1)} %get-tuple-element.31), channel_id=1, source_target_pairs={{0,12},{4,8},{8,4},{12,0},{1,13},{5,9},{9,5},{13,1},{2,14},{6,10},... | collective-permute-start | bytes 393224 | tf_op jit(solution)/shard_map/ppermute | solution.py:307
  47.9 11.0 %collective-permute-start.9 = (bf16[512,128]{1,0:T(8,128)(2,1)S(1)}, bf16[512,128]{1,0:T(8,128)(2,1)S(1)}, u32[]{:S(2)}, u32[]{:S(2)}) collective-permute-start(bf16[512,128]{1,0:T(8,128)(2,1)S(1)} %slice.9), channel_id=1, source_target_pairs={{4,0},{8,4},{12,8},{5,1},{9,5},{13,9},{6,2},{10,6},{14,10},{7,3},{... | collective-permute-start | bytes 393224 | tf_op jit(solution)/shard_map/ppermute | solution.py:416
  49.4 15.3 %collective-permute-start.13 = (bf16[40,1024]{1,0:T(8,128)(2,1)S(1)}, bf16[40,1024]{1,0:T(8,128)(2,1)S(1)}, u32[]{:S(2)}, u32[]{:S(2)}) collective-permute-start(bf16[40,1024]{1,0:T(8,128)(2,1)S(1)} %add_convert_fusion), channel_id=1, source_target_pairs={{0,8},{4,12},{8,0},{12,4},{1,9},{5,13},{9,1},{13,5},{2,10},{6,14},... | collective-permute-start | bytes 245768 | tf_op jit(solution)/shard_map/ppermute | solution.py:327

commit v3 on v2

--- a/solution.py
+++ b/solution.py
@@ -30,12 +30,13 @@
 VMEM_LIMIT = 16 * 1024 * 1024
 
 
-def call(kernel, outs, *args, scratch=(), name=None):
+def call(kernel, outs, *args, scratch=(), name=None, far=(), far_outs=()):
+    where = lambda k, away: pl.BlockSpec(memory_space=pltpu.HBM if k in away else pltpu.VMEM)
     return pl.pallas_call(
         kernel,
         out_shape=outs,
-        in_specs=[pl.BlockSpec(memory_space=pltpu.VMEM)] * len(args),
-        out_specs=jax.tree.map(lambda o: pl.BlockSpec(memory_space=pltpu.VMEM), outs),
+        in_specs=[where(k, far) for k in range(len(args))],
+        out_specs=tuple(where(k, far_outs) for k in range(len(outs))),
         scratch_shapes=list(scratch),
         compiler_params=pltpu.CompilerParams(vmem_limit_bytes=VMEM_LIMIT),
         name=name,
@@ -102,20 +103,39 @@
     out_ref[...] = scratch[...].astype(BF)
 
 
-def weight_kernel(wb_ref, vb_ref, d_ref, dt_ref, w_out, v_out, d_out, dt_out):
-    base = wb_ref[...].astype(F32)
-    base = jnp.concatenate([base, jnp.zeros((F, WIN - base.shape[1]), F32)], axis=1)
+def weight_kernel(time_ref, fiber_ref, w_out, v_out, d_out, dt_out, scratch):
+    for o4 in range(F // 4):
+        turned = time_ref[4 * o4 : 4 * (o4 + 1)].astype(F32).reshape(4 * F, TAPS)
+        turned = jnp.concatenate([turned, jnp.zeros((4 * F, 128 - TAPS), F32)], axis=1).T[0:TAPS]
+        for e in range(4):
+            scratch[pl.ds(4 * o4 + e, TAPS, stride=F), :] = roll(turned, -F * e)
+    group = lanes((1, 128)) // F
+    tiles = []
+    for k4 in range(TAPS // 4):
+        tile = scratch[F * 4 * k4 : F * (4 * k4 + 1)]
+        for e in range(1, 4):
+            tile = jnp.where(group == e, roll(scratch[F * (4 * k4 + e) : F * (4 * k4 + e + 1)], F * e), tile)
+        tiles.append(tile)
+    tiles.append(jnp.zeros((F, WIN - TAPS * F), F32))
+    base = jnp.concatenate(tiles, axis=1)
     for t in range(TB):
         w_out[F * t : F * (t + 1)] = roll(base, 2 * F * (t + 1)).astype(BF)
-    for p in range(2):
-        part = vb_ref[F * p : F * (p + 1)].astype(F32)
-        part = jnp.concatenate([part, jnp.zeros((F, VWIN - part.shape[1]), F32)], axis=1)
-        for h in range(TB):
-            v_out[F * (2 * h + p) : F * (2 * h + p + 1)] = roll(part, F * h).astype(BF)
-    step = (lanes((1, KF * GROWS)) % GROWS) // F
-    for t in range(TG):
-        d_out[F * t : F * (t + 1)] = jnp.where(step == t, d_ref[...].astype(F32), 0.0).astype(BF)
-        dt_out[F * t : F * (t + 1)] = jnp.where(step == t, dt_ref[...].astype(F32), 0.0).astype(BF)
+    size, step = TB * F, 2 * TB * F
+    for a in range(3):
+        v_out[:, size * a : size * (a + 1)] = w_out[:, step * (2 - a) : step * (3 - a)].T
+    taps = fiber_ref[...]
+    spread = (lax.broadcasted_iota(jnp.int32, (F, GROWS), 1) % F == lax.broadcasted_iota(jnp.int32, (F, GROWS), 0)).astype(BF)
+    wide = jnp.dot(taps, spread, preferred_element_type=F32).astype(BF)
+    row = lax.broadcasted_iota(jnp.int32, (GROWS, GROWS), 0)
+    col = lax.broadcasted_iota(jnp.int32, (GROWS, GROWS), 1)
+    together = (row // PER) == (col // PER)
+    which = lax.broadcasted_iota(jnp.int32, (GROWS, KF * PER), 1)
+    feat = lax.broadcasted_iota(jnp.int32, (GROWS, KF * PER), 0) % PER
+    for m in range(KF):
+        pick = (which == PER * m + feat).astype(BF)
+        block = jnp.where(together, jnp.dot(pick, wide, preferred_element_type=F32), 0.0)
+        dt_out[:, GROWS * m : GROWS * (m + 1)] = block.astype(BF)
+        d_out[:, GROWS * m : GROWS * (m + 1)] = block.T.astype(BF)
 
 
 def pack_edges(read):
@@ -191,9 +211,9 @@
     n, _, local, _ = chunks.shape
     for f2 in range(F // 2):
         both = jnp.concatenate([scratch[pl.ds(2 * f2 + e, TOUT, stride=F), :] for e in range(2)], axis=0)
-        turned = both.T
+        turned = both.astype(BF).T
         for q in range(n):
-            chunks[q, f2] = turned[local * q : local * (q + 1)].astype(BF)
+            chunks[q, f2] = turned[local * q : local * (q + 1)]
     place(chunks, refs[:-2])
 
 
@@ -266,7 +286,7 @@
     grad_out[F : F + 8] = jnp.concatenate(tiles, axis=1)
 
 
-def signal_kernel(du_ref, late_ref, v_ref, grad_out, scratch):
+def signal_kernel(du_ref, late_ref, v_ref, grad_out, scratch, ready, sems):
     size = TB * F
     last = TOUT * F
 
@@ -282,8 +302,16 @@
         part = jnp.dot(v_ref[...], pair, preferred_element_type=F32)
         for k in range(2):
             scratch[step * (b + k) : step * (b + k + 1)] = part[:, CH * k : CH * (k + 1)]
-    for i in range(F):
-        grad_out[i] = scratch[pl.ds(i, STEPS, stride=F), :].astype(BF).T
+    each = F // 4
+    copies = []
+    for k in range(4):
+        for i in range(each * k, each * (k + 1)):
+            ready[i] = scratch[pl.ds(i, STEPS, stride=F), :].astype(BF).T
+        part = pl.ds(each * k, each)
+        copies.append(pltpu.make_async_copy(ready.at[part], grad_out.at[part], sems.at[k]))
+        copies[-1].start()
+    for copy in copies:
+        copy.wait()
 
 
 def unpack_kernel(*refs):
@@ -300,6 +328,20 @@
             act_out[2 * f2 + 1, :, where] = jnp.where(low, roll(a, TOUT), b)
 
 
+def finish_kernel(scale, mine_ref, other_ref, time_out, fiber_out, scratch):
+    total = (mine_ref[...].astype(F32) + other_ref[...].astype(F32)) * scale
+    for k in range(TAPS):
+        tile = total[0:F, 128 * (k // 4) : 128 * (k // 4 + 1)]
+        scratch[pl.ds(k, F, stride=TAPS), :] = roll(tile, -F * (k % 4))
+    for o4 in range(F // 4):
+        turned = scratch[4 * TAPS * o4 : 4 * TAPS * (o4 + 1)].T[0:F]
+        for e in range(4):
+            time_out[4 * o4 + e] = roll(turned, -TAPS * e)[:, 0:TAPS]
+    for m in range(KF):
+        tile = total[F : F + 8, 128 * (m // 4) : 128 * (m // 4 + 1)]
+        fiber_out[m] = roll(tile, -F * (m % 4))[0:PER, 0:F]
+
+
 def exchanged(chunks):
     size = len(chunks)
     got = [chunks[0]]
@@ -318,16 +360,9 @@
     return before, after
 
 
-def summed(array, axes):
-    for axis in axes:
-        size = lax.axis_size(axis)
-        hop = 1
-        while hop < size:
-            mine = array.astype(BF)
-            other = lax.ppermute(mine, axis, [(i, i ^ hop) for i in range(size)])
-            array = mine.astype(F32) + other.astype(F32)
-            hop *= 2
-    return array
+def paired(array, axis, hop):
+    mine = array.astype(BF)
+    return mine, lax.ppermute(mine, axis, [(i, i ^ hop) for i in range(lax.axis_size(axis))])
 
 
 def on_device(strain, time_kernel, fiber_kernel, cotangent):
@@ -347,14 +382,6 @@
     sent = call(pack_kernel, (out(chunk, BF),) * n, cot, scratch=[pltpu.VMEM(packed, BF)], name="pack")
     upstream = exchanged(sent)
 
-    wb = jnp.transpose(time_kernel, (0, 2, 1)).reshape(F, TAPS * F)
-    vb = time_kernel.reshape(F, F, TAPS // 2, 2)[:, :, ::-1]
-    vb = jnp.transpose(vb, (3, 1, 2, 0)).reshape(2 * F, TAPS // 2 * F)
-    ids = jnp.arange(F, dtype=jnp.int32) // PER
-    same = ids[:, None] == ids[None, :]
-    dense = jnp.where(same[:, :, None], jnp.tile(fiber_kernel, (1, F // PER, 1)), jnp.zeros((), BF))
-    d0 = jnp.tile(jnp.transpose(dense, (0, 2, 1)), (1, 1, TG)).reshape(F, KF * GROWS)
-    dt0 = jnp.tile(jnp.transpose(dense, (1, 2, 0)), (1, 1, TG)).reshape(F, KF * GROWS)
     w, v, d, dt = call(
         weight_kernel,
         (
@@ -363,10 +390,9 @@
             out((GROWS, KF * GROWS), BF),
             out((GROWS, KF * GROWS), BF),
         ),
-        wb,
-        vb,
-        d0,
-        dt0,
+        time_kernel,
+        jnp.transpose(fiber_kernel, (2, 1, 0)).reshape(KF * PER, F),
+        scratch=[pltpu.VMEM((TAPS * F, 128), F32)],
         name="weights",
     )
     (turned,) = call(
@@ -413,24 +439,43 @@
         turned,
         name="backward",
     )
-    late = lax.ppermute(du[0 : LATE * F], "tm", [(i + 1, i) for i in range(n - 1)])
-    grads = summed(grads, ("rep", "fiber", "tm")) * scale
+    hops = [(axis, 1 << k) for axis in ("rep", "fiber", "tm") for k in range((lax.axis_size(axis) - 1).bit_length())]
+    head = du[0 : LATE * F]
+    for step, (axis, hop) in enumerate(hops):
+        if step == 0:
+            grads, *act = lax.optimization_barrier((grads, *act))
+            (activation,) = call(
+                unpack_kernel, (out((F, local, n * TOUT), BF),), *act, scratch=[pltpu.VMEM(packed, BF)], name="unpack"
+            )
+        if step == 2:
+            grads, head, activation = lax.optimization_barrier((grads, head, activation))
+        mine, other = paired(grads, axis, hop)
+        if step < len(hops) - 1:
+            grads = mine.astype(F32) + other.astype(F32)
+    late = lax.ppermute(head, "tm", [(i + 1, i) for i in range(n - 1)])
     (strain_grad,) = call(
         signal_kernel,
         (out((F, CH, STEPS), BF),),
         du,
         late,
         v,
-        scratch=[pltpu.VMEM((STEPS * F, CH), F32)],
+        scratch=[
+            pltpu.VMEM((STEPS * F, CH), F32),
+            pltpu.VMEM((F, CH, STEPS), BF),
+            pltpu.SemaphoreType.DMA((4,)),
+        ],
         name="signal",
-    )
-    (activation,) = call(
-        unpack_kernel, (out((F, local, n * TOUT), BF),), *act, scratch=[pltpu.VMEM(packed, BF)], name="unpack"
-    )
-    time_grad = jnp.transpose(grads[0:F].reshape(F, TAPS, F), (0, 2, 1))
-    fiber_grad = grads[F : F + PER, 0 : KF * F].reshape(PER, KF, F)
-    fiber_grad = jnp.transpose(fiber_grad, (2, 0, 1))
-    return activation[None, :, None], strain_grad[None], time_grad, fiber_grad
+        far_outs=(0,),
+    )
+    time_grad, fiber_grad = call(
+        functools.partial(finish_kernel, scale),
+        (out((F, F, TAPS), F32), out((KF, PER, F), F32)),
+        mine,
+        other,
+        scratch=[pltpu.VMEM((F * TAPS, 128), F32)],
+        name="finish",
+    )
+    return activation[None, :, None], strain_grad[None], time_grad, jnp.transpose(fiber_grad, (2, 1, 0))
 
 
 def solution(mesh):

time: 67 us -> 58.6 us (0.87)
  local copies, waits for them, and re-layouts: 8.39 us -> 2.29 us
  waiting for transfers between devices: 17.9 us -> 13.6 us
  Pallas kernels: 16.1 us -> 18.3 us
    ppermute x6, waiting for transfers between devices: 5.99 us -> 0.02 us  [exchanged(): lax.ppermute(chunks[hop], 'tm', [(i, i ^ hop) for i in range(size)])]
    unnamed x15 -> x10, local copies, waits for them, and re-layouts: 5.4 us -> 2.27 us
    pallas_call x10 -> x11, Pallas kernels: 16.1 us -> 18.3 us  [call(): pl.pallas_call(kernel, out_shape=outs, in_specs=[where(k, far) for k in r...]
    reshape x5 -> x1, local copies, waits for them, and re-layouts: 1.76 us -> 0.02 us  [on_device(): jnp.transpose(fiber_kernel, (2, 1, 0)).reshape(KF * PER, F)]
    ppermute x5, waiting for transfers between devices: 7.03 us -> 8.75 us  [the longest x4 8.22 us: paired(): lax.ppermute(mine, axis, [(i, i ^ hop) for i in range(lax.axis_size(axis))])]
    ppermute x6, starting transfers between devices: 8.84 us -> 9.56 us  [exchanged(): lax.ppermute(chunks[hop], 'tm', [(i, i ^ hop) for i in range(size)])]
  transfers between devices with their start and end apart: 14 -> 14, of which waited for: 6 -> 7; matrix products, arithmetic and copies ran while one was open for 4% -> 0% of each run, Pallas kernels for 16% -> 27%
where the time goes in v3:
time: 58.6 us; the launch traced here: 58.4 us
  starting transfers between devices  23.3 us (40%)
  Pallas kernels  18.3 us (31%)
  waiting for transfers between devices  13.6 us (23%)
  local copies, waits for them, and re-layouts  2.29 us (4%)
  between operations  0.83 us (1%)
    pallas_call x11, Pallas kernels, call(): pl.pallas_call(kernel, out_shape=outs, in_specs=[where(k, far) for k in r...  18.3 us
    ppermute x6, starting transfers between devices, exchanged(): lax.ppermute(chunks[hop], 'tm', [(i, i ^ hop) for i in range(size)])  9.56 us
    ppermute x4, waiting for transfers between devices, paired(): lax.ppermute(mine, axis, [(i, i ^ hop) for i in range(lax.axis_size(axis))])  8.22 us
    ppermute x1, starting transfers between devices, on_device(): halo = lax.ppermute(tail, 'tm', [(i, i + 1) for i in range(n - 1)])  4.94 us
    ppermute x2, waiting for transfers between devices, neighbours(): other = lax.ppermute(array, axis, [(0, 1), (1, 0)])  4.85 us
    ppermute x4, starting transfers between devices, paired(): lax.ppermute(mine, axis, [(i, i ^ hop) for i in range(lax.axis_size(axis))])  4.23 us
    ppermute x2, starting transfers between devices, neighbours(): other = lax.ppermute(array, axis, [(0, 1), (1, 0)])  3.11 us
    unnamed x10, local copies, waits for them, and re-layouts  2.27 us
  transfers between devices with their start and end apart: 14, of which 7 were waited for; matrix products, arithmetic and copies ran while one was open for 0% of the time, Pallas kernels for 27%

profile of v3, /device:TPU:0, one launch (start us, length us, event | category | flops | bytes accessed | tf_op | source)
XLA Modules:
  0.0 58.4 jit_solution(8649207762211179883)
XLA Ops:
  0.6 0.0 copy-start
  0.6 1.2 %copy-done = bf16[1,32,128,128]{3,2,1,0:T(8,128)(2,1)S(1)} copy-done((bf16[1,32,128,128]{3,2,1,0:T(8,128)(2,1)S(1)}, bf16[1,32,128,128]{3,2,1,0:T(8,128)(2,1)}, u32[]{:S(2)}) %copy-start) | copy-done | bytes 1048600
  1.9 0.0 copy-start.1
  1.9 0.8 %tail.1 = bf16[1024,128]{1,0:T(8,128)(2,1)S(1)} custom-call(bf16[32,128,128]{2,1,0:T(8,128)(2,1)S(1)} %bitcast.8), custom_call_target="tpu_custom_call" | custom-call | tf_op jit(solution)/shard_map/tail/pallas_call | solution.py:35
  2.7 4.9 %collective-permute-start = (bf16[1024,128]{1,0:T(8,128)(2,1)S(1)}, bf16[1024,128]{1,0:T(8,128)(2,1)S(1)}, u32[]{:S(2)}, u32[]{:S(2)}) collective-permute-start(bf16[1024,128]{1,0:T(8,128)(2,1)S(1)} %tail.1), channel_id=1, source_target_pairs={{0,4},{4,8},{8,12},{1,5},{5,9},{9,13},{2,6},{6,10},{10,14},{3,7},{... | collective-permute-start | bytes 786440 | tf_op jit(solution)/shard_map/ppermute | solution.py:380
  7.6 0.0 copy-start.2
  7.7 1.0 %copy-done.2 = bf16[1,32,1,32,256]{4,3,2,1,0:T(8,128)(2,1)S(1)} copy-done((bf16[1,32,1,32,256]{4,3,2,1,0:T(8,128)(2,1)S(1)}, bf16[1,32,1,32,256]{4,3,2,1,0:T(8,128)(2,1)}, u32[]{:S(2)}) %copy-start.2) | copy-done | bytes 524312
  8.7 0.3 pack.1
  9.0 1.6 %collective-permute-start.2 = (bf16[16,32,128]{2,1,0:T(8,128)(2,1)S(1)}, bf16[16,32,128]{2,1,0:T(8,128)(2,1)S(1)}, u32[]{:S(2)}, u32[]{:S(2)}) collective-permute-start(bf16[16,32,128]{2,1,0:T(8,128)(2,1)S(1)} %get-tuple-element.41), channel_id=1, source_target_pairs={{0,4},{4,0},{8,12},{12,8},{1,5},{5,1},{9,13},{13,9},{2,6},{6,2},{1... | collective-permute-start | bytes 393224 | tf_op jit(solution)/shard_map/ppermute | solution.py:349
  10.6 1.1 %collective-permute-start.3 = (bf16[16,32,128]{2,1,0:T(8,128)(2,1)S(1)}, bf16[16,32,128]{2,1,0:T(8,128)(2,1)S(1)}, u32[]{:S(2)}, u32[]{:S(2)}) collective-permute-start(bf16[16,32,128]{2,1,0:T(8,128)(2,1)S(1)} %get-tuple-element.42), channel_id=1, source_target_pairs={{0,8},{4,12},{8,0},{12,4},{1,9},{5,13},{9,1},{13,5},{2,10},{6,14},... | collective-permute-start | bytes 393224 | tf_op jit(solution)/shard_map/ppermute | solution.py:349
  11.7 0.0 copy-start.4
  11.7 1.7 %collective-permute-start.4 = (bf16[16,32,128]{2,1,0:T(8,128)(2,1)S(1)}, bf16[16,32,128]{2,1,0:T(8,128)(2,1)S(1)}, u32[]{:S(2)}, u32[]{:S(2)}) collective-permute-start(bf16[16,32,128]{2,1,0:T(8,128)(2,1)S(1)} %get-tuple-element.43), channel_id=1, source_target_pairs={{0,12},{4,8},{8,4},{12,0},{1,13},{5,9},{9,5},{13,1},{2,14},{6,10},... | collective-permute-start | bytes 393224 | tf_op jit(solution)/shard_map/ppermute | solution.py:349
  13.4 0.0 copy-done.1
  13.4 1.8 %turn.1.strain_ref = bf16[4096,128]{1,0:T(8,128)(2,1)S(1)} custom-call(bf16[32,128,128]{2,1,0:T(8,128)(2,1)S(1)} %bitcast.9), custom_call_target="tpu_custom_call" | custom-call | tf_op jit(solution)/shard_map/turn/pallas_call | solution.py:35
  15.3 0.0 copy-done.4
  15.3 0.0 copy-done.3
  15.3 1.1 %weights.1 = (bf16[256,1536]{1,0:T(8,128)(2,1)S(1)}, bf16[512,768]{1,0:T(8,128)(2,1)S(1)}, bf16[128,1152]{1,0:T(8,128)(2,1)S(1)}, bf16[128,1152]{1,0:T(8,128)(2,1)S(1)}) custom-call(bf16[32,32,32]{2,1,0:T(8,128)(2,1)S(1)} %copy-done.3, bf16[36,32]{1,0:T(8,128)(2,1)S(1)} %reshape.11.fiber_ref), custom_call_target="tpu_custom_call" | custom-call | tf_op jit(solution)/shard_map/weights/pallas_call | solution.py:35
  16.4 0.0 collective-permute-done.halo_ref
  16.4 1.1 %inner.1 = (bf16[2048,128]{1,0:T(8,128)(2,1)S(1)}, bf16[128,128]{1,0:T(8,128)(2,1)S(1)}) custom-call(bf16[1024,128]{1,0:T(8,128)(2,1)S(1)} %collective-permute-done.halo_ref, bf16[4096,128]{1,0:T(8,128)(2,1)S(1)} %turn.1.strain_ref, bf16[256,1536]{1,0:T(8,128)(2,1)S(1)} %get-tuple-element.34.w_ref), custom_call_target="tpu_custom_call" | custom-call | tf_op jit(solution)/shard_map/inner/pallas_call | solution.py:35
  17.5 1.6 %collective-permute-start.1 = (bf16[128,128]{1,0:T(8,128)(2,1)S(1)}, bf16[128,128]{1,0:T(8,128)(2,1)S(1)}, u32[]{:S(2)}, u32[]{:S(2)}) collective-permute-start(bf16[128,128]{1,0:T(8,128)(2,1)S(1)} %get-tuple-element.36), channel_id=1, source_target_pairs={{0,2},{2,0},{1,3},{3,1},{4,6},{6,4},{5,7},{7,5},{8,10},{10,8},{9,1... | collective-permute-start | bytes 98312 | tf_op jit(solution)/shard_map/ppermute | solution.py:356
  19.1 2.4 %collective-permute-done.1.before_ref.after_ref = bf16[128,128]{1,0:T(8,128)(2,1)S(1)} collective-permute-done((bf16[128,128]{1,0:T(8,128)(2,1)S(1)}, bf16[128,128]{1,0:T(8,128)(2,1)S(1)}, u32[]{:S(2)}, u32[]{:S(2)}) %collective-permute-start.1) | collective-permute-done | bytes 32800 | tf_op jit(solution)/shard_map/ppermute | solution.py:356
  21.5 2.9 %forward.1 = (f32[2048,128]{1,0:T(8,128)S(1)}, bf16[16,32,128]{2,1,0:T(8,128)(2,1)S(1)}, bf16[16,32,128]{2,1,0:T(8,128)(2,1)S(1)}, bf16[16,32,128]{2,1,0:T(8,128)(2,1)S(1)}, bf16[16,32,128]{2,1,0:T(8,128)(2,1)S(1)}) custom-call(bf16[2048,128]{1,0:T(8,128)(2,1)S(1)} %get-tuple-element.35.u_ref, ...), custom_call_target="tpu_custom_call" | custom-call | tf_op jit(solution)/shard_map/forward/pallas_call | solution.py:35
  24.4 0.7 %collective-permute-start.6 = (bf16[16,32,128]{2,1,0:T(8,128)(2,1)S(1)}, bf16[16,32,128]{2,1,0:T(8,128)(2,1)S(1)}, u32[]{:S(2)}, u32[]{:S(2)}) collective-permute-start(bf16[16,32,128]{2,1,0:T(8,128)(2,1)S(1)} %get-tuple-element.49), channel_id=1, source_target_pairs={{0,4},{4,0},{8,12},{12,8},{1,5},{5,1},{9,13},{13,9},{2,6},{6,2},{1... | collective-permute-start | bytes 393224 | tf_op jit(solution)/shard_map/ppermute | solution.py:349
  25.1 4.4 %collective-permute-start.7 = (bf16[16,32,128]{2,1,0:T(8,128)(2,1)S(1)}, bf16[16,32,128]{2,1,0:T(8,128)(2,1)S(1)}, u32[]{:S(2)}, u32[]{:S(2)}) collective-permute-start(bf16[16,32,128]{2,1,0:T(8,128)(2,1)S(1)} %get-tuple-element.50), channel_id=1, source_target_pairs={{0,8},{4,12},{8,0},{12,4},{1,9},{5,13},{9,1},{13,5},{2,10},{6,14},... | collective-permute-start | bytes 393224 | tf_op jit(solution)/shard_map/ppermute | solution.py:349
  29.5 0.0 collective-permute-done.2.refs_1_
  29.5 0.0 collective-permute-start.8
  29.5 0.0 collective-permute-done.3.refs_2_
  29.5 0.0 collective-permute-done.4.refs_3_
  29.5 1.2 %slope.1 = (bf16[2048,128]{1,0:T(8,128)(2,1)S(1)}, bf16[128,128]{1,0:T(8,128)(2,1)S(1)}) custom-call(f32[2048,128]{1,0:T(8,128)S(1)} %get-tuple-element.38.slope_ref, bf16[16,32,128]{2,1,0:T(8,128)(2,1)S(1)} %get-tuple-element.40.refs_0_, bf16[16,32,128]{2,1,0:T(8,128)(2,1)S(1)} %collective-permute-done.2.refs_1_, ...), custom_call_target="tpu_custom_call" | custom-call | tf_op jit(solution)/shard_map/slope/pallas_call | solution.py:35
  30.7 1.6 %collective-permute-start.5 = (bf16[128,128]{1,0:T(8,128)(2,1)S(1)}, bf16[128,128]{1,0:T(8,128)(2,1)S(1)}, u32[]{:S(2)}, u32[]{:S(2)}) collective-permute-start(bf16[128,128]{1,0:T(8,128)(2,1)S(1)} %get-tuple-element.45), channel_id=1, source_target_pairs={{0,2},{2,0},{1,3},{3,1},{4,6},{6,4},{5,7},{7,5},{8,10},{10,8},{9,1... | collective-permute-start | bytes 98312 | tf_op jit(solution)/shard_map/ppermute | solution.py:356
  32.3 2.4 %collective-permute-done.5.before_ref.after_ref = bf16[128,128]{1,0:T(8,128)(2,1)S(1)} collective-permute-done((bf16[128,128]{1,0:T(8,128)(2,1)S(1)}, bf16[128,128]{1,0:T(8,128)(2,1)S(1)}, u32[]{:S(2)}, u32[]{:S(2)}) %collective-permute-start.5) | collective-permute-done | bytes 32800 | tf_op jit(solution)/shard_map/ppermute | solution.py:356
  34.7 3.5 %backward.1 = (bf16[2048,128]{1,0:T(8,128)(2,1)S(1)}, f32[40,1024]{1,0:T(8,128)S(1)}) custom-call(bf16[2048,128]{1,0:T(8,128)(2,1)S(1)} %get-tuple-element.44.dz_ref, bf16[128,128]{1,0:T(8,128)(2,1)S(1)} %collective-permute-done.5.before_ref.after_ref, bf16[128,128]{1,0:T(8,128)(2,1)S(1)} %collective-permute-done.5.before_ref.after_ref, ...), custom_call_target="tpu_custom_call" | custom-call | tf_op jit(solution)/shard_map/backward/pallas_call | solution.py:35
  38.2 0.0 collective-permute-done.6.refs_1_
  38.2 0.0 collective-permute-done.7.refs_2_
  38.2 0.0 collective-permute-done.8.refs_3_
  38.3 0.1 collective-permute-start.9
  38.3 1.3 %collective-permute-done.9 = bf16[40,1024]{1,0:T(8,128)(2,1)S(1)} collective-permute-done((bf16[40,1024]{1,0:T(8,128)(2,1)S(1)}, bf16[40,1024]{1,0:T(8,128)(2,1)S(1)}, u32[]{:S(2)}, u32[]{:S(2)}) %collective-permute-start.9) | collective-permute-done | bytes 81952 | tf_op jit(solution)/shard_map/ppermute | solution.py:365
  39.6 1.6 %collective-permute-start.10 = (bf16[40,1024]{1,0:T(8,128)(2,1)S(1)}, bf16[40,1024]{1,0:T(8,128)(2,1)S(1)}, u32[]{:S(2)}, u32[]{:S(2)}) collective-permute-start(bf16[40,1024]{1,0:T(8,128)(2,1)S(1)} %add_convert_fusion.1), channel_id=1, source_target_pairs={{0,2},{2,0},{1,3},{3,1},{4,6},{6,4},{5,7},{7,5},{8,10},{10,8},{9,1... | collective-permute-start | bytes 245768 | tf_op jit(solution)/shard_map/ppermute | solution.py:365
  41.2 1.0 %unpack.1 = bf16[32,32,256]{2,1,0:T(8,128)(2,1)} custom-call(bf16[16,32,128]{2,1,0:T(8,128)(2,1)S(1)} %get-tuple-element.54.refs_0_, bf16[16,32,128]{2,1,0:T(8,128)(2,1)S(1)} %collective-permute-done.6.refs_1_, bf16[16,32,128]{2,1,0:T(8,128)(2,1)S(1)} %collective-permute-done.7.refs_2_, bf16[16,32,128]{2,1,0:T(8,128)(2,1)S(1)} %collective-permute-done.8.refs_3_), custom_call_target="tpu_custom_call" | custom-call | tf_op jit(solution)/shard_map/unpack/pallas_call | solution.py:35
  42.2 2.0 %collective-permute-done.10 = bf16[40,1024]{1,0:T(8,128)(2,1)S(1)} collective-permute-done((bf16[40,1024]{1,0:T(8,128)(2,1)S(1)}, bf16[40,1024]{1,0:T(8,128)(2,1)S(1)}, u32[]{:S(2)}, u32[]{:S(2)}) %collective-permute-start.10) | collective-permute-done | bytes 81952 | tf_op jit(solution)/shard_map/ppermute | solution.py:365
  44.2 0.6 %collective-permute-start.12 = (bf16[40,1024]{1,0:T(8,128)(2,1)S(1)}, bf16[40,1024]{1,0:T(8,128)(2,1)S(1)}, u32[]{:S(2)}, u32[]{:S(2)}) collective-permute-start(bf16[40,1024]{1,0:T(8,128)(2,1)S(1)} %convert_add_fusion), channel_id=1, source_target_pairs={{0,4},{4,0},{8,12},{12,8},{1,5},{5,1},{9,13},{13,9},{2,6},{6,2},{1... | collective-permute-start | bytes 245768 | tf_op jit(solution)/shard_map/ppermute | solution.py:365
  44.8 1.5 %collective-permute-start.11 = (bf16[512,128]{1,0:T(8,128)(2,1)S(1)}, bf16[512,128]{1,0:T(8,128)(2,1)S(1)}, u32[]{:S(2)}, u32[]{:S(2)}) collective-permute-start(bf16[512,128]{1,0:T(8,128)(2,1)S(1)} %slice.3), channel_id=1, source_target_pairs={{4,0},{8,4},{12,8},{5,1},{9,5},{13,9},{6,2},{10,6},{14,10},{7,3},{... | collective-permute-start | bytes 393224 | tf_op jit(solution)/shard_map/ppermute | solution.py:455
  46.3 2.8 %collective-permute-done.12 = bf16[40,1024]{1,0:T(8,128)(2,1)S(1)} collective-permute-done((bf16[40,1024]{1,0:T(8,128)(2,1)S(1)}, bf16[40,1024]{1,0:T(8,128)(2,1)S(1)}, u32[]{:S(2)}, u32[]{:S(2)}) %collective-permute-start.12) | collective-permute-done | bytes 81952 | tf_op jit(solution)/shard_map/ppermute | solution.py:365
  49.2 2.0 %collective-permute-start.13 = (bf16[40,1024]{1,0:T(8,128)(2,1)S(1)}, bf16[40,1024]{1,0:T(8,128)(2,1)S(1)}, u32[]{:S(2)}, u32[]{:S(2)}) collective-permute-start(bf16[40,1024]{1,0:T(8,128)(2,1)S(1)} %add_convert_fusion.mine_ref), channel_id=1, source_target_pairs={{0,8},{4,12},{8,0},{12,4},{1,9},{5,13},{9,1},{13,5},{2,10},{6,14},... | collective-permute-start | bytes 245768 | tf_op jit(solution)/shard_map/ppermute | solution.py:365
  51.2 0.5 collective-permute-done.11.late_ref
  51.7 2.9 %signal.1 = bf16[32,128,128]{2,1,0:T(8,128)(2,1)} custom-call(bf16[2048,128]{1,0:T(8,128)(2,1)S(1)} %get-tuple-element.53.du_ref, bf16[512,128]{1,0:T(8,128)(2,1)S(1)} %collective-permute-done.11.late_ref, bf16[512,768]{1,0:T(8,128)(2,1)S(1)} %get-tuple-element.60.v_ref), custom_call_target="tpu_custom_call" | custom-call | tf_op jit(solution)/shard_map/signal/pallas_call | solution.py:35
  54.6 2.2 %collective-permute-done.13.other_ref = bf16[40,1024]{1,0:T(8,128)(2,1)S(1)} collective-permute-done((bf16[40,1024]{1,0:T(8,128)(2,1)S(1)}, bf16[40,1024]{1,0:T(8,128)(2,1)S(1)}, u32[]{:S(2)}, u32[]{:S(2)}) %collective-permute-start.13) | collective-permute-done | bytes 81952 | tf_op jit(solution)/shard_map/ppermute | solution.py:365
  56.8 1.6 %finish.1 = (f32[32,32,32]{2,1,0:T(8,128)}, f32[9,4,32]{2,1,0:T(4,128)}) custom-call(bf16[40,1024]{1,0:T(8,128)(2,1)S(1)} %add_convert_fusion.mine_ref, bf16[40,1024]{1,0:T(8,128)(2,1)S(1)} %collective-permute-done.13.other_ref), custom_call_target="tpu_custom_call" | custom-call | tf_op jit(solution)/shard_map/finish/pallas_call | solution.py:35
  (7 shorter events, 0.1 us)
Async XLA Ops:
  0.6 1.2 %copy-start = (bf16[1,32,128,128]{3,2,1,0:T(8,128)(2,1)S(1)}, bf16[1,32,128,128]{3,2,1,0:T(8,128)(2,1)}, u32[]{:S(2)}) copy-start(bf16[1,32,128,128]{3,2,1,0:T(8,128)(2,1)} %param.4) | copy-start | bytes 3145732
  1.9 11.6 %copy-start.1 = (bf16[1,32,128,128]{3,2,1,0:T(8,128)(2,1)S(1)}, bf16[1,32,128,128]{3,2,1,0:T(8,128)(2,1)}, u32[]{:S(2)}) copy-start(bf16[1,32,128,128]{3,2,1,0:T(8,128)(2,1)} %param.4) | copy-start | bytes 3145732
  2.7 13.7 %collective-permute-start = (bf16[1024,128]{1,0:T(8,128)(2,1)S(1)}, bf16[1024,128]{1,0:T(8,128)(2,1)S(1)}, u32[]{:S(2)}, u32[]{:S(2)}) collective-permute-start(bf16[1024,128]{1,0:T(8,128)(2,1)S(1)} %tail.1), channel_id=1, source_target_pairs={{0,4},{4,8},{8,12},{1,5},{5,9},{9,13},{2,6},{6,10},{10,14},{3,7},{... | collective-permute-start | bytes 786440 | tf_op jit(solution)/shard_map/ppermute | solution.py:380
  7.6 1.0 %copy-start.2 = (bf16[1,32,1,32,256]{4,3,2,1,0:T(8,128)(2,1)S(1)}, bf16[1,32,1,32,256]{4,3,2,1,0:T(8,128)(2,1)}, u32[]{:S(2)}) copy-start(bf16[1,32,1,32,256]{4,3,2,1,0:T(8,128)(2,1)} %param.7) | copy-start | bytes 1572868
  9.0 20.5 %collective-permute-start.2 = (bf16[16,32,128]{2,1,0:T(8,128)(2,1)S(1)}, bf16[16,32,128]{2,1,0:T(8,128)(2,1)S(1)}, u32[]{:S(2)}, u32[]{:S(2)}) collective-permute-start(bf16[16,32,128]{2,1,0:T(8,128)(2,1)S(1)} %get-tuple-element.41), channel_id=1, source_target_pairs={{0,4},{4,0},{8,12},{12,8},{1,5},{5,1},{9,13},{13,9},{2,6},{6,2},{1... | collective-permute-start | bytes 393224 | tf_op jit(solution)/shard_map/ppermute | solution.py:349
  10.6 18.9 %collective-permute-start.3 = (bf16[16,32,128]{2,1,0:T(8,128)(2,1)S(1)}, bf16[16,32,128]{2,1,0:T(8,128)(2,1)S(1)}, u32[]{:S(2)}, u32[]{:S(2)}) collective-permute-start(bf16[16,32,128]{2,1,0:T(8,128)(2,1)S(1)} %get-tuple-element.42), channel_id=1, source_target_pairs={{0,8},{4,12},{8,0},{12,4},{1,9},{5,13},{9,1},{13,5},{2,10},{6,14},... | collective-permute-start | bytes 393224 | tf_op jit(solution)/shard_map/ppermute | solution.py:349
  11.7 3.6 %copy-start.4 = (bf16[32,4,9]{0,1,2:T(4,128)(2,1)S(1)}, bf16[32,4,9]{0,1,2:T(4,128)(2,1)}, u32[]{:S(2)}) copy-start(bf16[32,4,9]{0,1,2:T(4,128)(2,1)} %param.6) | copy-start | bytes 6916
  11.7 3.6 %copy-start.3 = (bf16[32,32,32]{2,1,0:T(8,128)(2,1)S(1)}, bf16[32,32,32]{2,1,0:T(8,128)(2,1)}, u32[]{:S(2)}) copy-start(bf16[32,32,32]{2,1,0:T(8,128)(2,1)} %time_ref.1) | copy-start | bytes 196612
  11.7 17.8 %collective-permute-start.4 = (bf16[16,32,128]{2,1,0:T(8,128)(2,1)S(1)}, bf16[16,32,128]{2,1,0:T(8,128)(2,1)S(1)}, u32[]{:S(2)}, u32[]{:S(2)}) collective-permute-start(bf16[16,32,128]{2,1,0:T(8,128)(2,1)S(1)} %get-tuple-element.43), channel_id=1, source_target_pairs={{0,12},{4,8},{8,4},{12,0},{1,13},{5,9},{9,5},{13,1},{2,14},{6,10},... | collective-permute-start | bytes 393224 | tf_op jit(solution)/shard_map/ppermute | solution.py:349
  17.5 4.0 %collective-permute-start.1 = (bf16[128,128]{1,0:T(8,128)(2,1)S(1)}, bf16[128,128]{1,0:T(8,128)(2,1)S(1)}, u32[]{:S(2)}, u32[]{:S(2)}) collective-permute-start(bf16[128,128]{1,0:T(8,128)(2,1)S(1)} %get-tuple-element.36), channel_id=1, source_target_pairs={{0,2},{2,0},{1,3},{3,1},{4,6},{6,4},{5,7},{7,5},{8,10},{10,8},{9,1... | collective-permute-start | bytes 98312 | tf_op jit(solution)/shard_map/ppermute | solution.py:356
  24.4 13.8 %collective-permute-start.6 = (bf16[16,32,128]{2,1,0:T(8,128)(2,1)S(1)}, bf16[16,32,128]{2,1,0:T(8,128)(2,1)S(1)}, u32[]{:S(2)}, u32[]{:S(2)}) collective-permute-start(bf16[16,32,128]{2,1,0:T(8,128)(2,1)S(1)} %get-tuple-element.49), channel_id=1, source_target_pairs={{0,4},{4,0},{8,12},{12,8},{1,5},{5,1},{9,13},{13,9},{2,6},{6,2},{1... | collective-permute-start | bytes 393224 | tf_op jit(solution)/shard_map/ppermute | solution.py:349
  25.1 13.1 %collective-permute-start.7 = (bf16[16,32,128]{2,1,0:T(8,128)(2,1)S(1)}, bf16[16,32,128]{2,1,0:T(8,128)(2,1)S(1)}, u32[]{:S(2)}, u32[]{:S(2)}) collective-permute-start(bf16[16,32,128]{2,1,0:T(8,128)(2,1)S(1)} %get-tuple-element.50), channel_id=1, source_target_pairs={{0,8},{4,12},{8,0},{12,4},{1,9},{5,13},{9,1},{13,5},{2,10},{6,14},... | collective-permute-start | bytes 393224 | tf_op jit(solution)/shard_map/ppermute | solution.py:349
  29.5 8.8 %collective-permute-start.8 = (bf16[16,32,128]{2,1,0:T(8,128)(2,1)S(1)}, bf16[16,32,128]{2,1,0:T(8,128)(2,1)S(1)}, u32[]{:S(2)}, u32[]{:S(2)}) collective-permute-start(bf16[16,32,128]{2,1,0:T(8,128)(2,1)S(1)} %get-tuple-element.51), channel_id=1, source_target_pairs={{0,12},{4,8},{8,4},{12,0},{1,13},{5,9},{9,5},{13,1},{2,14},{6,10},... | collective-permute-start | bytes 393224 | tf_op jit(solution)/shard_map/ppermute | solution.py:349
  30.7 4.0 %collective-permute-start.5 = (bf16[128,128]{1,0:T(8,128)(2,1)S(1)}, bf16[128,128]{1,0:T(8,128)(2,1)S(1)}, u32[]{:S(2)}, u32[]{:S(2)}) collective-permute-start(bf16[128,128]{1,0:T(8,128)(2,1)S(1)} %get-tuple-element.45), channel_id=1, source_target_pairs={{0,2},{2,0},{1,3},{3,1},{4,6},{6,4},{5,7},{7,5},{8,10},{10,8},{9,1... | collective-permute-start | bytes 98312 | tf_op jit(solution)/shard_map/ppermute | solution.py:356
  38.3 1.3 %collective-permute-start.9 = (bf16[40,1024]{1,0:T(8,128)(2,1)S(1)}, bf16[40,1024]{1,0:T(8,128)(2,1)S(1)}, u32[]{:S(2)}, u32[]{:S(2)}) collective-permute-start(bf16[40,1024]{1,0:T(8,128)(2,1)S(1)} %convert_element_type.30), channel_id=1, source_target_pairs={{0,1},{1,0},{2,3},{3,2},{4,5},{5,4},{6,7},{7,6},{8,9},{9,8},{10,11... | collective-permute-start | bytes 245768 | tf_op jit(solution)/shard_map/ppermute | solution.py:365
  39.6 4.6 %collective-permute-start.10 = (bf16[40,1024]{1,0:T(8,128)(2,1)S(1)}, bf16[40,1024]{1,0:T(8,128)(2,1)S(1)}, u32[]{:S(2)}, u32[]{:S(2)}) collective-permute-start(bf16[40,1024]{1,0:T(8,128)(2,1)S(1)} %add_convert_fusion.1), channel_id=1, source_target_pairs={{0,2},{2,0},{1,3},{3,1},{4,6},{6,4},{5,7},{7,5},{8,10},{10,8},{9,1... | collective-permute-start | bytes 245768 | tf_op jit(solution)/shard_map/ppermute | solution.py:365
  44.2 4.9 %collective-permute-start.12 = (bf16[40,1024]{1,0:T(8,128)(2,1)S(1)}, bf16[40,1024]{1,0:T(8,128)(2,1)S(1)}, u32[]{:S(2)}, u32[]{:S(2)}) collective-permute-start(bf16[40,1024]{1,0:T(8,128)(2,1)S(1)} %convert_add_fusion), channel_id=1, source_target_pairs={{0,4},{4,0},{8,12},{12,8},{1,5},{5,1},{9,13},{13,9},{2,6},{6,2},{1... | collective-permute-start | bytes 245768 | tf_op jit(solution)/shard_map/ppermute | solution.py:365
  44.8 6.8 %collective-permute-start.11 = (bf16[512,128]{1,0:T(8,128)(2,1)S(1)}, bf16[512,128]{1,0:T(8,128)(2,1)S(1)}, u32[]{:S(2)}, u32[]{:S(2)}) collective-permute-start(bf16[512,128]{1,0:T(8,128)(2,1)S(1)} %slice.3), channel_id=1, source_target_pairs={{4,0},{8,4},{12,8},{5,1},{9,5},{13,9},{6,2},{10,6},{14,10},{7,3},{... | collective-permute-start | bytes 393224 | tf_op jit(solution)/shard_map/ppermute | solution.py:455
  49.2 7.6 %collective-permute-start.13 = (bf16[40,1024]{1,0:T(8,128)(2,1)S(1)}, bf16[40,1024]{1,0:T(8,128)(2,1)S(1)}, u32[]{:S(2)}, u32[]{:S(2)}) collective-permute-start(bf16[40,1024]{1,0:T(8,128)(2,1)S(1)} %add_convert_fusion.mine_ref), channel_id=1, source_target_pairs={{0,8},{4,12},{8,0},{12,4},{1,9},{5,13},{9,1},{13,5},{2,10},{6,14},... | collective-permute-start | bytes 245768 | tf_op jit(solution)/shard_map/ppermute | solution.py:365

commit v4 on v3

--- a/solution.py
+++ b/solution.py
@@ -23,6 +23,9 @@
 GROWS = TG * F
 NG = TOUT // TG
 VWIN = 24 * F
+CORES = [(0, 1), (1, 0)]
+HALF = TAPS * F // 2
+EARLY = STEPS - HALO
 LATE = 16
 BF = jnp.bfloat16
 F32 = jnp.float32
@@ -85,12 +88,21 @@
     place(chunks, refs[:-1])
 
 
-def tail_kernel(strain_ref, halo_out, scratch):
+def tail_kernel(strain_ref, halo_out, strain_out, scratch, sems):
+    each = F // 4
+    copies = [
+        pltpu.make_async_copy(strain_ref.at[pl.ds(each * k, each)], strain_out.at[pl.ds(each * k, each)], sems.at[k])
+        for k in range(4)
+    ]
+    for copy in copies:
+        copy.start()
     group = lanes((1, 128)) // HALO
     for i4 in range(F // 4):
-        tile = roll(strain_ref[4 * i4], HALO)
+        if i4 % 2 == 0:
+            copies[i4 // 2].wait()
+        tile = roll(strain_out[4 * i4], HALO)
         for e in range(1, 4):
-            tile = jnp.where(group == e, roll(strain_ref[4 * i4 + e], HALO * (e + 1)), tile)
+            tile = jnp.where(group == e, roll(strain_out[4 * i4 + e], HALO * (e + 1)), tile)
         turned = tile.T.astype(F32)
         for e in range(4):
             scratch[pl.ds(4 * i4 + e, HALO, stride=F), :] = turned[HALO * e : HALO * (e + 1)]
@@ -232,7 +244,7 @@
     edge_out[...] = pack_edges(lambda g: dz_out[GROWS * g : GROWS * (g + 1)])
 
 
-def backward_kernel(dz_ref, before_ref, after_ref, dt_ref, u_ref, halo_ref, strain_ref, du_out, grad_out):
+def backward_kernel(dz_ref, before_ref, after_ref, dt_ref, u_ref, halo_ref, strain_ref, du_out, keep_out, give_out):
     edges = edges_of(before_ref, after_ref)
     taps = jnp.zeros((GROWS, KF * GROWS), F32)
     for g in range(0, NG, 2):
@@ -281,35 +293,52 @@
     total = jnp.zeros((F, WIN), F32)
     for t in range(TB):
         total = total + roll(wide[F * t : F * (t + 1)], -2 * F * (t + 1))
-    grad_out[0:F] = total[:, 0 : TAPS * F]
     tiles.append(jnp.zeros((8, TAPS * F - len(tiles) * GROWS), F32))
-    grad_out[F : F + 8] = jnp.concatenate(tiles, axis=1)
-
-
-def signal_kernel(du_ref, late_ref, v_ref, grad_out, scratch, ready, sems):
-    size = TB * F
-    last = TOUT * F
-
-    def rows_of(b):
-        start, stop = size * b, size * b + VWIN
-        if stop <= last:
-            return du_ref[start:stop]
-        return jnp.concatenate([du_ref[start:last], late_ref[0 : stop - last]], axis=0)
-
+    total = jnp.concatenate([total[:, 0 : TAPS * F], jnp.concatenate(tiles, axis=1)], axis=0)
+    lower, upper = total[:, 0:HALF], total[:, HALF : 2 * HALF]
+    first = lax.axis_index("rep") == 0
+    keep_out[...] = jnp.where(first, lower, upper)
+    give_out[...] = jnp.where(first, upper, lower).astype(BF)
+
+
+def signal_blocks(v_ref, rows_of, blocks, scratch):
     step = 2 * TB * F
-    for b in range(0, TOUT // TB, 2):
-        pair = jnp.concatenate([rows_of(b + k) for k in range(2)], axis=1)
+    for b in range(0, len(blocks), 2):
+        pair = jnp.concatenate([rows_of(blocks[b + k]) for k in range(2)], axis=1)
         part = jnp.dot(v_ref[...], pair, preferred_element_type=F32)
         for k in range(2):
             scratch[step * (b + k) : step * (b + k + 1)] = part[:, CH * k : CH * (k + 1)]
-    each = F // 4
+
+
+def early_kernel(du_ref, v_ref, early_out, scratch):
+    size = TB * F
+    scratch[EARLY * F :] = jnp.zeros(((STEPS - EARLY) * F, CH), F32)
+    signal_blocks(v_ref, lambda b: du_ref[size * b : size * b + VWIN], range(TOUT // TB - 2), scratch)
+    for i in range(F):
+        early_out[i] = scratch[pl.ds(i, STEPS, stride=F), :].astype(BF).T
+
+
+def signal_kernel(du_ref, late_ref, v_ref, early_ref, grad_out, scratch, ready, sems):
+    size = TB * F
+    last = TOUT * F
+
+    def rows_of(b):
+        start, stop = size * b, size * b + VWIN
+        return jnp.concatenate([du_ref[start:last], late_ref[0 : stop - last]], axis=0)
+
+    signal_blocks(v_ref, rows_of, range(TOUT // TB - 2, TOUT // TB), scratch)
+    count = STEPS - EARLY
+    ends = lanes((1, 128)) >= EARLY
     copies = []
-    for k in range(4):
-        for i in range(each * k, each * (k + 1)):
-            ready[i] = scratch[pl.ds(i, STEPS, stride=F), :].astype(BF).T
-        part = pl.ds(each * k, each)
-        copies.append(pltpu.make_async_copy(ready.at[part], grad_out.at[part], sems.at[k]))
-        copies[-1].start()
+    for i4 in range(F // 4):
+        four = jnp.concatenate([scratch[pl.ds(4 * i4 + e, count, stride=F), :] for e in range(4)], axis=0)
+        turned = four.astype(BF).T
+        for e in range(4):
+            ready[4 * i4 + e] = jnp.where(ends, roll(turned, EARLY - count * e), early_ref[4 * i4 + e])
+        if i4 % 2 == 1:
+            part = pl.ds(4 * (i4 - 1), 8)
+            copies.append(pltpu.make_async_copy(ready.at[part], grad_out.at[part], sems.at[i4 // 2]))
+            copies[-1].start()
     for copy in copies:
         copy.wait()
 
@@ -329,7 +358,9 @@
 
 
 def finish_kernel(scale, mine_ref, other_ref, time_out, fiber_out, scratch):
-    total = (mine_ref[...].astype(F32) + other_ref[...].astype(F32)) * scale
+    first = lax.axis_index("rep") == 0
+    mine, other = mine_ref[...], other_ref[...]
+    total = jnp.concatenate([jnp.where(first, mine, other), jnp.where(first, other, mine)], axis=1) * scale
     for k in range(TAPS):
         tile = total[0:F, 128 * (k // 4) : 128 * (k // 4 + 1)]
         scratch[pl.ds(k, F, stride=TAPS), :] = roll(tile, -F * (k % 4))
@@ -374,13 +405,17 @@
     chunk = (F // 2, local, 128)
     packed = (n,) + chunk
     flat = (TOUT * F, CH)
-    (tail,) = call(
-        tail_kernel, (out((HALO * F, CH), BF),), x, scratch=[pltpu.VMEM((HALO * F, CH), F32)], name="tail"
+    tail, x = call(
+        tail_kernel,
+        (out((HALO * F, CH), BF), out(x.shape, BF)),
+        x,
+        scratch=[pltpu.VMEM((HALO * F, CH), F32), pltpu.SemaphoreType.DMA((4,))],
+        name="tail",
+        far=(0,),
     )
     halo = lax.ppermute(tail, "tm", [(i, i + 1) for i in range(n - 1)])
     cot, tail = lax.optimization_barrier((cotangent[0, :, 0], tail))
     sent = call(pack_kernel, (out(chunk, BF),) * n, cot, scratch=[pltpu.VMEM(packed, BF)], name="pack")
-    upstream = exchanged(sent)
 
     w, v, d, dt = call(
         weight_kernel,
@@ -398,6 +433,8 @@
     (turned,) = call(
         turn_kernel, (out((STEPS * F, CH), BF),), x, scratch=[pltpu.VMEM((STEPS * F, CH), F32)], name="turn"
     )
+    sent = [*sent[:2], *lax.optimization_barrier((turned, w, *sent[2:3]))[2:], *sent[3:]]
+    upstream = exchanged(sent)
     u, u_edge = call(
         inner_kernel,
         (out(flat, BF), out((GROWS, CH), BF)),
@@ -427,9 +464,9 @@
         name="slope",
     )
     before, after = neighbours(dz_edge, "fiber")
-    du, grads = call(
+    du, grads, give = call(
         backward_kernel,
-        (out(flat, BF), out((F + 8, TAPS * F), F32)),
+        (out(flat, BF), out((F + 8, HALF), F32), out((F + 8, HALF), BF)),
         dz,
         before,
         after,
@@ -439,39 +476,51 @@
         turned,
         name="backward",
     )
-    hops = [(axis, 1 << k) for axis in ("rep", "fiber", "tm") for k in range((lax.axis_size(axis) - 1).bit_length())]
     head = du[0 : LATE * F]
+    grads, give, *act = lax.optimization_barrier((grads, give, *act))
+    (activation,) = call(
+        unpack_kernel, (out((F, local, n * TOUT), BF),), *act, scratch=[pltpu.VMEM(packed, BF)], name="unpack"
+    )
+    grads = grads + lax.ppermute(give, "rep", CORES).astype(F32)
+    hops = [(axis, 1 << k) for axis in ("fiber", "tm") for k in range((lax.axis_size(axis) - 1).bit_length())]
+    late = lax.ppermute(head, "tm", [(i + 1, i) for i in range(n - 1)])
+    (early,) = call(
+        early_kernel,
+        (out((F, CH, STEPS), BF),),
+        du,
+        v,
+        scratch=[pltpu.VMEM((STEPS * F, CH), F32)],
+        name="early",
+    )
     for step, (axis, hop) in enumerate(hops):
-        if step == 0:
-            grads, *act = lax.optimization_barrier((grads, *act))
-            (activation,) = call(
-                unpack_kernel, (out((F, local, n * TOUT), BF),), *act, scratch=[pltpu.VMEM(packed, BF)], name="unpack"
-            )
+        if step == 1:
+            grads, activation = lax.optimization_barrier((grads, activation))
         if step == 2:
-            grads, head, activation = lax.optimization_barrier((grads, head, activation))
+            grads, early = lax.optimization_barrier((grads, early))
         mine, other = paired(grads, axis, hop)
-        if step < len(hops) - 1:
-            grads = mine.astype(F32) + other.astype(F32)
-    late = lax.ppermute(head, "tm", [(i + 1, i) for i in range(n - 1)])
+        grads = mine.astype(F32) + other.astype(F32)
     (strain_grad,) = call(
         signal_kernel,
         (out((F, CH, STEPS), BF),),
         du,
         late,
         v,
+        early,
         scratch=[
-            pltpu.VMEM((STEPS * F, CH), F32),
+            pltpu.VMEM(((STEPS - EARLY) * F, CH), F32),
             pltpu.VMEM((F, CH, STEPS), BF),
             pltpu.SemaphoreType.DMA((4,)),
         ],
         name="signal",
         far_outs=(0,),
     )
+    grads, strain_grad = lax.optimization_barrier((grads, strain_grad))
+    others = lax.ppermute(grads, "rep", CORES)
     time_grad, fiber_grad = call(
         functools.partial(finish_kernel, scale),
         (out((F, F, TAPS), F32), out((KF, PER, F), F32)),
-        mine,
-        other,
+        grads,
+        others,
         scratch=[pltpu.VMEM((F * TAPS, 128), F32)],
         name="finish",
     )

time: 58.6 us -> 55.9 us (0.954)
  waiting for transfers between devices: 13.6 us -> 8.95 us
  starting transfers between devices: 23.3 us -> 24.9 us
  Pallas kernels: 18.3 us -> 19.7 us
  local copies, waits for them, and re-layouts: 2.29 us -> 1.26 us
    ppermute x4 -> x3, waiting for transfers between devices: 8.22 us -> 1.51 us  [paired(): lax.ppermute(mine, axis, [(i, i ^ hop) for i in range(lax.axis_size(axis))])]
    ppermute x0 -> x2, waiting for transfers between devices: none -> 2.47 us  [the longest x1 1.26 us: on_device(): others = lax.ppermute(grads, 'rep', CORES)]
    ppermute x4 -> x3, starting transfers between devices: 4.23 us -> 6.62 us  [paired(): lax.ppermute(mine, axis, [(i, i ^ hop) for i in range(lax.axis_size(axis))])]
    pallas_call x11 -> x12, Pallas kernels: 18.3 us -> 19.7 us  [call(): pl.pallas_call(kernel, out_shape=outs, in_specs=[where(k, far) for k in r...]
    unnamed x10 -> x8, local copies, waits for them, and re-layouts: 2.27 us -> 1.23 us
    ppermute x6, starting transfers between devices: 9.56 us -> 8.64 us  [exchanged(): lax.ppermute(chunks[hop], 'tm', [(i, i ^ hop) for i in range(size)])]
  transfers between devices with their start and end apart: 14 -> 15, of which waited for: 7 -> 6; matrix products, arithmetic and copies ran while one was open for 0% -> 0% of each run, Pallas kernels for 27% -> 30%
where the time goes in v4:
time: 55.9 us; the launch traced here: 55.7 us
  starting transfers between devices  24.9 us (45%)
  Pallas kernels  19.7 us (35%)
  waiting for transfers between devices  8.95 us (16%)
  local copies, waits for them, and re-layouts  1.26 us (2%)
  between operations  0.85 us (2%)
    pallas_call x12, Pallas kernels, call(): pl.pallas_call(kernel, out_shape=outs, in_specs=[where(k, far) for k in r...  19.7 us
    ppermute x6, starting transfers between devices, exchanged(): lax.ppermute(chunks[hop], 'tm', [(i, i ^ hop) for i in range(size)])  8.64 us
    ppermute x3, starting transfers between devices, paired(): lax.ppermute(mine, axis, [(i, i ^ hop) for i in range(lax.axis_size(axis))])  6.62 us
    ppermute x1, starting transfers between devices, on_device(): halo = lax.ppermute(tail, 'tm', [(i, i + 1) for i in range(n - 1)])  4.94 us
    ppermute x2, waiting for transfers between devices, neighbours(): other = lax.ppermute(array, axis, [(0, 1), (1, 0)])  4.84 us
    ppermute x2, starting transfers between devices, neighbours(): other = lax.ppermute(array, axis, [(0, 1), (1, 0)])  3.12 us
    ppermute x3, waiting for transfers between devices, paired(): lax.ppermute(mine, axis, [(i, i ^ hop) for i in range(lax.axis_size(axis))])  1.51 us
    ppermute x1, starting transfers between devices, on_device(): late = lax.ppermute(head, 'tm', [(i + 1, i) for i in range(n - 1)])  1.47 us
  transfers between devices with their start and end apart: 15, of which 6 were waited for; matrix products, arithmetic and copies ran while one was open for 0% of the time, Pallas kernels for 30%

profile of v4, /device:TPU:0, one launch (start us, length us, event | category | flops | bytes accessed | tf_op | source)
XLA Modules:
  0.0 55.7 jit_solution(5232662553662826061)
XLA Ops:
  0.6 0.0 copy-start
  0.6 1.2 %copy-done = bf16[1,32,128,128]{3,2,1,0:T(8,128)(2,1)S(1)} copy-done((bf16[1,32,128,128]{3,2,1,0:T(8,128)(2,1)S(1)}, bf16[1,32,128,128]{3,2,1,0:T(8,128)(2,1)}, u32[]{:S(2)}) %copy-start) | copy-done | bytes 1048600
  1.9 1.2 %tail.1 = (bf16[1024,128]{1,0:T(8,128)(2,1)S(1)}, bf16[32,128,128]{2,1,0:T(8,128)(2,1)S(1)}) custom-call(bf16[32,128,128]{2,1,0:T(8,128)(2,1)S(1)} %bitcast.8), custom_call_target="tpu_custom_call" | custom-call | tf_op jit(solution)/shard_map/tail/pallas_call | solution.py:38
  3.1 4.9 %collective-permute-start = (bf16[1024,128]{1,0:T(8,128)(2,1)S(1)}, bf16[1024,128]{1,0:T(8,128)(2,1)S(1)}, u32[]{:S(2)}, u32[]{:S(2)}) collective-permute-start(bf16[1024,128]{1,0:T(8,128)(2,1)S(1)} %get-tuple-element.42), channel_id=1, source_target_pairs={{0,4},{4,8},{8,12},{1,5},{5,9},{9,13},{2,6},{6,10},{10,14},{3,7},{... | collective-permute-start | bytes 786440 | tf_op jit(solution)/shard_map/ppermute | solution.py:416
  8.0 0.0 copy-done.1
  8.0 0.0 copy-start.3
  8.0 0.3 pack.1
  8.3 1.6 %collective-permute-start.2 = (bf16[16,32,128]{2,1,0:T(8,128)(2,1)S(1)}, bf16[16,32,128]{2,1,0:T(8,128)(2,1)S(1)}, u32[]{:S(2)}, u32[]{:S(2)}) collective-permute-start(bf16[16,32,128]{2,1,0:T(8,128)(2,1)S(1)} %get-tuple-element.51), channel_id=1, source_target_pairs={{0,4},{4,0},{8,12},{12,8},{1,5},{5,1},{9,13},{13,9},{2,6},{6,2},{1... | collective-permute-start | bytes 393224 | tf_op jit(solution)/shard_map/ppermute | solution.py:380
  10.0 2.5 %collective-permute-start.4 = (bf16[16,32,128]{2,1,0:T(8,128)(2,1)S(1)}, bf16[16,32,128]{2,1,0:T(8,128)(2,1)S(1)}, u32[]{:S(2)}, u32[]{:S(2)}) collective-permute-start(bf16[16,32,128]{2,1,0:T(8,128)(2,1)S(1)} %get-tuple-element.54), channel_id=1, source_target_pairs={{0,12},{4,8},{8,4},{12,0},{1,13},{5,9},{9,5},{13,1},{2,14},{6,10},... | collective-permute-start | bytes 393224 | tf_op jit(solution)/shard_map/ppermute | solution.py:380
  12.4 0.0 copy-done.3
  12.5 1.8 %turn.1.strain_ref = bf16[4096,128]{1,0:T(8,128)(2,1)S(1)} custom-call(bf16[32,128,128]{2,1,0:T(8,128)(2,1)S(1)} %get-tuple-element.43.strain_ref), custom_call_target="tpu_custom_call" | custom-call | tf_op jit(solution)/shard_map/turn/pallas_call | solution.py:38
  14.3 0.0 copy-done.2
  14.3 1.1 %weights.1 = (bf16[256,1536]{1,0:T(8,128)(2,1)S(1)}, bf16[512,768]{1,0:T(8,128)(2,1)S(1)}, bf16[128,1152]{1,0:T(8,128)(2,1)S(1)}, bf16[128,1152]{1,0:T(8,128)(2,1)S(1)}) custom-call(bf16[32,32,32]{2,1,0:T(8,128)(2,1)S(1)} %copy-done.2, bf16[36,32]{1,0:T(8,128)(2,1)S(1)} %reshape.11.fiber_ref), custom_call_target="tpu_custom_call" | custom-call | tf_op jit(solution)/shard_map/weights/pallas_call | solution.py:38
  15.4 0.1 collective-permute-start.3
  15.5 0.0 collective-permute-done.halo_ref
  15.5 1.1 %inner.1 = (bf16[2048,128]{1,0:T(8,128)(2,1)S(1)}, bf16[128,128]{1,0:T(8,128)(2,1)S(1)}) custom-call(bf16[1024,128]{1,0:T(8,128)(2,1)S(1)} %collective-permute-done.halo_ref, bf16[4096,128]{1,0:T(8,128)(2,1)S(1)} %turn.1.strain_ref, bf16[256,1536]{1,0:T(8,128)(2,1)S(1)} %get-tuple-element.44.w_ref), custom_call_target="tpu_custom_call" | custom-call | tf_op jit(solution)/shard_map/inner/pallas_call | solution.py:38
  16.6 1.6 %collective-permute-start.1 = (bf16[128,128]{1,0:T(8,128)(2,1)S(1)}, bf16[128,128]{1,0:T(8,128)(2,1)S(1)}, u32[]{:S(2)}, u32[]{:S(2)}) collective-permute-start(bf16[128,128]{1,0:T(8,128)(2,1)S(1)} %get-tuple-element.46), channel_id=1, source_target_pairs={{0,2},{2,0},{1,3},{3,1},{4,6},{6,4},{5,7},{7,5},{8,10},{10,8},{9,1... | collective-permute-start | bytes 98312 | tf_op jit(solution)/shard_map/ppermute | solution.py:387
  18.2 2.4 %collective-permute-done.1.before_ref.after_ref = bf16[128,128]{1,0:T(8,128)(2,1)S(1)} collective-permute-done((bf16[128,128]{1,0:T(8,128)(2,1)S(1)}, bf16[128,128]{1,0:T(8,128)(2,1)S(1)}, u32[]{:S(2)}, u32[]{:S(2)}) %collective-permute-start.1) | collective-permute-done | bytes 32800 | tf_op jit(solution)/shard_map/ppermute | solution.py:387
  20.6 2.9 %forward.1 = (f32[2048,128]{1,0:T(8,128)S(1)}, bf16[16,32,128]{2,1,0:T(8,128)(2,1)S(1)}, bf16[16,32,128]{2,1,0:T(8,128)(2,1)S(1)}, bf16[16,32,128]{2,1,0:T(8,128)(2,1)S(1)}, bf16[16,32,128]{2,1,0:T(8,128)(2,1)S(1)}) custom-call(bf16[2048,128]{1,0:T(8,128)(2,1)S(1)} %get-tuple-element.45.u_ref, ...), custom_call_target="tpu_custom_call" | custom-call | tf_op jit(solution)/shard_map/forward/pallas_call | solution.py:38
  23.5 2.0 %collective-permute-start.6 = (bf16[16,32,128]{2,1,0:T(8,128)(2,1)S(1)}, bf16[16,32,128]{2,1,0:T(8,128)(2,1)S(1)}, u32[]{:S(2)}, u32[]{:S(2)}) collective-permute-start(bf16[16,32,128]{2,1,0:T(8,128)(2,1)S(1)} %get-tuple-element.61), channel_id=1, source_target_pairs={{0,4},{4,0},{8,12},{12,8},{1,5},{5,1},{9,13},{13,9},{2,6},{6,2},{1... | collective-permute-start | bytes 393224 | tf_op jit(solution)/shard_map/ppermute | solution.py:380
  25.4 2.4 %collective-permute-start.7 = (bf16[16,32,128]{2,1,0:T(8,128)(2,1)S(1)}, bf16[16,32,128]{2,1,0:T(8,128)(2,1)S(1)}, u32[]{:S(2)}, u32[]{:S(2)}) collective-permute-start(bf16[16,32,128]{2,1,0:T(8,128)(2,1)S(1)} %get-tuple-element.62), channel_id=1, source_target_pairs={{0,8},{4,12},{8,0},{12,4},{1,9},{5,13},{9,1},{13,5},{2,10},{6,14},... | collective-permute-start | bytes 393224 | tf_op jit(solution)/shard_map/ppermute | solution.py:380
  27.8 0.0 collective-permute-done.2.refs_1_
  27.8 0.1 collective-permute-start.8
  27.9 0.0 collective-permute-done.4.refs_3_
  27.9 0.0 collective-permute-done.3.refs_2_
  27.9 1.2 %slope.1 = (bf16[2048,128]{1,0:T(8,128)(2,1)S(1)}, bf16[128,128]{1,0:T(8,128)(2,1)S(1)}) custom-call(f32[2048,128]{1,0:T(8,128)S(1)} %get-tuple-element.48.slope_ref, bf16[16,32,128]{2,1,0:T(8,128)(2,1)S(1)} %get-tuple-element.50.refs_0_, bf16[16,32,128]{2,1,0:T(8,128)(2,1)S(1)} %collective-permute-done.2.refs_1_, ...), custom_call_target="tpu_custom_call" | custom-call | tf_op jit(solution)/shard_map/slope/pallas_call | solution.py:38
  29.2 1.6 %collective-permute-start.5 = (bf16[128,128]{1,0:T(8,128)(2,1)S(1)}, bf16[128,128]{1,0:T(8,128)(2,1)S(1)}, u32[]{:S(2)}, u32[]{:S(2)}) collective-permute-start(bf16[128,128]{1,0:T(8,128)(2,1)S(1)} %get-tuple-element.56), channel_id=1, source_target_pairs={{0,2},{2,0},{1,3},{3,1},{4,6},{6,4},{5,7},{7,5},{8,10},{10,8},{9,1... | collective-permute-start | bytes 98312 | tf_op jit(solution)/shard_map/ppermute | solution.py:387
  30.7 2.4 %collective-permute-done.5.before_ref.after_ref = bf16[128,128]{1,0:T(8,128)(2,1)S(1)} collective-permute-done((bf16[128,128]{1,0:T(8,128)(2,1)S(1)}, bf16[128,128]{1,0:T(8,128)(2,1)S(1)}, u32[]{:S(2)}, u32[]{:S(2)}) %collective-permute-start.5) | collective-permute-done | bytes 32800 | tf_op jit(solution)/shard_map/ppermute | solution.py:387
  33.2 3.6 %backward.1 = (bf16[2048,128]{1,0:T(8,128)(2,1)S(1)}, f32[40,512]{1,0:T(8,128)S(1)}, bf16[40,512]{1,0:T(8,128)(2,1)S(1)}) custom-call(bf16[2048,128]{1,0:T(8,128)(2,1)S(1)} %get-tuple-element.55.dz_ref, bf16[128,128]{1,0:T(8,128)(2,1)S(1)} %collective-permute-done.5.before_ref.after_ref, bf16[128,128]{1,0:T(8,128)(2,1)S(1)} %collective-permute-done.5.before_ref.after_ref, ...), custom_call_target="tpu_custom_call" | custom-call | tf_op jit(solution)/shard_map/backward/pallas_call | solution.py:38
  36.7 0.0 collective-permute-done.6.refs_1_
  36.7 0.0 collective-permute-done.7.refs_2_
  36.7 0.0 collective-permute-done.8.refs_3_
  36.8 0.1 collective-permute-start.9
  36.8 1.2 %collective-permute-done.9 = bf16[40,512]{1,0:T(8,128)(2,1)S(1)} collective-permute-done((bf16[40,512]{1,0:T(8,128)(2,1)S(1)}, bf16[40,512]{1,0:T(8,128)(2,1)S(1)}, u32[]{:S(2)}, u32[]{:S(2)}) %collective-permute-start.9) | collective-permute-done | bytes 40992 | tf_op jit(solution)/shard_map/ppermute | solution.py:484
  38.1 1.6 %collective-permute-start.10 = (bf16[40,512]{1,0:T(8,128)(2,1)S(1)}, bf16[40,512]{1,0:T(8,128)(2,1)S(1)}, u32[]{:S(2)}, u32[]{:S(2)}) collective-permute-start(bf16[40,512]{1,0:T(8,128)(2,1)S(1)} %add_convert_fusion), channel_id=1, source_target_pairs={{0,2},{2,0},{1,3},{3,1},{4,6},{6,4},{5,7},{7,5},{8,10},{10,8},{9,1... | collective-permute-start | bytes 122888 | tf_op jit(solution)/shard_map/ppermute | solution.py:396
  39.6 1.0 %unpack.1 = bf16[32,32,256]{2,1,0:T(8,128)(2,1)} custom-call(bf16[16,32,128]{2,1,0:T(8,128)(2,1)S(1)} %get-tuple-element.66.refs_0_, bf16[16,32,128]{2,1,0:T(8,128)(2,1)S(1)} %collective-permute-done.6.refs_1_, bf16[16,32,128]{2,1,0:T(8,128)(2,1)S(1)} %collective-permute-done.7.refs_2_, bf16[16,32,128]{2,1,0:T(8,128)(2,1)S(1)} %collective-permute-done.8.refs_3_), custom_call_target="tpu_custom_call" | custom-call | tf_op jit(solution)/shard_map/unpack/pallas_call | solution.py:38
  40.7 1.5 %collective-permute-done.10 = bf16[40,512]{1,0:T(8,128)(2,1)S(1)} collective-permute-done((bf16[40,512]{1,0:T(8,128)(2,1)S(1)}, bf16[40,512]{1,0:T(8,128)(2,1)S(1)}, u32[]{:S(2)}, u32[]{:S(2)}) %collective-permute-start.10) | collective-permute-done | bytes 40992 | tf_op jit(solution)/shard_map/ppermute | solution.py:396
  42.1 1.5 %collective-permute-start.11 = (bf16[40,512]{1,0:T(8,128)(2,1)S(1)}, bf16[40,512]{1,0:T(8,128)(2,1)S(1)}, u32[]{:S(2)}, u32[]{:S(2)}) collective-permute-start(bf16[40,512]{1,0:T(8,128)(2,1)S(1)} %convert_add_fusion.2), channel_id=1, source_target_pairs={{0,4},{4,0},{8,12},{12,8},{1,5},{5,1},{9,13},{13,9},{2,6},{6,2},{1... | collective-permute-start | bytes 122888 | tf_op jit(solution)/shard_map/ppermute | solution.py:396
  43.7 1.5 %collective-permute-start.13 = (bf16[512,128]{1,0:T(8,128)(2,1)S(1)}, bf16[512,128]{1,0:T(8,128)(2,1)S(1)}, u32[]{:S(2)}, u32[]{:S(2)}) collective-permute-start(bf16[512,128]{1,0:T(8,128)(2,1)S(1)} %slice.3), channel_id=1, source_target_pairs={{4,0},{8,4},{12,8},{5,1},{9,5},{13,9},{6,2},{10,6},{14,10},{7,3},{... | collective-permute-start | bytes 393224 | tf_op jit(solution)/shard_map/ppermute | solution.py:486
  45.2 2.0 %early.1.early_ref = bf16[32,128,128]{2,1,0:T(8,128)(2,1)S(1)} custom-call(bf16[2048,128]{1,0:T(8,128)(2,1)S(1)} %get-tuple-element.72.du_ref, bf16[512,768]{1,0:T(8,128)(2,1)S(1)} %get-tuple-element.73.v_ref), custom_call_target="tpu_custom_call" | custom-call | tf_op jit(solution)/shard_map/early/pallas_call | solution.py:38
  47.2 0.0 collective-permute-done.11
  47.2 3.5 %collective-permute-start.12 = (bf16[40,512]{1,0:T(8,128)(2,1)S(1)}, bf16[40,512]{1,0:T(8,128)(2,1)S(1)}, u32[]{:S(2)}, u32[]{:S(2)}) collective-permute-start(bf16[40,512]{1,0:T(8,128)(2,1)S(1)} %convert_add_fusion.1), channel_id=1, source_target_pairs={{0,8},{4,12},{8,0},{12,4},{1,9},{5,13},{9,1},{13,5},{2,10},{6,14},... | collective-permute-start | bytes 122888 | tf_op jit(solution)/shard_map/ppermute | solution.py:396
  50.8 0.1 collective-permute-done.13.late_ref
  50.9 1.9 %signal.1 = bf16[32,128,128]{2,1,0:T(8,128)(2,1)} custom-call(bf16[2048,128]{1,0:T(8,128)(2,1)S(1)} %get-tuple-element.72.du_ref, bf16[512,128]{1,0:T(8,128)(2,1)S(1)} %collective-permute-done.13.late_ref, bf16[512,768]{1,0:T(8,128)(2,1)S(1)} %get-tuple-element.73.v_ref, bf16[32,128,128]{2,1,0:T(8,128)(2,1)S(1)} %early.1.early_ref), custom_call_target="tpu_custom_call" | custom-call | tf_op jit(solution)/shard_map/signal/pallas_call | solution.py:38
  52.7 0.0 collective-permute-done.12
  52.8 0.1 collective-permute-start.14
  52.9 1.3 %collective-permute-done.14.other_ref = f32[40,512]{1,0:T(8,128)S(1)} collective-permute-done((f32[40,512]{1,0:T(8,128)S(1)}, f32[40,512]{1,0:T(8,128)S(1)}, u32[]{:S(2)}, u32[]{:S(2)}) %collective-permute-start.14) | collective-permute-done | bytes 81952 | tf_op jit(solution)/shard_map/ppermute | solution.py:518
  54.1 1.6 %finish.1 = (f32[32,32,32]{2,1,0:T(8,128)}, f32[9,4,32]{2,1,0:T(4,128)}) custom-call(f32[40,512]{1,0:T(8,128)S(1)} %convert_add_fusion.mine_ref, f32[40,512]{1,0:T(8,128)S(1)} %collective-permute-done.14.other_ref), custom_call_target="tpu_custom_call" | custom-call | tf_op jit(solution)/shard_map/finish/pallas_call | solution.py:38
  (8 shorter events, 0.1 us)
Async XLA Ops:
  0.6 1.2 %copy-start = (bf16[1,32,128,128]{3,2,1,0:T(8,128)(2,1)S(1)}, bf16[1,32,128,128]{3,2,1,0:T(8,128)(2,1)}, u32[]{:S(2)}) copy-start(bf16[1,32,128,128]{3,2,1,0:T(8,128)(2,1)} %param.4) | copy-start | bytes 3145732
  1.9 6.2 %copy-start.1 = (bf16[1,32,1,32,256]{4,3,2,1,0:T(8,128)(2,1)S(1)}, bf16[1,32,1,32,256]{4,3,2,1,0:T(8,128)(2,1)}, u32[]{:S(2)}) copy-start(bf16[1,32,1,32,256]{4,3,2,1,0:T(8,128)(2,1)} %param.7) | copy-start | bytes 1572868
  3.1 12.4 %collective-permute-start = (bf16[1024,128]{1,0:T(8,128)(2,1)S(1)}, bf16[1024,128]{1,0:T(8,128)(2,1)S(1)}, u32[]{:S(2)}, u32[]{:S(2)}) collective-permute-start(bf16[1024,128]{1,0:T(8,128)(2,1)S(1)} %get-tuple-element.42), channel_id=1, source_target_pairs={{0,4},{4,8},{8,12},{1,5},{5,9},{9,13},{2,6},{6,10},{10,14},{3,7},{... | collective-permute-start | bytes 786440 | tf_op jit(solution)/shard_map/ppermute | solution.py:416
  8.0 4.4 %copy-start.3 = (bf16[32,4,9]{0,1,2:T(4,128)(2,1)S(1)}, bf16[32,4,9]{0,1,2:T(4,128)(2,1)}, u32[]{:S(2)}) copy-start(bf16[32,4,9]{0,1,2:T(4,128)(2,1)} %param.6) | copy-start | bytes 6916
  8.3 19.5 %collective-permute-start.2 = (bf16[16,32,128]{2,1,0:T(8,128)(2,1)S(1)}, bf16[16,32,128]{2,1,0:T(8,128)(2,1)S(1)}, u32[]{:S(2)}, u32[]{:S(2)}) collective-permute-start(bf16[16,32,128]{2,1,0:T(8,128)(2,1)S(1)} %get-tuple-element.51), channel_id=1, source_target_pairs={{0,4},{4,0},{8,12},{12,8},{1,5},{5,1},{9,13},{13,9},{2,6},{6,2},{1... | collective-permute-start | bytes 393224 | tf_op jit(solution)/shard_map/ppermute | solution.py:380
  10.0 18.0 %collective-permute-start.4 = (bf16[16,32,128]{2,1,0:T(8,128)(2,1)S(1)}, bf16[16,32,128]{2,1,0:T(8,128)(2,1)S(1)}, u32[]{:S(2)}, u32[]{:S(2)}) collective-permute-start(bf16[16,32,128]{2,1,0:T(8,128)(2,1)S(1)} %get-tuple-element.54), channel_id=1, source_target_pairs={{0,12},{4,8},{8,4},{12,0},{1,13},{5,9},{9,5},{13,1},{2,14},{6,10},... | collective-permute-start | bytes 393224 | tf_op jit(solution)/shard_map/ppermute | solution.py:380
  12.5 1.8 %copy-start.2 = (bf16[32,32,32]{2,1,0:T(8,128)(2,1)S(1)}, bf16[32,32,32]{2,1,0:T(8,128)(2,1)}, u32[]{:S(2)}) copy-start(bf16[32,32,32]{2,1,0:T(8,128)(2,1)} %time_ref.1) | copy-start | bytes 196612
  15.4 12.6 %collective-permute-start.3 = (bf16[16,32,128]{2,1,0:T(8,128)(2,1)S(1)}, bf16[16,32,128]{2,1,0:T(8,128)(2,1)S(1)}, u32[]{:S(2)}, u32[]{:S(2)}) collective-permute-start(bf16[16,32,128]{2,1,0:T(8,128)(2,1)S(1)} %get-tuple-element.53), channel_id=1, source_target_pairs={{0,8},{4,12},{8,0},{12,4},{1,9},{5,13},{9,1},{13,5},{2,10},{6,14},... | collective-permute-start | bytes 393224 | tf_op jit(solution)/shard_map/ppermute | solution.py:380
  16.6 4.0 %collective-permute-start.1 = (bf16[128,128]{1,0:T(8,128)(2,1)S(1)}, bf16[128,128]{1,0:T(8,128)(2,1)S(1)}, u32[]{:S(2)}, u32[]{:S(2)}) collective-permute-start(bf16[128,128]{1,0:T(8,128)(2,1)S(1)} %get-tuple-element.46), channel_id=1, source_target_pairs={{0,2},{2,0},{1,3},{3,1},{4,6},{6,4},{5,7},{7,5},{8,10},{10,8},{9,1... | collective-permute-start | bytes 98312 | tf_op jit(solution)/shard_map/ppermute | solution.py:387
  23.5 13.3 %collective-permute-start.6 = (bf16[16,32,128]{2,1,0:T(8,128)(2,1)S(1)}, bf16[16,32,128]{2,1,0:T(8,128)(2,1)S(1)}, u32[]{:S(2)}, u32[]{:S(2)}) collective-permute-start(bf16[16,32,128]{2,1,0:T(8,128)(2,1)S(1)} %get-tuple-element.61), channel_id=1, source_target_pairs={{0,4},{4,0},{8,12},{12,8},{1,5},{5,1},{9,13},{13,9},{2,6},{6,2},{1... | collective-permute-start | bytes 393224 | tf_op jit(solution)/shard_map/ppermute | solution.py:380
  25.4 11.3 %collective-permute-start.7 = (bf16[16,32,128]{2,1,0:T(8,128)(2,1)S(1)}, bf16[16,32,128]{2,1,0:T(8,128)(2,1)S(1)}, u32[]{:S(2)}, u32[]{:S(2)}) collective-permute-start(bf16[16,32,128]{2,1,0:T(8,128)(2,1)S(1)} %get-tuple-element.62), channel_id=1, source_target_pairs={{0,8},{4,12},{8,0},{12,4},{1,9},{5,13},{9,1},{13,5},{2,10},{6,14},... | collective-permute-start | bytes 393224 | tf_op jit(solution)/shard_map/ppermute | solution.py:380
  27.8 8.9 %collective-permute-start.8 = (bf16[16,32,128]{2,1,0:T(8,128)(2,1)S(1)}, bf16[16,32,128]{2,1,0:T(8,128)(2,1)S(1)}, u32[]{:S(2)}, u32[]{:S(2)}) collective-permute-start(bf16[16,32,128]{2,1,0:T(8,128)(2,1)S(1)} %get-tuple-element.63), channel_id=1, source_target_pairs={{0,12},{4,8},{8,4},{12,0},{1,13},{5,9},{9,5},{13,1},{2,14},{6,10},... | collective-permute-start | bytes 393224 | tf_op jit(solution)/shard_map/ppermute | solution.py:380
  29.2 4.0 %collective-permute-start.5 = (bf16[128,128]{1,0:T(8,128)(2,1)S(1)}, bf16[128,128]{1,0:T(8,128)(2,1)S(1)}, u32[]{:S(2)}, u32[]{:S(2)}) collective-permute-start(bf16[128,128]{1,0:T(8,128)(2,1)S(1)} %get-tuple-element.56), channel_id=1, source_target_pairs={{0,2},{2,0},{1,3},{3,1},{4,6},{6,4},{5,7},{7,5},{8,10},{10,8},{9,1... | collective-permute-start | bytes 98312 | tf_op jit(solution)/shard_map/ppermute | solution.py:387
  36.8 1.3 %collective-permute-start.9 = (bf16[40,512]{1,0:T(8,128)(2,1)S(1)}, bf16[40,512]{1,0:T(8,128)(2,1)S(1)}, u32[]{:S(2)}, u32[]{:S(2)}) collective-permute-start(bf16[40,512]{1,0:T(8,128)(2,1)S(1)} %get-tuple-element.65), channel_id=1, source_target_pairs={{0,1},{1,0},{2,3},{3,2},{4,5},{5,4},{6,7},{7,6},{8,9},{9,8},{10,11... | collective-permute-start | bytes 122888 | tf_op jit(solution)/shard_map/ppermute | solution.py:484
  38.1 4.1 %collective-permute-start.10 = (bf16[40,512]{1,0:T(8,128)(2,1)S(1)}, bf16[40,512]{1,0:T(8,128)(2,1)S(1)}, u32[]{:S(2)}, u32[]{:S(2)}) collective-permute-start(bf16[40,512]{1,0:T(8,128)(2,1)S(1)} %add_convert_fusion), channel_id=1, source_target_pairs={{0,2},{2,0},{1,3},{3,1},{4,6},{6,4},{5,7},{7,5},{8,10},{10,8},{9,1... | collective-permute-start | bytes 122888 | tf_op jit(solution)/shard_map/ppermute | solution.py:396
  42.1 5.1 %collective-permute-start.11 = (bf16[40,512]{1,0:T(8,128)(2,1)S(1)}, bf16[40,512]{1,0:T(8,128)(2,1)S(1)}, u32[]{:S(2)}, u32[]{:S(2)}) collective-permute-start(bf16[40,512]{1,0:T(8,128)(2,1)S(1)} %convert_add_fusion.2), channel_id=1, source_target_pairs={{0,4},{4,0},{8,12},{12,8},{1,5},{5,1},{9,13},{13,9},{2,6},{6,2},{1... | collective-permute-start | bytes 122888 | tf_op jit(solution)/shard_map/ppermute | solution.py:396
  43.7 7.2 %collective-permute-start.13 = (bf16[512,128]{1,0:T(8,128)(2,1)S(1)}, bf16[512,128]{1,0:T(8,128)(2,1)S(1)}, u32[]{:S(2)}, u32[]{:S(2)}) collective-permute-start(bf16[512,128]{1,0:T(8,128)(2,1)S(1)} %slice.3), channel_id=1, source_target_pairs={{4,0},{8,4},{12,8},{5,1},{9,5},{13,9},{6,2},{10,6},{14,10},{7,3},{... | collective-permute-start | bytes 393224 | tf_op jit(solution)/shard_map/ppermute | solution.py:486
  47.2 5.6 %collective-permute-start.12 = (bf16[40,512]{1,0:T(8,128)(2,1)S(1)}, bf16[40,512]{1,0:T(8,128)(2,1)S(1)}, u32[]{:S(2)}, u32[]{:S(2)}) collective-permute-start(bf16[40,512]{1,0:T(8,128)(2,1)S(1)} %convert_add_fusion.1), channel_id=1, source_target_pairs={{0,8},{4,12},{8,0},{12,4},{1,9},{5,13},{9,1},{13,5},{2,10},{6,14},... | collective-permute-start | bytes 122888 | tf_op jit(solution)/shard_map/ppermute | solution.py:396
  52.8 1.3 %collective-permute-start.14 = (f32[40,512]{1,0:T(8,128)S(1)}, f32[40,512]{1,0:T(8,128)S(1)}, u32[]{:S(2)}, u32[]{:S(2)}) collective-permute-start(f32[40,512]{1,0:T(8,128)S(1)} %convert_add_fusion.mine_ref), channel_id=1, source_target_pairs={{0,1},{1,0},{2,3},{3,2},{4,5},{5,4},{6,7},{7,6},{8,9},{9,8},{10,11... | collective-permute-start | bytes 245768 | tf_op jit(solution)/shard_map/ppermute | solution.py:518

commit v5 on v4

--- a/solution.py
+++ b/solution.py
@@ -33,7 +33,7 @@
 VMEM_LIMIT = 16 * 1024 * 1024
 
 
-def call(kernel, outs, *args, scratch=(), name=None, far=(), far_outs=()):
+def call(kernel, outs, *args, scratch=(), name=None, far=(), far_outs=(), same={}):
     where = lambda k, away: pl.BlockSpec(memory_space=pltpu.HBM if k in away else pltpu.VMEM)
     return pl.pallas_call(
         kernel,
@@ -41,6 +41,7 @@
         in_specs=[where(k, far) for k in range(len(args))],
         out_specs=tuple(where(k, far_outs) for k in range(len(outs))),
         scratch_shapes=list(scratch),
+        input_output_aliases=same,
         compiler_params=pltpu.CompilerParams(vmem_limit_bytes=VMEM_LIMIT),
         name=name,
     )(*args)
@@ -88,21 +89,12 @@
     place(chunks, refs[:-1])
 
 
-def tail_kernel(strain_ref, halo_out, strain_out, scratch, sems):
-    each = F // 4
-    copies = [
-        pltpu.make_async_copy(strain_ref.at[pl.ds(each * k, each)], strain_out.at[pl.ds(each * k, each)], sems.at[k])
-        for k in range(4)
-    ]
-    for copy in copies:
-        copy.start()
+def tail_kernel(strain_ref, halo_out, strain_out, scratch):
     group = lanes((1, 128)) // HALO
     for i4 in range(F // 4):
-        if i4 % 2 == 0:
-            copies[i4 // 2].wait()
-        tile = roll(strain_out[4 * i4], HALO)
+        tile = roll(strain_ref[4 * i4], HALO)
         for e in range(1, 4):
-            tile = jnp.where(group == e, roll(strain_out[4 * i4 + e], HALO * (e + 1)), tile)
+            tile = jnp.where(group == e, roll(strain_ref[4 * i4 + e], HALO * (e + 1)), tile)
         turned = tile.T.astype(F32)
         for e in range(4):
             scratch[pl.ds(4 * i4 + e, HALO, stride=F), :] = turned[HALO * e : HALO * (e + 1)]
@@ -409,9 +401,9 @@
         tail_kernel,
         (out((HALO * F, CH), BF), out(x.shape, BF)),
         x,
-        scratch=[pltpu.VMEM((HALO * F, CH), F32), pltpu.SemaphoreType.DMA((4,))],
+        scratch=[pltpu.VMEM((HALO * F, CH), F32)],
         name="tail",
-        far=(0,),
+        same={0: 1},
     )
     halo = lax.ppermute(tail, "tm", [(i, i + 1) for i in range(n - 1)])
     cot, tail = lax.optimization_barrier((cotangent[0, :, 0], tail))

time: 55.9 us -> 55.6 us (level)
    unnamed x8 -> x7, local copies, waits for them, and re-layouts: 1.23 us -> 1.24 us
  transfers between devices with their start and end apart: 15 -> 15, of which waited for: 6 -> 6; matrix products, arithmetic and copies ran while one was open for 0% -> 0% of each run, Pallas kernels for 30% -> 31%
where the time goes in v5:
time: 55.6 us; the launch traced here: 55.4 us
  starting transfers between devices  24.9 us (45%)
  Pallas kernels  19.3 us (35%)
  waiting for transfers between devices  8.96 us (16%)
  local copies, waits for them, and re-layouts  1.27 us (2%)
  between operations  0.84 us (2%)
    pallas_call x12, Pallas kernels, call(): pl.pallas_call(kernel, out_shape=outs, in_specs=[where(k, far) for k in r...  19.3 us
    ppermute x6, starting transfers between devices, exchanged(): lax.ppermute(chunks[hop], 'tm', [(i, i ^ hop) for i in range(size)])  8.64 us
    ppermute x3, starting transfers between devices, paired(): lax.ppermute(mine, axis, [(i, i ^ hop) for i in range(lax.axis_size(axis))])  6.62 us
    ppermute x1, starting transfers between devices, on_device(): halo = lax.ppermute(tail, 'tm', [(i, i + 1) for i in range(n - 1)])  4.94 us
    ppermute x2, waiting for transfers between devices, neighbours(): other = lax.ppermute(array, axis, [(0, 1), (1, 0)])  4.85 us
    ppermute x2, starting transfers between devices, neighbours(): other = lax.ppermute(array, axis, [(0, 1), (1, 0)])  3.11 us
    ppermute x3, waiting for transfers between devices, paired(): lax.ppermute(mine, axis, [(i, i ^ hop) for i in range(lax.axis_size(axis))])  1.52 us
    ppermute x1, starting transfers between devices, on_device(): late = lax.ppermute(head, 'tm', [(i + 1, i) for i in range(n - 1)])  1.47 us
  transfers between devices with their start and end apart: 15, of which 6 were waited for; matrix products, arithmetic and copies ran while one was open for 0% of the time, Pallas kernels for 31%

profile of v5, /device:TPU:0, one launch (start us, length us, event | category | flops | bytes accessed | tf_op | source)
XLA Modules:
  0.0 55.4 jit_solution(14471324286927648749)
XLA Ops:
  0.6 1.2 %copy.13 = bf16[1,32,128,128]{3,2,1,0:T(8,128)(2,1)S(1)} copy(bf16[1,32,128,128]{3,2,1,0:T(8,128)(2,1)} %param.4) | data formatting | bytes 2097152
  1.9 0.0 copy-start
  1.9 0.8 %tail.1 = (bf16[1024,128]{1,0:T(8,128)(2,1)S(1)}, bf16[32,128,128]{2,1,0:T(8,128)(2,1)S(1)}) custom-call(bf16[32,128,128]{2,1,0:T(8,128)(2,1)S(1)} %bitcast.8), custom_call_target="tpu_custom_call", output_to_operand_aliasing={{1}: (0, {})} | custom-call | tf_op jit(solution)/shard_map/tail/pallas_call | solution.py:38
  2.7 4.9 %collective-permute-start = (bf16[1024,128]{1,0:T(8,128)(2,1)S(1)}, bf16[1024,128]{1,0:T(8,128)(2,1)S(1)}, u32[]{:S(2)}, u32[]{:S(2)}) collective-permute-start(bf16[1024,128]{1,0:T(8,128)(2,1)S(1)} %get-tuple-element.42), channel_id=1, source_target_pairs={{0,4},{4,8},{8,12},{1,5},{5,9},{9,13},{2,6},{6,10},{10,14},{3,7},{... | collective-permute-start | bytes 786440 | tf_op jit(solution)/shard_map/ppermute | solution.py:408
  7.6 0.0 copy-done
  7.6 0.0 copy-start.2
  7.7 0.3 pack.1
  8.0 1.6 %collective-permute-start.2 = (bf16[16,32,128]{2,1,0:T(8,128)(2,1)S(1)}, bf16[16,32,128]{2,1,0:T(8,128)(2,1)S(1)}, u32[]{:S(2)}, u32[]{:S(2)}) collective-permute-start(bf16[16,32,128]{2,1,0:T(8,128)(2,1)S(1)} %get-tuple-element.51), channel_id=1, source_target_pairs={{0,4},{4,0},{8,12},{12,8},{1,5},{5,1},{9,13},{13,9},{2,6},{6,2},{1... | collective-permute-start | bytes 393224 | tf_op jit(solution)/shard_map/ppermute | solution.py:372
  9.6 2.5 %collective-permute-start.4 = (bf16[16,32,128]{2,1,0:T(8,128)(2,1)S(1)}, bf16[16,32,128]{2,1,0:T(8,128)(2,1)S(1)}, u32[]{:S(2)}, u32[]{:S(2)}) collective-permute-start(bf16[16,32,128]{2,1,0:T(8,128)(2,1)S(1)} %get-tuple-element.54), channel_id=1, source_target_pairs={{0,12},{4,8},{8,4},{12,0},{1,13},{5,9},{9,5},{13,1},{2,14},{6,10},... | collective-permute-start | bytes 393224 | tf_op jit(solution)/shard_map/ppermute | solution.py:372
  12.1 0.0 copy-done.2
  12.1 1.8 %turn.1.strain_ref = bf16[4096,128]{1,0:T(8,128)(2,1)S(1)} custom-call(bf16[32,128,128]{2,1,0:T(8,128)(2,1)S(1)} %get-tuple-element.43.strain_ref), custom_call_target="tpu_custom_call" | custom-call | tf_op jit(solution)/shard_map/turn/pallas_call | solution.py:38
  13.9 0.0 copy-done.1
  13.9 1.1 %weights.1 = (bf16[256,1536]{1,0:T(8,128)(2,1)S(1)}, bf16[512,768]{1,0:T(8,128)(2,1)S(1)}, bf16[128,1152]{1,0:T(8,128)(2,1)S(1)}, bf16[128,1152]{1,0:T(8,128)(2,1)S(1)}) custom-call(bf16[32,32,32]{2,1,0:T(8,128)(2,1)S(1)} %copy-done.1, bf16[36,32]{1,0:T(8,128)(2,1)S(1)} %reshape.11.fiber_ref), custom_call_target="tpu_custom_call" | custom-call | tf_op jit(solution)/shard_map/weights/pallas_call | solution.py:38
  15.0 0.1 collective-permute-start.3
  15.1 0.0 collective-permute-done.halo_ref
  15.1 1.1 %inner.1 = (bf16[2048,128]{1,0:T(8,128)(2,1)S(1)}, bf16[128,128]{1,0:T(8,128)(2,1)S(1)}) custom-call(bf16[1024,128]{1,0:T(8,128)(2,1)S(1)} %collective-permute-done.halo_ref, bf16[4096,128]{1,0:T(8,128)(2,1)S(1)} %turn.1.strain_ref, bf16[256,1536]{1,0:T(8,128)(2,1)S(1)} %get-tuple-element.44.w_ref), custom_call_target="tpu_custom_call" | custom-call | tf_op jit(solution)/shard_map/inner/pallas_call | solution.py:38
  16.3 1.6 %collective-permute-start.1 = (bf16[128,128]{1,0:T(8,128)(2,1)S(1)}, bf16[128,128]{1,0:T(8,128)(2,1)S(1)}, u32[]{:S(2)}, u32[]{:S(2)}) collective-permute-start(bf16[128,128]{1,0:T(8,128)(2,1)S(1)} %get-tuple-element.46), channel_id=1, source_target_pairs={{0,2},{2,0},{1,3},{3,1},{4,6},{6,4},{5,7},{7,5},{8,10},{10,8},{9,1... | collective-permute-start | bytes 98312 | tf_op jit(solution)/shard_map/ppermute | solution.py:379
  17.8 2.4 %collective-permute-done.1.before_ref.after_ref = bf16[128,128]{1,0:T(8,128)(2,1)S(1)} collective-permute-done((bf16[128,128]{1,0:T(8,128)(2,1)S(1)}, bf16[128,128]{1,0:T(8,128)(2,1)S(1)}, u32[]{:S(2)}, u32[]{:S(2)}) %collective-permute-start.1) | collective-permute-done | bytes 32800 | tf_op jit(solution)/shard_map/ppermute | solution.py:379
  20.2 2.9 %forward.1 = (f32[2048,128]{1,0:T(8,128)S(1)}, bf16[16,32,128]{2,1,0:T(8,128)(2,1)S(1)}, bf16[16,32,128]{2,1,0:T(8,128)(2,1)S(1)}, bf16[16,32,128]{2,1,0:T(8,128)(2,1)S(1)}, bf16[16,32,128]{2,1,0:T(8,128)(2,1)S(1)}) custom-call(bf16[2048,128]{1,0:T(8,128)(2,1)S(1)} %get-tuple-element.45.u_ref, ...), custom_call_target="tpu_custom_call" | custom-call | tf_op jit(solution)/shard_map/forward/pallas_call | solution.py:38
  23.1 2.0 %collective-permute-start.6 = (bf16[16,32,128]{2,1,0:T(8,128)(2,1)S(1)}, bf16[16,32,128]{2,1,0:T(8,128)(2,1)S(1)}, u32[]{:S(2)}, u32[]{:S(2)}) collective-permute-start(bf16[16,32,128]{2,1,0:T(8,128)(2,1)S(1)} %get-tuple-element.61), channel_id=1, source_target_pairs={{0,4},{4,0},{8,12},{12,8},{1,5},{5,1},{9,13},{13,9},{2,6},{6,2},{1... | collective-permute-start | bytes 393224 | tf_op jit(solution)/shard_map/ppermute | solution.py:372
  25.1 2.4 %collective-permute-start.7 = (bf16[16,32,128]{2,1,0:T(8,128)(2,1)S(1)}, bf16[16,32,128]{2,1,0:T(8,128)(2,1)S(1)}, u32[]{:S(2)}, u32[]{:S(2)}) collective-permute-start(bf16[16,32,128]{2,1,0:T(8,128)(2,1)S(1)} %get-tuple-element.62), channel_id=1, source_target_pairs={{0,8},{4,12},{8,0},{12,4},{1,9},{5,13},{9,1},{13,5},{2,10},{6,14},... | collective-permute-start | bytes 393224 | tf_op jit(solution)/shard_map/ppermute | solution.py:372
  27.5 0.0 collective-permute-done.2.refs_1_
  27.5 0.1 collective-permute-start.8
  27.6 0.0 collective-permute-done.4.refs_3_
  27.6 0.0 collective-permute-done.3.refs_2_
  27.6 1.2 %slope.1 = (bf16[2048,128]{1,0:T(8,128)(2,1)S(1)}, bf16[128,128]{1,0:T(8,128)(2,1)S(1)}) custom-call(f32[2048,128]{1,0:T(8,128)S(1)} %get-tuple-element.48.slope_ref, bf16[16,32,128]{2,1,0:T(8,128)(2,1)S(1)} %get-tuple-element.50.refs_0_, bf16[16,32,128]{2,1,0:T(8,128)(2,1)S(1)} %collective-permute-done.2.refs_1_, ...), custom_call_target="tpu_custom_call" | custom-call | tf_op jit(solution)/shard_map/slope/pallas_call | solution.py:38
  28.8 1.6 %collective-permute-start.5 = (bf16[128,128]{1,0:T(8,128)(2,1)S(1)}, bf16[128,128]{1,0:T(8,128)(2,1)S(1)}, u32[]{:S(2)}, u32[]{:S(2)}) collective-permute-start(bf16[128,128]{1,0:T(8,128)(2,1)S(1)} %get-tuple-element.56), channel_id=1, source_target_pairs={{0,2},{2,0},{1,3},{3,1},{4,6},{6,4},{5,7},{7,5},{8,10},{10,8},{9,1... | collective-permute-start | bytes 98312 | tf_op jit(solution)/shard_map/ppermute | solution.py:379
  30.4 2.4 %collective-permute-done.5.before_ref.after_ref = bf16[128,128]{1,0:T(8,128)(2,1)S(1)} collective-permute-done((bf16[128,128]{1,0:T(8,128)(2,1)S(1)}, bf16[128,128]{1,0:T(8,128)(2,1)S(1)}, u32[]{:S(2)}, u32[]{:S(2)}) %collective-permute-start.5) | collective-permute-done | bytes 32800 | tf_op jit(solution)/shard_map/ppermute | solution.py:379
  32.8 3.6 %backward.1 = (bf16[2048,128]{1,0:T(8,128)(2,1)S(1)}, f32[40,512]{1,0:T(8,128)S(1)}, bf16[40,512]{1,0:T(8,128)(2,1)S(1)}) custom-call(bf16[2048,128]{1,0:T(8,128)(2,1)S(1)} %get-tuple-element.55.dz_ref, bf16[128,128]{1,0:T(8,128)(2,1)S(1)} %collective-permute-done.5.before_ref.after_ref, bf16[128,128]{1,0:T(8,128)(2,1)S(1)} %collective-permute-done.5.before_ref.after_ref, ...), custom_call_target="tpu_custom_call" | custom-call | tf_op jit(solution)/shard_map/backward/pallas_call | solution.py:38
  36.4 0.0 collective-permute-done.6.refs_1_
  36.4 0.0 collective-permute-done.7.refs_2_
  36.4 0.0 collective-permute-done.8.refs_3_
  36.4 0.1 collective-permute-start.9
  36.5 1.2 %collective-permute-done.9 = bf16[40,512]{1,0:T(8,128)(2,1)S(1)} collective-permute-done((bf16[40,512]{1,0:T(8,128)(2,1)S(1)}, bf16[40,512]{1,0:T(8,128)(2,1)S(1)}, u32[]{:S(2)}, u32[]{:S(2)}) %collective-permute-start.9) | collective-permute-done | bytes 40992 | tf_op jit(solution)/shard_map/ppermute | solution.py:476
  37.7 1.6 %collective-permute-start.10 = (bf16[40,512]{1,0:T(8,128)(2,1)S(1)}, bf16[40,512]{1,0:T(8,128)(2,1)S(1)}, u32[]{:S(2)}, u32[]{:S(2)}) collective-permute-start(bf16[40,512]{1,0:T(8,128)(2,1)S(1)} %add_convert_fusion), channel_id=1, source_target_pairs={{0,2},{2,0},{1,3},{3,1},{4,6},{6,4},{5,7},{7,5},{8,10},{10,8},{9,1... | collective-permute-start | bytes 122888 | tf_op jit(solution)/shard_map/ppermute | solution.py:388
  39.2 1.0 %unpack.1 = bf16[32,32,256]{2,1,0:T(8,128)(2,1)} custom-call(bf16[16,32,128]{2,1,0:T(8,128)(2,1)S(1)} %get-tuple-element.66.refs_0_, bf16[16,32,128]{2,1,0:T(8,128)(2,1)S(1)} %collective-permute-done.6.refs_1_, bf16[16,32,128]{2,1,0:T(8,128)(2,1)S(1)} %collective-permute-done.7.refs_2_, bf16[16,32,128]{2,1,0:T(8,128)(2,1)S(1)} %collective-permute-done.8.refs_3_), custom_call_target="tpu_custom_call" | custom-call | tf_op jit(solution)/shard_map/unpack/pallas_call | solution.py:38
  40.3 1.5 %collective-permute-done.10 = bf16[40,512]{1,0:T(8,128)(2,1)S(1)} collective-permute-done((bf16[40,512]{1,0:T(8,128)(2,1)S(1)}, bf16[40,512]{1,0:T(8,128)(2,1)S(1)}, u32[]{:S(2)}, u32[]{:S(2)}) %collective-permute-start.10) | collective-permute-done | bytes 40992 | tf_op jit(solution)/shard_map/ppermute | solution.py:388
  41.8 1.5 %collective-permute-start.11 = (bf16[40,512]{1,0:T(8,128)(2,1)S(1)}, bf16[40,512]{1,0:T(8,128)(2,1)S(1)}, u32[]{:S(2)}, u32[]{:S(2)}) collective-permute-start(bf16[40,512]{1,0:T(8,128)(2,1)S(1)} %convert_add_fusion.2), channel_id=1, source_target_pairs={{0,4},{4,0},{8,12},{12,8},{1,5},{5,1},{9,13},{13,9},{2,6},{6,2},{1... | collective-permute-start | bytes 122888 | tf_op jit(solution)/shard_map/ppermute | solution.py:388
  43.3 1.5 %collective-permute-start.13 = (bf16[512,128]{1,0:T(8,128)(2,1)S(1)}, bf16[512,128]{1,0:T(8,128)(2,1)S(1)}, u32[]{:S(2)}, u32[]{:S(2)}) collective-permute-start(bf16[512,128]{1,0:T(8,128)(2,1)S(1)} %slice.3), channel_id=1, source_target_pairs={{4,0},{8,4},{12,8},{5,1},{9,5},{13,9},{6,2},{10,6},{14,10},{7,3},{... | collective-permute-start | bytes 393224 | tf_op jit(solution)/shard_map/ppermute | solution.py:478
  44.8 2.0 %early.1.early_ref = bf16[32,128,128]{2,1,0:T(8,128)(2,1)S(1)} custom-call(bf16[2048,128]{1,0:T(8,128)(2,1)S(1)} %get-tuple-element.72.du_ref, bf16[512,768]{1,0:T(8,128)(2,1)S(1)} %get-tuple-element.73.v_ref), custom_call_target="tpu_custom_call" | custom-call | tf_op jit(solution)/shard_map/early/pallas_call | solution.py:38
  46.8 0.0 collective-permute-done.11
  46.9 3.5 %collective-permute-start.12 = (bf16[40,512]{1,0:T(8,128)(2,1)S(1)}, bf16[40,512]{1,0:T(8,128)(2,1)S(1)}, u32[]{:S(2)}, u32[]{:S(2)}) collective-permute-start(bf16[40,512]{1,0:T(8,128)(2,1)S(1)} %convert_add_fusion.1), channel_id=1, source_target_pairs={{0,8},{4,12},{8,0},{12,4},{1,9},{5,13},{9,1},{13,5},{2,10},{6,14},... | collective-permute-start | bytes 122888 | tf_op jit(solution)/shard_map/ppermute | solution.py:388
  50.4 0.1 collective-permute-done.13.late_ref
  50.5 1.9 %signal.1 = bf16[32,128,128]{2,1,0:T(8,128)(2,1)} custom-call(bf16[2048,128]{1,0:T(8,128)(2,1)S(1)} %get-tuple-element.72.du_ref, bf16[512,128]{1,0:T(8,128)(2,1)S(1)} %collective-permute-done.13.late_ref, bf16[512,768]{1,0:T(8,128)(2,1)S(1)} %get-tuple-element.73.v_ref, bf16[32,128,128]{2,1,0:T(8,128)(2,1)S(1)} %early.1.early_ref), custom_call_target="tpu_custom_call" | custom-call | tf_op jit(solution)/shard_map/signal/pallas_call | solution.py:38
  52.4 0.0 collective-permute-done.12
  52.4 0.1 collective-permute-start.14
  52.5 1.3 %collective-permute-done.14.other_ref = f32[40,512]{1,0:T(8,128)S(1)} collective-permute-done((f32[40,512]{1,0:T(8,128)S(1)}, f32[40,512]{1,0:T(8,128)S(1)}, u32[]{:S(2)}, u32[]{:S(2)}) %collective-permute-start.14) | collective-permute-done | bytes 81952 | tf_op jit(solution)/shard_map/ppermute | solution.py:510
  53.8 1.6 %finish.1 = (f32[32,32,32]{2,1,0:T(8,128)}, f32[9,4,32]{2,1,0:T(4,128)}) custom-call(f32[40,512]{1,0:T(8,128)S(1)} %convert_add_fusion.mine_ref, f32[40,512]{1,0:T(8,128)S(1)} %collective-permute-done.14.other_ref), custom_call_target="tpu_custom_call" | custom-call | tf_op jit(solution)/shard_map/finish/pallas_call | solution.py:38
  (7 shorter events, 0.1 us)
Async XLA Ops:
  1.9 5.8 %copy-start = (bf16[1,32,1,32,256]{4,3,2,1,0:T(8,128)(2,1)S(1)}, bf16[1,32,1,32,256]{4,3,2,1,0:T(8,128)(2,1)}, u32[]{:S(2)}) copy-start(bf16[1,32,1,32,256]{4,3,2,1,0:T(8,128)(2,1)} %param.7) | copy-start | bytes 1572868
  2.7 12.4 %collective-permute-start = (bf16[1024,128]{1,0:T(8,128)(2,1)S(1)}, bf16[1024,128]{1,0:T(8,128)(2,1)S(1)}, u32[]{:S(2)}, u32[]{:S(2)}) collective-permute-start(bf16[1024,128]{1,0:T(8,128)(2,1)S(1)} %get-tuple-element.42), channel_id=1, source_target_pairs={{0,4},{4,8},{8,12},{1,5},{5,9},{9,13},{2,6},{6,10},{10,14},{3,7},{... | collective-permute-start | bytes 786440 | tf_op jit(solution)/shard_map/ppermute | solution.py:408
  7.6 4.4 %copy-start.2 = (bf16[32,4,9]{0,1,2:T(4,128)(2,1)S(1)}, bf16[32,4,9]{0,1,2:T(4,128)(2,1)}, u32[]{:S(2)}) copy-start(bf16[32,4,9]{0,1,2:T(4,128)(2,1)} %param.6) | copy-start | bytes 6916
  8.0 19.5 %collective-permute-start.2 = (bf16[16,32,128]{2,1,0:T(8,128)(2,1)S(1)}, bf16[16,32,128]{2,1,0:T(8,128)(2,1)S(1)}, u32[]{:S(2)}, u32[]{:S(2)}) collective-permute-start(bf16[16,32,128]{2,1,0:T(8,128)(2,1)S(1)} %get-tuple-element.51), channel_id=1, source_target_pairs={{0,4},{4,0},{8,12},{12,8},{1,5},{5,1},{9,13},{13,9},{2,6},{6,2},{1... | collective-permute-start | bytes 393224 | tf_op jit(solution)/shard_map/ppermute | solution.py:372
  9.6 18.0 %collective-permute-start.4 = (bf16[16,32,128]{2,1,0:T(8,128)(2,1)S(1)}, bf16[16,32,128]{2,1,0:T(8,128)(2,1)S(1)}, u32[]{:S(2)}, u32[]{:S(2)}) collective-permute-start(bf16[16,32,128]{2,1,0:T(8,128)(2,1)S(1)} %get-tuple-element.54), channel_id=1, source_target_pairs={{0,12},{4,8},{8,4},{12,0},{1,13},{5,9},{9,5},{13,1},{2,14},{6,10},... | collective-permute-start | bytes 393224 | tf_op jit(solution)/shard_map/ppermute | solution.py:372
  12.1 1.8 %copy-start.1 = (bf16[32,32,32]{2,1,0:T(8,128)(2,1)S(1)}, bf16[32,32,32]{2,1,0:T(8,128)(2,1)}, u32[]{:S(2)}) copy-start(bf16[32,32,32]{2,1,0:T(8,128)(2,1)} %time_ref.1) | copy-start | bytes 196612
  15.0 12.6 %collective-permute-start.3 = (bf16[16,32,128]{2,1,0:T(8,128)(2,1)S(1)}, bf16[16,32,128]{2,1,0:T(8,128)(2,1)S(1)}, u32[]{:S(2)}, u32[]{:S(2)}) collective-permute-start(bf16[16,32,128]{2,1,0:T(8,128)(2,1)S(1)} %get-tuple-element.53), channel_id=1, source_target_pairs={{0,8},{4,12},{8,0},{12,4},{1,9},{5,13},{9,1},{13,5},{2,10},{6,14},... | collective-permute-start | bytes 393224 | tf_op jit(solution)/shard_map/ppermute | solution.py:372
  16.3 4.0 %collective-permute-start.1 = (bf16[128,128]{1,0:T(8,128)(2,1)S(1)}, bf16[128,128]{1,0:T(8,128)(2,1)S(1)}, u32[]{:S(2)}, u32[]{:S(2)}) collective-permute-start(bf16[128,128]{1,0:T(8,128)(2,1)S(1)} %get-tuple-element.46), channel_id=1, source_target_pairs={{0,2},{2,0},{1,3},{3,1},{4,6},{6,4},{5,7},{7,5},{8,10},{10,8},{9,1... | collective-permute-start | bytes 98312 | tf_op jit(solution)/shard_map/ppermute | solution.py:379
  23.1 13.3 %collective-permute-start.6 = (bf16[16,32,128]{2,1,0:T(8,128)(2,1)S(1)}, bf16[16,32,128]{2,1,0:T(8,128)(2,1)S(1)}, u32[]{:S(2)}, u32[]{:S(2)}) collective-permute-start(bf16[16,32,128]{2,1,0:T(8,128)(2,1)S(1)} %get-tuple-element.61), channel_id=1, source_target_pairs={{0,4},{4,0},{8,12},{12,8},{1,5},{5,1},{9,13},{13,9},{2,6},{6,2},{1... | collective-permute-start | bytes 393224 | tf_op jit(solution)/shard_map/ppermute | solution.py:372
  25.1 11.3 %collective-permute-start.7 = (bf16[16,32,128]{2,1,0:T(8,128)(2,1)S(1)}, bf16[16,32,128]{2,1,0:T(8,128)(2,1)S(1)}, u32[]{:S(2)}, u32[]{:S(2)}) collective-permute-start(bf16[16,32,128]{2,1,0:T(8,128)(2,1)S(1)} %get-tuple-element.62), channel_id=1, source_target_pairs={{0,8},{4,12},{8,0},{12,4},{1,9},{5,13},{9,1},{13,5},{2,10},{6,14},... | collective-permute-start | bytes 393224 | tf_op jit(solution)/shard_map/ppermute | solution.py:372
  27.5 8.9 %collective-permute-start.8 = (bf16[16,32,128]{2,1,0:T(8,128)(2,1)S(1)}, bf16[16,32,128]{2,1,0:T(8,128)(2,1)S(1)}, u32[]{:S(2)}, u32[]{:S(2)}) collective-permute-start(bf16[16,32,128]{2,1,0:T(8,128)(2,1)S(1)} %get-tuple-element.63), channel_id=1, source_target_pairs={{0,12},{4,8},{8,4},{12,0},{1,13},{5,9},{9,5},{13,1},{2,14},{6,10},... | collective-permute-start | bytes 393224 | tf_op jit(solution)/shard_map/ppermute | solution.py:372
  28.8 4.0 %collective-permute-start.5 = (bf16[128,128]{1,0:T(8,128)(2,1)S(1)}, bf16[128,128]{1,0:T(8,128)(2,1)S(1)}, u32[]{:S(2)}, u32[]{:S(2)}) collective-permute-start(bf16[128,128]{1,0:T(8,128)(2,1)S(1)} %get-tuple-element.56), channel_id=1, source_target_pairs={{0,2},{2,0},{1,3},{3,1},{4,6},{6,4},{5,7},{7,5},{8,10},{10,8},{9,1... | collective-permute-start | bytes 98312 | tf_op jit(solution)/shard_map/ppermute | solution.py:379
  36.4 1.3 %collective-permute-start.9 = (bf16[40,512]{1,0:T(8,128)(2,1)S(1)}, bf16[40,512]{1,0:T(8,128)(2,1)S(1)}, u32[]{:S(2)}, u32[]{:S(2)}) collective-permute-start(bf16[40,512]{1,0:T(8,128)(2,1)S(1)} %get-tuple-element.65), channel_id=1, source_target_pairs={{0,1},{1,0},{2,3},{3,2},{4,5},{5,4},{6,7},{7,6},{8,9},{9,8},{10,11... | collective-permute-start | bytes 122888 | tf_op jit(solution)/shard_map/ppermute | solution.py:476
  37.7 4.1 %collective-permute-start.10 = (bf16[40,512]{1,0:T(8,128)(2,1)S(1)}, bf16[40,512]{1,0:T(8,128)(2,1)S(1)}, u32[]{:S(2)}, u32[]{:S(2)}) collective-permute-start(bf16[40,512]{1,0:T(8,128)(2,1)S(1)} %add_convert_fusion), channel_id=1, source_target_pairs={{0,2},{2,0},{1,3},{3,1},{4,6},{6,4},{5,7},{7,5},{8,10},{10,8},{9,1... | collective-permute-start | bytes 122888 | tf_op jit(solution)/shard_map/ppermute | solution.py:388
  41.8 5.1 %collective-permute-start.11 = (bf16[40,512]{1,0:T(8,128)(2,1)S(1)}, bf16[40,512]{1,0:T(8,128)(2,1)S(1)}, u32[]{:S(2)}, u32[]{:S(2)}) collective-permute-start(bf16[40,512]{1,0:T(8,128)(2,1)S(1)} %convert_add_fusion.2), channel_id=1, source_target_pairs={{0,4},{4,0},{8,12},{12,8},{1,5},{5,1},{9,13},{13,9},{2,6},{6,2},{1... | collective-permute-start | bytes 122888 | tf_op jit(solution)/shard_map/ppermute | solution.py:388
  43.3 7.2 %collective-permute-start.13 = (bf16[512,128]{1,0:T(8,128)(2,1)S(1)}, bf16[512,128]{1,0:T(8,128)(2,1)S(1)}, u32[]{:S(2)}, u32[]{:S(2)}) collective-permute-start(bf16[512,128]{1,0:T(8,128)(2,1)S(1)} %slice.3), channel_id=1, source_target_pairs={{4,0},{8,4},{12,8},{5,1},{9,5},{13,9},{6,2},{10,6},{14,10},{7,3},{... | collective-permute-start | bytes 393224 | tf_op jit(solution)/shard_map/ppermute | solution.py:478
  46.9 5.6 %collective-permute-start.12 = (bf16[40,512]{1,0:T(8,128)(2,1)S(1)}, bf16[40,512]{1,0:T(8,128)(2,1)S(1)}, u32[]{:S(2)}, u32[]{:S(2)}) collective-permute-start(bf16[40,512]{1,0:T(8,128)(2,1)S(1)} %convert_add_fusion.1), channel_id=1, source_target_pairs={{0,8},{4,12},{8,0},{12,4},{1,9},{5,13},{9,1},{13,5},{2,10},{6,14},... | collective-permute-start | bytes 122888 | tf_op jit(solution)/shard_map/ppermute | solution.py:388
  52.4 1.3 %collective-permute-start.14 = (f32[40,512]{1,0:T(8,128)S(1)}, f32[40,512]{1,0:T(8,128)S(1)}, u32[]{:S(2)}, u32[]{:S(2)}) collective-permute-start(f32[40,512]{1,0:T(8,128)S(1)} %convert_add_fusion.mine_ref), channel_id=1, source_target_pairs={{0,1},{1,0},{2,3},{3,2},{4,5},{5,4},{6,7},{7,6},{8,9},{9,8},{10,11... | collective-permute-start | bytes 245768 | tf_op jit(solution)/shard_map/ppermute | solution.py:510

commit v6 on v5

--- a/solution.py
+++ b/solution.py
@@ -98,7 +98,7 @@
         turned = tile.T.astype(F32)
         for e in range(4):
             scratch[pl.ds(4 * i4 + e, HALO, stride=F), :] = turned[HALO * e : HALO * (e + 1)]
-    halo_out[...] = scratch[...].astype(BF)
+    halo_out[...] = scratch[(HALO - TAPS + 2) * F :].astype(BF)
 
 
 def turn_kernel(strain_ref, out_ref, scratch):
@@ -174,11 +174,13 @@
 
 
 def window(early_ref, main_ref, b, size):
-    start = 2 * TB * F * b
-    early = early_ref.shape[0]
+    start, early = 2 * TB * F * b, HALO * F
     if start >= early:
         return main_ref[start - early : start - early + size]
-    return jnp.concatenate([early_ref[start:early], main_ref[0 : size - (early - start)]], axis=0)
+    unused = early - early_ref.shape[0]
+    pieces = [main_ref[start:unused]] if start < unused else []
+    pieces += [early_ref[max(start - unused, 0) :], main_ref[0 : size - (early - start)]]
+    return jnp.concatenate(pieces, axis=0)
 
 
 def inner_kernel(halo_ref, strain_ref, w_ref, u_out, edge_out):
@@ -399,7 +401,7 @@
     flat = (TOUT * F, CH)
     tail, x = call(
         tail_kernel,
-        (out((HALO * F, CH), BF), out(x.shape, BF)),
+        (out(((TAPS - 2) * F, CH), BF), out(x.shape, BF)),
         x,
         scratch=[pltpu.VMEM((HALO * F, CH), F32)],
         name="tail",
@@ -486,9 +488,9 @@
     )
     for step, (axis, hop) in enumerate(hops):
         if step == 1:
+            grads, early = lax.optimization_barrier((grads, early))
+        if step == 2:
             grads, activation = lax.optimization_barrier((grads, activation))
-        if step == 2:
-            grads, early = lax.optimization_barrier((grads, early))
         mine, other = paired(grads, axis, hop)
         grads = mine.astype(F32) + other.astype(F32)
     (strain_grad,) = call(

time: 55.6 us -> 55.6 us (level)
  waiting for transfers between devices: 8.96 us -> 9.77 us
  starting transfers between devices: 24.9 us -> 24.2 us
    ppermute x1, waiting for transfers between devices: 0.11 us -> 1.76 us  [on_device(): late = lax.ppermute(head, 'tm', [(i + 1, i) for i in range(n - 1)])]
    ppermute x3, waiting for transfers between devices: 1.52 us -> 0.66 us  [paired(): lax.ppermute(mine, axis, [(i, i ^ hop) for i in range(lax.axis_size(axis))])]
  transfers between devices with their start and end apart: 15 -> 15, of which waited for: 6 -> 7; matrix products, arithmetic and copies ran while one was open for 0% -> 0% of each run, Pallas kernels for 31% -> 31%
where the time goes in v6:
time: 55.6 us; the launch traced here: 55.4 us
  starting transfers between devices  24.2 us (44%)
  Pallas kernels  19.3 us (35%)
  waiting for transfers between devices  9.77 us (18%)
  local copies, waits for them, and re-layouts  1.27 us (2%)
  between operations  0.84 us (2%)
    pallas_call x12, Pallas kernels, call(): pl.pallas_call(kernel, out_shape=outs, in_specs=[where(k, far) for k in r...  19.3 us
    ppermute x6, starting transfers between devices, exchanged(): lax.ppermute(chunks[hop], 'tm', [(i, i ^ hop) for i in range(size)])  8.64 us
    ppermute x3, starting transfers between devices, paired(): lax.ppermute(mine, axis, [(i, i ^ hop) for i in range(lax.axis_size(axis))])  6.1 us
    ppermute x1, starting transfers between devices, on_device(): halo = lax.ppermute(tail, 'tm', [(i, i + 1) for i in range(n - 1)])  4.94 us
    ppermute x2, waiting for transfers between devices, neighbours(): other = lax.ppermute(array, axis, [(0, 1), (1, 0)])  4.85 us
    ppermute x2, starting transfers between devices, neighbours(): other = lax.ppermute(array, axis, [(0, 1), (1, 0)])  3.11 us
    ppermute x1, waiting for transfers between devices, on_device(): late = lax.ppermute(head, 'tm', [(i + 1, i) for i in range(n - 1)])  1.76 us
    ppermute x1, starting transfers between devices, on_device(): late = lax.ppermute(head, 'tm', [(i + 1, i) for i in range(n - 1)])  1.29 us
  transfers between devices with their start and end apart: 15, of which 7 were waited for; matrix products, arithmetic and copies ran while one was open for 0% of the time, Pallas kernels for 31%

profile of v6, /device:TPU:0, one launch (start us, length us, event | category | flops | bytes accessed | tf_op | source)
XLA Modules:
  0.0 55.4 jit_solution(10331940695634073978)
XLA Ops:
  0.6 1.2 %copy.13 = bf16[1,32,128,128]{3,2,1,0:T(8,128)(2,1)S(1)} copy(bf16[1,32,128,128]{3,2,1,0:T(8,128)(2,1)} %param.4) | data formatting | bytes 2097152
  1.9 0.0 copy-start
  1.9 0.8 %tail.1 = (bf16[960,128]{1,0:T(8,128)(2,1)S(1)}, bf16[32,128,128]{2,1,0:T(8,128)(2,1)S(1)}) custom-call(bf16[32,128,128]{2,1,0:T(8,128)(2,1)S(1)} %bitcast.8), custom_call_target="tpu_custom_call", output_to_operand_aliasing={{1}: (0, {})} | custom-call | tf_op jit(solution)/shard_map/tail/pallas_call | solution.py:38
  2.6 4.9 %collective-permute-start = (bf16[960,128]{1,0:T(8,128)(2,1)S(1)}, bf16[960,128]{1,0:T(8,128)(2,1)S(1)}, u32[]{:S(2)}, u32[]{:S(2)}) collective-permute-start(bf16[960,128]{1,0:T(8,128)(2,1)S(1)} %get-tuple-element.42), channel_id=1, source_target_pairs={{0,4},{4,8},{8,12},{1,5},{5,9},{9,13},{2,6},{6,10},{10,14},{3,7},{... | collective-permute-start | bytes 737288 | tf_op jit(solution)/shard_map/ppermute | solution.py:410
  7.6 0.0 copy-done
  7.6 0.0 copy-start.2
  7.6 0.3 pack.1
  7.9 1.6 %collective-permute-start.2 = (bf16[16,32,128]{2,1,0:T(8,128)(2,1)S(1)}, bf16[16,32,128]{2,1,0:T(8,128)(2,1)S(1)}, u32[]{:S(2)}, u32[]{:S(2)}) collective-permute-start(bf16[16,32,128]{2,1,0:T(8,128)(2,1)S(1)} %get-tuple-element.51), channel_id=1, source_target_pairs={{0,4},{4,0},{8,12},{12,8},{1,5},{5,1},{9,13},{13,9},{2,6},{6,2},{1... | collective-permute-start | bytes 393224 | tf_op jit(solution)/shard_map/ppermute | solution.py:374
  9.5 2.5 %collective-permute-start.4 = (bf16[16,32,128]{2,1,0:T(8,128)(2,1)S(1)}, bf16[16,32,128]{2,1,0:T(8,128)(2,1)S(1)}, u32[]{:S(2)}, u32[]{:S(2)}) collective-permute-start(bf16[16,32,128]{2,1,0:T(8,128)(2,1)S(1)} %get-tuple-element.54), channel_id=1, source_target_pairs={{0,12},{4,8},{8,4},{12,0},{1,13},{5,9},{9,5},{13,1},{2,14},{6,10},... | collective-permute-start | bytes 393224 | tf_op jit(solution)/shard_map/ppermute | solution.py:374
  12.0 0.0 copy-done.2
  12.1 1.8 %turn.1.strain_ref = bf16[4096,128]{1,0:T(8,128)(2,1)S(1)} custom-call(bf16[32,128,128]{2,1,0:T(8,128)(2,1)S(1)} %get-tuple-element.43.strain_ref), custom_call_target="tpu_custom_call" | custom-call | tf_op jit(solution)/shard_map/turn/pallas_call | solution.py:38
  13.9 0.0 copy-done.1
  13.9 1.1 %weights.1 = (bf16[256,1536]{1,0:T(8,128)(2,1)S(1)}, bf16[512,768]{1,0:T(8,128)(2,1)S(1)}, bf16[128,1152]{1,0:T(8,128)(2,1)S(1)}, bf16[128,1152]{1,0:T(8,128)(2,1)S(1)}) custom-call(bf16[32,32,32]{2,1,0:T(8,128)(2,1)S(1)} %copy-done.1, bf16[36,32]{1,0:T(8,128)(2,1)S(1)} %reshape.11.fiber_ref), custom_call_target="tpu_custom_call" | custom-call | tf_op jit(solution)/shard_map/weights/pallas_call | solution.py:38
  15.0 0.1 collective-permute-start.3
  15.0 0.0 collective-permute-done.halo_ref
  15.1 1.1 %inner.1 = (bf16[2048,128]{1,0:T(8,128)(2,1)S(1)}, bf16[128,128]{1,0:T(8,128)(2,1)S(1)}) custom-call(bf16[960,128]{1,0:T(8,128)(2,1)S(1)} %collective-permute-done.halo_ref, bf16[4096,128]{1,0:T(8,128)(2,1)S(1)} %turn.1.strain_ref, bf16[256,1536]{1,0:T(8,128)(2,1)S(1)} %get-tuple-element.44.w_ref), custom_call_target="tpu_custom_call" | custom-call | tf_op jit(solution)/shard_map/inner/pallas_call | solution.py:38
  16.2 1.6 %collective-permute-start.1 = (bf16[128,128]{1,0:T(8,128)(2,1)S(1)}, bf16[128,128]{1,0:T(8,128)(2,1)S(1)}, u32[]{:S(2)}, u32[]{:S(2)}) collective-permute-start(bf16[128,128]{1,0:T(8,128)(2,1)S(1)} %get-tuple-element.46), channel_id=1, source_target_pairs={{0,2},{2,0},{1,3},{3,1},{4,6},{6,4},{5,7},{7,5},{8,10},{10,8},{9,1... | collective-permute-start | bytes 98312 | tf_op jit(solution)/shard_map/ppermute | solution.py:381
  17.8 2.4 %collective-permute-done.1.before_ref.after_ref = bf16[128,128]{1,0:T(8,128)(2,1)S(1)} collective-permute-done((bf16[128,128]{1,0:T(8,128)(2,1)S(1)}, bf16[128,128]{1,0:T(8,128)(2,1)S(1)}, u32[]{:S(2)}, u32[]{:S(2)}) %collective-permute-start.1) | collective-permute-done | bytes 32800 | tf_op jit(solution)/shard_map/ppermute | solution.py:381
  20.2 2.9 %forward.1 = (f32[2048,128]{1,0:T(8,128)S(1)}, bf16[16,32,128]{2,1,0:T(8,128)(2,1)S(1)}, bf16[16,32,128]{2,1,0:T(8,128)(2,1)S(1)}, bf16[16,32,128]{2,1,0:T(8,128)(2,1)S(1)}, bf16[16,32,128]{2,1,0:T(8,128)(2,1)S(1)}) custom-call(bf16[2048,128]{1,0:T(8,128)(2,1)S(1)} %get-tuple-element.45.u_ref, ...), custom_call_target="tpu_custom_call" | custom-call | tf_op jit(solution)/shard_map/forward/pallas_call | solution.py:38
  23.1 2.0 %collective-permute-start.6 = (bf16[16,32,128]{2,1,0:T(8,128)(2,1)S(1)}, bf16[16,32,128]{2,1,0:T(8,128)(2,1)S(1)}, u32[]{:S(2)}, u32[]{:S(2)}) collective-permute-start(bf16[16,32,128]{2,1,0:T(8,128)(2,1)S(1)} %get-tuple-element.61), channel_id=1, source_target_pairs={{0,4},{4,0},{8,12},{12,8},{1,5},{5,1},{9,13},{13,9},{2,6},{6,2},{1... | collective-permute-start | bytes 393224 | tf_op jit(solution)/shard_map/ppermute | solution.py:374
  25.0 2.0 %collective-permute-start.7 = (bf16[16,32,128]{2,1,0:T(8,128)(2,1)S(1)}, bf16[16,32,128]{2,1,0:T(8,128)(2,1)S(1)}, u32[]{:S(2)}, u32[]{:S(2)}) collective-permute-start(bf16[16,32,128]{2,1,0:T(8,128)(2,1)S(1)} %get-tuple-element.62), channel_id=1, source_target_pairs={{0,8},{4,12},{8,0},{12,4},{1,9},{5,13},{9,1},{13,5},{2,10},{6,14},... | collective-permute-start | bytes 393224 | tf_op jit(solution)/shard_map/ppermute | solution.py:374
  27.1 0.0 collective-permute-done.2.refs_1_
  27.1 0.5 collective-permute-start.8
  27.5 0.0 collective-permute-done.4.refs_3_
  27.5 0.0 collective-permute-done.3.refs_2_
  27.5 1.2 %slope.1 = (bf16[2048,128]{1,0:T(8,128)(2,1)S(1)}, bf16[128,128]{1,0:T(8,128)(2,1)S(1)}) custom-call(f32[2048,128]{1,0:T(8,128)S(1)} %get-tuple-element.48.slope_ref, bf16[16,32,128]{2,1,0:T(8,128)(2,1)S(1)} %get-tuple-element.50.refs_0_, bf16[16,32,128]{2,1,0:T(8,128)(2,1)S(1)} %collective-permute-done.2.refs_1_, ...), custom_call_target="tpu_custom_call" | custom-call | tf_op jit(solution)/shard_map/slope/pallas_call | solution.py:38
  28.8 1.6 %collective-permute-start.5 = (bf16[128,128]{1,0:T(8,128)(2,1)S(1)}, bf16[128,128]{1,0:T(8,128)(2,1)S(1)}, u32[]{:S(2)}, u32[]{:S(2)}) collective-permute-start(bf16[128,128]{1,0:T(8,128)(2,1)S(1)} %get-tuple-element.56), channel_id=1, source_target_pairs={{0,2},{2,0},{1,3},{3,1},{4,6},{6,4},{5,7},{7,5},{8,10},{10,8},{9,1... | collective-permute-start | bytes 98312 | tf_op jit(solution)/shard_map/ppermute | solution.py:381
  30.3 2.4 %collective-permute-done.5.before_ref.after_ref = bf16[128,128]{1,0:T(8,128)(2,1)S(1)} collective-permute-done((bf16[128,128]{1,0:T(8,128)(2,1)S(1)}, bf16[128,128]{1,0:T(8,128)(2,1)S(1)}, u32[]{:S(2)}, u32[]{:S(2)}) %collective-permute-start.5) | collective-permute-done | bytes 32800 | tf_op jit(solution)/shard_map/ppermute | solution.py:381
  32.7 3.6 %backward.1 = (bf16[2048,128]{1,0:T(8,128)(2,1)S(1)}, f32[40,512]{1,0:T(8,128)S(1)}, bf16[40,512]{1,0:T(8,128)(2,1)S(1)}) custom-call(bf16[2048,128]{1,0:T(8,128)(2,1)S(1)} %get-tuple-element.55.dz_ref, bf16[128,128]{1,0:T(8,128)(2,1)S(1)} %collective-permute-done.5.before_ref.after_ref, bf16[128,128]{1,0:T(8,128)(2,1)S(1)} %collective-permute-done.5.before_ref.after_ref, ...), custom_call_target="tpu_custom_call" | custom-call | tf_op jit(solution)/shard_map/backward/pallas_call | solution.py:38
  36.3 0.0 collective-permute-done.6.refs_1_
  36.3 0.0 collective-permute-done.7.refs_2_
  36.3 0.0 collective-permute-done.8.refs_3_
  36.3 0.1 collective-permute-start.9
  36.4 1.2 %collective-permute-done.9 = bf16[40,512]{1,0:T(8,128)(2,1)S(1)} collective-permute-done((bf16[40,512]{1,0:T(8,128)(2,1)S(1)}, bf16[40,512]{1,0:T(8,128)(2,1)S(1)}, u32[]{:S(2)}, u32[]{:S(2)}) %collective-permute-start.9) | collective-permute-done | bytes 40992 | tf_op jit(solution)/shard_map/ppermute | solution.py:478
  37.6 1.6 %collective-permute-start.10 = (bf16[40,512]{1,0:T(8,128)(2,1)S(1)}, bf16[40,512]{1,0:T(8,128)(2,1)S(1)}, u32[]{:S(2)}, u32[]{:S(2)}) collective-permute-start(bf16[40,512]{1,0:T(8,128)(2,1)S(1)} %add_convert_fusion), channel_id=1, source_target_pairs={{0,2},{2,0},{1,3},{3,1},{4,6},{6,4},{5,7},{7,5},{8,10},{10,8},{9,1... | collective-permute-start | bytes 122888 | tf_op jit(solution)/shard_map/ppermute | solution.py:390
  39.2 2.0 %early.1.early_ref = bf16[32,128,128]{2,1,0:T(8,128)(2,1)S(1)} custom-call(bf16[2048,128]{1,0:T(8,128)(2,1)S(1)} %get-tuple-element.66.du_ref, bf16[512,768]{1,0:T(8,128)(2,1)S(1)} %get-tuple-element.67.v_ref), custom_call_target="tpu_custom_call" | custom-call | tf_op jit(solution)/shard_map/early/pallas_call | solution.py:38
  41.2 0.5 collective-permute-done.10
  41.7 1.5 %collective-permute-start.11 = (bf16[40,512]{1,0:T(8,128)(2,1)S(1)}, bf16[40,512]{1,0:T(8,128)(2,1)S(1)}, u32[]{:S(2)}, u32[]{:S(2)}) collective-permute-start(bf16[40,512]{1,0:T(8,128)(2,1)S(1)} %convert_add_fusion.2), channel_id=1, source_target_pairs={{0,4},{4,0},{8,12},{12,8},{1,5},{5,1},{9,13},{13,9},{2,6},{6,2},{1... | collective-permute-start | bytes 122888 | tf_op jit(solution)/shard_map/ppermute | solution.py:390
  43.3 1.3 %collective-permute-start.13 = (bf16[512,128]{1,0:T(8,128)(2,1)S(1)}, bf16[512,128]{1,0:T(8,128)(2,1)S(1)}, u32[]{:S(2)}, u32[]{:S(2)}) collective-permute-start(bf16[512,128]{1,0:T(8,128)(2,1)S(1)} %slice.3), channel_id=1, source_target_pairs={{4,0},{8,4},{12,8},{5,1},{9,5},{13,9},{6,2},{10,6},{14,10},{7,3},{... | collective-permute-start | bytes 393224 | tf_op jit(solution)/shard_map/ppermute | solution.py:480
  44.6 1.0 %unpack.1 = bf16[32,32,256]{2,1,0:T(8,128)(2,1)} custom-call(bf16[16,32,128]{2,1,0:T(8,128)(2,1)S(1)} %get-tuple-element.69.refs_0_, bf16[16,32,128]{2,1,0:T(8,128)(2,1)S(1)} %collective-permute-done.6.refs_1_, bf16[16,32,128]{2,1,0:T(8,128)(2,1)S(1)} %collective-permute-done.7.refs_2_, bf16[16,32,128]{2,1,0:T(8,128)(2,1)S(1)} %collective-permute-done.8.refs_3_), custom_call_target="tpu_custom_call" | custom-call | tf_op jit(solution)/shard_map/unpack/pallas_call | solution.py:38
  45.6 0.2 collective-permute-done.11
  45.8 3.0 %collective-permute-start.12 = (bf16[40,512]{1,0:T(8,128)(2,1)S(1)}, bf16[40,512]{1,0:T(8,128)(2,1)S(1)}, u32[]{:S(2)}, u32[]{:S(2)}) collective-permute-start(bf16[40,512]{1,0:T(8,128)(2,1)S(1)} %convert_add_fusion.1), channel_id=1, source_target_pairs={{0,8},{4,12},{8,0},{12,4},{1,9},{5,13},{9,1},{13,5},{2,10},{6,14},... | collective-permute-start | bytes 122888 | tf_op jit(solution)/shard_map/ppermute | solution.py:390
  48.8 1.8 %collective-permute-done.13.late_ref = bf16[512,128]{1,0:T(8,128)(2,1)S(1)} collective-permute-done((bf16[512,128]{1,0:T(8,128)(2,1)S(1)}, bf16[512,128]{1,0:T(8,128)(2,1)S(1)}, u32[]{:S(2)}, u32[]{:S(2)}) %collective-permute-start.13) | collective-permute-done | bytes 131104 | tf_op jit(solution)/shard_map/ppermute | solution.py:480
  50.6 1.9 %signal.1 = bf16[32,128,128]{2,1,0:T(8,128)(2,1)} custom-call(bf16[2048,128]{1,0:T(8,128)(2,1)S(1)} %get-tuple-element.66.du_ref, bf16[512,128]{1,0:T(8,128)(2,1)S(1)} %collective-permute-done.13.late_ref, bf16[512,768]{1,0:T(8,128)(2,1)S(1)} %get-tuple-element.67.v_ref, bf16[32,128,128]{2,1,0:T(8,128)(2,1)S(1)} %early.1.early_ref), custom_call_target="tpu_custom_call" | custom-call | tf_op jit(solution)/shard_map/signal/pallas_call | solution.py:38
  52.5 0.0 collective-permute-done.12
  52.5 0.1 collective-permute-start.14
  52.6 1.3 %collective-permute-done.14.other_ref = f32[40,512]{1,0:T(8,128)S(1)} collective-permute-done((f32[40,512]{1,0:T(8,128)S(1)}, f32[40,512]{1,0:T(8,128)S(1)}, u32[]{:S(2)}, u32[]{:S(2)}) %collective-permute-start.14) | collective-permute-done | bytes 81952 | tf_op jit(solution)/shard_map/ppermute | solution.py:512
  53.8 1.6 %finish.1 = (f32[32,32,32]{2,1,0:T(8,128)}, f32[9,4,32]{2,1,0:T(4,128)}) custom-call(f32[40,512]{1,0:T(8,128)S(1)} %convert_add_fusion.mine_ref, f32[40,512]{1,0:T(8,128)S(1)} %collective-permute-done.14.other_ref), custom_call_target="tpu_custom_call" | custom-call | tf_op jit(solution)/shard_map/finish/pallas_call | solution.py:38
  (7 shorter events, 0.1 us)
Async XLA Ops:
  1.9 5.7 %copy-start = (bf16[1,32,1,32,256]{4,3,2,1,0:T(8,128)(2,1)S(1)}, bf16[1,32,1,32,256]{4,3,2,1,0:T(8,128)(2,1)}, u32[]{:S(2)}) copy-start(bf16[1,32,1,32,256]{4,3,2,1,0:T(8,128)(2,1)} %param.7) | copy-start | bytes 1572868
  2.6 12.4 %collective-permute-start = (bf16[960,128]{1,0:T(8,128)(2,1)S(1)}, bf16[960,128]{1,0:T(8,128)(2,1)S(1)}, u32[]{:S(2)}, u32[]{:S(2)}) collective-permute-start(bf16[960,128]{1,0:T(8,128)(2,1)S(1)} %get-tuple-element.42), channel_id=1, source_target_pairs={{0,4},{4,8},{8,12},{1,5},{5,9},{9,13},{2,6},{6,10},{10,14},{3,7},{... | collective-permute-start | bytes 737288 | tf_op jit(solution)/shard_map/ppermute | solution.py:410
  7.6 4.4 %copy-start.2 = (bf16[32,4,9]{0,1,2:T(4,128)(2,1)S(1)}, bf16[32,4,9]{0,1,2:T(4,128)(2,1)}, u32[]{:S(2)}) copy-start(bf16[32,4,9]{0,1,2:T(4,128)(2,1)} %param.6) | copy-start | bytes 6916
  7.9 19.1 %collective-permute-start.2 = (bf16[16,32,128]{2,1,0:T(8,128)(2,1)S(1)}, bf16[16,32,128]{2,1,0:T(8,128)(2,1)S(1)}, u32[]{:S(2)}, u32[]{:S(2)}) collective-permute-start(bf16[16,32,128]{2,1,0:T(8,128)(2,1)S(1)} %get-tuple-element.51), channel_id=1, source_target_pairs={{0,4},{4,0},{8,12},{12,8},{1,5},{5,1},{9,13},{13,9},{2,6},{6,2},{1... | collective-permute-start | bytes 393224 | tf_op jit(solution)/shard_map/ppermute | solution.py:374
  9.5 18.0 %collective-permute-start.4 = (bf16[16,32,128]{2,1,0:T(8,128)(2,1)S(1)}, bf16[16,32,128]{2,1,0:T(8,128)(2,1)S(1)}, u32[]{:S(2)}, u32[]{:S(2)}) collective-permute-start(bf16[16,32,128]{2,1,0:T(8,128)(2,1)S(1)} %get-tuple-element.54), channel_id=1, source_target_pairs={{0,12},{4,8},{8,4},{12,0},{1,13},{5,9},{9,5},{13,1},{2,14},{6,10},... | collective-permute-start | bytes 393224 | tf_op jit(solution)/shard_map/ppermute | solution.py:374
  12.0 1.8 %copy-start.1 = (bf16[32,32,32]{2,1,0:T(8,128)(2,1)S(1)}, bf16[32,32,32]{2,1,0:T(8,128)(2,1)}, u32[]{:S(2)}) copy-start(bf16[32,32,32]{2,1,0:T(8,128)(2,1)} %time_ref.1) | copy-start | bytes 196612
  15.0 12.5 %collective-permute-start.3 = (bf16[16,32,128]{2,1,0:T(8,128)(2,1)S(1)}, bf16[16,32,128]{2,1,0:T(8,128)(2,1)S(1)}, u32[]{:S(2)}, u32[]{:S(2)}) collective-permute-start(bf16[16,32,128]{2,1,0:T(8,128)(2,1)S(1)} %get-tuple-element.53), channel_id=1, source_target_pairs={{0,8},{4,12},{8,0},{12,4},{1,9},{5,13},{9,1},{13,5},{2,10},{6,14},... | collective-permute-start | bytes 393224 | tf_op jit(solution)/shard_map/ppermute | solution.py:374
  16.2 4.0 %collective-permute-start.1 = (bf16[128,128]{1,0:T(8,128)(2,1)S(1)}, bf16[128,128]{1,0:T(8,128)(2,1)S(1)}, u32[]{:S(2)}, u32[]{:S(2)}) collective-permute-start(bf16[128,128]{1,0:T(8,128)(2,1)S(1)} %get-tuple-element.46), channel_id=1, source_target_pairs={{0,2},{2,0},{1,3},{3,1},{4,6},{6,4},{5,7},{7,5},{8,10},{10,8},{9,1... | collective-permute-start | bytes 98312 | tf_op jit(solution)/shard_map/ppermute | solution.py:381
  23.1 13.3 %collective-permute-start.6 = (bf16[16,32,128]{2,1,0:T(8,128)(2,1)S(1)}, bf16[16,32,128]{2,1,0:T(8,128)(2,1)S(1)}, u32[]{:S(2)}, u32[]{:S(2)}) collective-permute-start(bf16[16,32,128]{2,1,0:T(8,128)(2,1)S(1)} %get-tuple-element.61), channel_id=1, source_target_pairs={{0,4},{4,0},{8,12},{12,8},{1,5},{5,1},{9,13},{13,9},{2,6},{6,2},{1... | collective-permute-start | bytes 393224 | tf_op jit(solution)/shard_map/ppermute | solution.py:374
  25.0 11.3 %collective-permute-start.7 = (bf16[16,32,128]{2,1,0:T(8,128)(2,1)S(1)}, bf16[16,32,128]{2,1,0:T(8,128)(2,1)S(1)}, u32[]{:S(2)}, u32[]{:S(2)}) collective-permute-start(bf16[16,32,128]{2,1,0:T(8,128)(2,1)S(1)} %get-tuple-element.62), channel_id=1, source_target_pairs={{0,8},{4,12},{8,0},{12,4},{1,9},{5,13},{9,1},{13,5},{2,10},{6,14},... | collective-permute-start | bytes 393224 | tf_op jit(solution)/shard_map/ppermute | solution.py:374
  27.1 9.3 %collective-permute-start.8 = (bf16[16,32,128]{2,1,0:T(8,128)(2,1)S(1)}, bf16[16,32,128]{2,1,0:T(8,128)(2,1)S(1)}, u32[]{:S(2)}, u32[]{:S(2)}) collective-permute-start(bf16[16,32,128]{2,1,0:T(8,128)(2,1)S(1)} %get-tuple-element.63), channel_id=1, source_target_pairs={{0,12},{4,8},{8,4},{12,0},{1,13},{5,9},{9,5},{13,1},{2,14},{6,10},... | collective-permute-start | bytes 393224 | tf_op jit(solution)/shard_map/ppermute | solution.py:374
  28.8 4.0 %collective-permute-start.5 = (bf16[128,128]{1,0:T(8,128)(2,1)S(1)}, bf16[128,128]{1,0:T(8,128)(2,1)S(1)}, u32[]{:S(2)}, u32[]{:S(2)}) collective-permute-start(bf16[128,128]{1,0:T(8,128)(2,1)S(1)} %get-tuple-element.56), channel_id=1, source_target_pairs={{0,2},{2,0},{1,3},{3,1},{4,6},{6,4},{5,7},{7,5},{8,10},{10,8},{9,1... | collective-permute-start | bytes 98312 | tf_op jit(solution)/shard_map/ppermute | solution.py:381
  36.3 1.3 %collective-permute-start.9 = (bf16[40,512]{1,0:T(8,128)(2,1)S(1)}, bf16[40,512]{1,0:T(8,128)(2,1)S(1)}, u32[]{:S(2)}, u32[]{:S(2)}) collective-permute-start(bf16[40,512]{1,0:T(8,128)(2,1)S(1)} %get-tuple-element.65), channel_id=1, source_target_pairs={{0,1},{1,0},{2,3},{3,2},{4,5},{5,4},{6,7},{7,6},{8,9},{9,8},{10,11... | collective-permute-start | bytes 122888 | tf_op jit(solution)/shard_map/ppermute | solution.py:478
  37.6 4.1 %collective-permute-start.10 = (bf16[40,512]{1,0:T(8,128)(2,1)S(1)}, bf16[40,512]{1,0:T(8,128)(2,1)S(1)}, u32[]{:S(2)}, u32[]{:S(2)}) collective-permute-start(bf16[40,512]{1,0:T(8,128)(2,1)S(1)} %add_convert_fusion), channel_id=1, source_target_pairs={{0,2},{2,0},{1,3},{3,1},{4,6},{6,4},{5,7},{7,5},{8,10},{10,8},{9,1... | collective-permute-start | bytes 122888 | tf_op jit(solution)/shard_map/ppermute | solution.py:390
  41.7 4.1 %collective-permute-start.11 = (bf16[40,512]{1,0:T(8,128)(2,1)S(1)}, bf16[40,512]{1,0:T(8,128)(2,1)S(1)}, u32[]{:S(2)}, u32[]{:S(2)}) collective-permute-start(bf16[40,512]{1,0:T(8,128)(2,1)S(1)} %convert_add_fusion.2), channel_id=1, source_target_pairs={{0,4},{4,0},{8,12},{12,8},{1,5},{5,1},{9,13},{13,9},{2,6},{6,2},{1... | collective-permute-start | bytes 122888 | tf_op jit(solution)/shard_map/ppermute | solution.py:390
  43.3 7.3 %collective-permute-start.13 = (bf16[512,128]{1,0:T(8,128)(2,1)S(1)}, bf16[512,128]{1,0:T(8,128)(2,1)S(1)}, u32[]{:S(2)}, u32[]{:S(2)}) collective-permute-start(bf16[512,128]{1,0:T(8,128)(2,1)S(1)} %slice.3), channel_id=1, source_target_pairs={{4,0},{8,4},{12,8},{5,1},{9,5},{13,9},{6,2},{10,6},{14,10},{7,3},{... | collective-permute-start | bytes 393224 | tf_op jit(solution)/shard_map/ppermute | solution.py:480
  45.8 6.6 %collective-permute-start.12 = (bf16[40,512]{1,0:T(8,128)(2,1)S(1)}, bf16[40,512]{1,0:T(8,128)(2,1)S(1)}, u32[]{:S(2)}, u32[]{:S(2)}) collective-permute-start(bf16[40,512]{1,0:T(8,128)(2,1)S(1)} %convert_add_fusion.1), channel_id=1, source_target_pairs={{0,8},{4,12},{8,0},{12,4},{1,9},{5,13},{9,1},{13,5},{2,10},{6,14},... | collective-permute-start | bytes 122888 | tf_op jit(solution)/shard_map/ppermute | solution.py:390
  52.5 1.3 %collective-permute-start.14 = (f32[40,512]{1,0:T(8,128)S(1)}, f32[40,512]{1,0:T(8,128)S(1)}, u32[]{:S(2)}, u32[]{:S(2)}) collective-permute-start(f32[40,512]{1,0:T(8,128)S(1)} %convert_add_fusion.mine_ref), channel_id=1, source_target_pairs={{0,1},{1,0},{2,3},{3,2},{4,5},{5,4},{6,7},{7,6},{8,9},{9,8},{10,11... | collective-permute-start | bytes 245768 | tf_op jit(solution)/shard_map/ppermute | solution.py:512
